TPU v7x, 128 devices: a whole 4x4x4 slice. The times are simulated.
128 devices in a mesh: comp: 2 (over z_lo), tile: 64 (over x, y, z_hi, core).
Axes of the slice: x: 4, y: 4, z: 4 (z_hi: 2, z_lo: 2; z = z_hi * 2 + z_lo), core: 2. Of those that a mesh axis runs over, the one named last changes fastest.
Arguments:
- state: float32 [2, 4, 16, 16, 32768], P('comp', None, None, None, 'tile'), may hold values from -6 to 6
- metric: float32 [2, 32768], P('comp', 'tile'), may hold values from 0.5 to 2
- element_coupling: float32 [2, 16, 16], P('comp'), may hold values from -0.2 to 0.2
- level_coupling: float32 [2, 16, 16], P('comp'), may hold values from -0.2 to 0.2
- coeffs: float32 [2, 3], P('comp'), may hold values from 0.1 to 0.4
- edge_partner: int32 [2, 131072], P('comp', 'tile'), may hold values from 0 to 3071, as said below
- sea_mask: int32 [2, 16, 32768], P('comp', None, 'tile'), may hold values 0 or 1
- forcing: float32 [2, 4, 16, 32768], P('comp', None, None, 'tile'), may hold values from -6 to 6
- remap_weights: bfloat16 [2, 5120, 128, 128], P('comp', 'tile'), may hold values from -0.375 to 0.375
- remap_rows: int32 [2, 5120], P('comp', 'tile'), may hold values from 0 to 64, as said below
- remap_cols: int32 [2, 5120], P('comp', 'tile'), may hold values from 0 to 191
Outputs:
- state_next: float32 [2, 4, 16, 16, 32768], P('comp', None, None, None, 'tile')
- forcing_next: float32 [2, 4, 16, 32768], P('comp', None, None, 'tile')
Inputs may be any that keep to these rules, and one draw needn't show every extreme that they name: `edge_partner`: edge slots are edge-major (slot e * 512 + k). The pairing is symmetric: slots 0 to 511 meet the previous tile's last 512 slots, the last 512 slots meet the next tile's first 512, all other slots meet slots of their own tile; no slot meets itself. `remap_rows`: within a tile every row block 0 to 63 has at least one slot; a slot holding 64 is unused and adds nothing; the number of used slots differs from tile to tile, and some tile uses all 80.
All inputs are finite; a program needn't handle non-finite values. No bound on the sum of `sea_mask` on one device may be relied on, other than what follows from the above.
Results may differ from a plain program's by a relative error of at most 0.0029.
Values may be sent and summed in bfloat16 or wider, within the bound.
No kernel may reach another device: no remote copies, remote signals or barrier semaphores. Data moves between devices by JAX's collectives and lax.ppermute only.
A program may use at most 192 MiB of HBM per device.

v0:
```python
import jax
import jax.numpy as jnp
import numpy as np
from jax import lax
from jax.sharding import PartitionSpec as P

HIGHEST_PRECISION = lax.Precision.HIGHEST
EDGE_NODES = np.array(
    [[0, 1, 2, 3], [3, 7, 11, 15], [0, 4, 8, 12], [12, 13, 14, 15]], dtype=np.int32
)
OWN_ORDER = EDGE_NODES.T.reshape(-1)
FLIP_ORDER = EDGE_NODES[:, ::-1].T.reshape(-1)
SPREAD_TABLE = (np.arange(16)[:, None] == OWN_ORDER[None, :]).astype(np.float32)


def with_halo(shard, sides, width):
    for axis, dim in sides:
        devices, length = (lax.axis_size(axis), shard.shape[dim])
        up = [(i, (i + 1) % devices) for i in range(devices)]
        down = [(j, i) for i, j in up]
        last = lax.slice_in_dim(shard, length - width, length, axis=dim)
        leading = lax.slice_in_dim(shard, 0, width, axis=dim)
        before = lax.ppermute(last, axis, up)
        after = lax.ppermute(leading, axis, down)
        shard = jnp.concatenate([before, shard, after], axis=dim)
    return shard


def from_partner(value, axis, distance):
    mask = 2**distance
    pairs = [(source, source ^ mask) for source in range(lax.axis_size(axis))]
    return lax.ppermute(value, axis, pairs)


def shards(
    state,
    metric,
    element_coupling,
    level_coupling,
    coeffs,
    edge_partner,
    sea_mask,
    forcing,
    remap_weights,
    remap_rows,
    remap_cols,
):
    current = state[0]
    variables, levels, nodes, elements = current.shape
    metric_own = metric[0]
    mask_own = sea_mask[0].astype(jnp.float32)
    exchange_rate = coeffs[0, 1] * mask_own + coeffs[0, 2] * (1.0 - mask_own)
    partner = edge_partner[0]
    penalty = coeffs[0, 0]
    node_matrix = element_coupling[0] - 0.3 * jnp.eye(nodes, dtype=jnp.float32)
    level_matrix = level_coupling[0] - 0.2 * jnp.eye(levels, dtype=jnp.float32)
    spread_table = jnp.asarray(SPREAD_TABLE)
    bottom = (jnp.arange(levels, dtype=jnp.int32) == 0).astype(jnp.float32)
    forcing_own = forcing[0]
    for substep in range(2):
        own_rows = current[:, :, OWN_ORDER, :].reshape(variables, levels, 4, 4 * elements)
        flipped = current[:, :, FLIP_ORDER, :].reshape(variables, levels, 4, 4 * elements)
        extended = with_halo(flipped, (("tile", 3),), elements)
        partner_rows = jnp.take(extended, partner, axis=3)
        differ = (partner_rows - own_rows).reshape(variables, levels, 16, elements)
        spread = jnp.einsum("np,vlpk->vlnk", spread_table, differ, precision=HIGHEST_PRECISION)
        across = jnp.einsum("nm,vlmk->vlnk", node_matrix, current, precision=HIGHEST_PRECISION)
        across = across * metric_own
        upward = jnp.einsum("lm,vmnk->vlnk", level_matrix, current, precision=HIGHEST_PRECISION)
        total = across + upward + penalty * spread
        lowest = current[:, 0]
        exchange = exchange_rate[None] * (forcing_own - lowest)
        total = total + bottom[None, :, None, None] * exchange[:, None]
        current = current + total
    surface = current[:, 0].astype(jnp.bfloat16)
    flattened = surface.reshape(variables, nodes * elements)
    columns = flattened.shape[1]
    nearby = with_halo(flattened, (("tile", 1),), columns)
    window = from_partner(nearby, "comp", 0)
    blocks = remap_weights[0]
    block_width = blocks.shape[-1]
    row_blocks = columns // block_width
    row_index = remap_rows[0]
    col_index = remap_cols[0]
    blocked = window.reshape(variables, 3 * row_blocks, block_width)
    picked = jnp.take(blocked, col_index, axis=1)
    product = jnp.einsum("brc,vbc->vbr", blocks, picked, preferred_element_type=jnp.float32)
    onehot = (row_index[None, :] == jnp.arange(row_blocks, dtype=jnp.int32)[:, None]).astype(
        jnp.float32
    )
    summed = jnp.einsum("rb,vbi->vri", onehot, product, precision=HIGHEST_PRECISION)
    new_forcing = summed.reshape(variables, nodes, elements)
    return (current[None], new_forcing[None])


def solution(mesh):
    placed = (
        P("comp", None, None, None, "tile"),
        P("comp", "tile"),
        P("comp", None, None),
        P("comp", None, None),
        P("comp", None),
        P("comp", "tile"),
        P("comp", None, "tile"),
        P("comp", None, None, "tile"),
        P("comp", "tile", None, None),
        P("comp", "tile"),
        P("comp", "tile"),
    )
    return jax.shard_map(
        shards,
        mesh=mesh,
        in_specs=placed,
        out_specs=(P("comp", None, None, None, "tile"), P("comp", None, None, "tile")),
        check_vma=False,
    )
```

profile of v0, /device:TPU:0, one launch (start us, length us, event | category | flops | bytes accessed | tf_op | source)
XLA Modules:
  0.0 352.8 jit_solution(14093673862350893906)
XLA Ops:
  0.7 4.3 %copy.107 = f32[4,16,16,512]{3,1,2,0:T(8,128)} copy(f32[4,16,16,512]{3,2,1,0:T(8,128)} %bitcast.128) | data formatting | bytes 4194304 | tf_op jit(solution)/shard_map/squeeze | solution.py:48
  8.6 4.1 %copy.110 = f32[4,16,16,512]{3,2,1,0:T(8,128)} copy(f32[4,16,16,512]{3,1,0,2:T(8,128)} %bitcast.134) | data formatting | bytes 4194304 | tf_op jit(solution)/shard_map/gather | solution.py:62
  19.4 8.2 %collective-permute-start.1 = (f32[4,16,4,512]{3,1,2,0:T(8,128)}, f32[4,16,4,512]{3,1,2,0:T(8,128)}, u32[]{:S(2)}, u32[]{:S(2)}) collective-permute-start(f32[4,16,4,512]{3,1,2,0:T(8,128)} %copy.112), channel_id=1, source_target_pairs={{1,0},{2,1},{3,2},{4,3},{5,4},{6,5},{7,6},{8,7},{9,8},{10,9},{11,1... | collective-permute-start | bytes 1572872 | tf_op jit(solution)/shard_map/ppermute | solution.py:24
  27.6 13.9 %copy.114 = f32[4,16,4,2048]{1,2,3,0:T(4,128)} copy(f32[4,16,4,2048]{3,2,1,0:T(4,128)} %reshape.96) | data formatting | bytes 4194304 | tf_op jit(solution)/shard_map/reshape | solution.py:62
  45.2 4.1 %copy.118 = f32[4,16,16,512]{3,2,1,0:T(8,128)} copy(f32[4,16,16,512]{3,1,0,2:T(8,128)} %bitcast.132) | data formatting | bytes 4194304 | tf_op jit(solution)/shard_map/gather | solution.py:61
  53.6 5.8 %fusion.26 = f32[16,4,16,512]{3,0,2,1:T(8,128)} fusion(f32[1,16,16]{2,1,0:T(8,128)S(1)} %copy-done.7, f32[4,16,16,512]{3,2,1,0:T(8,128)} %bitcast.129), kind=kOutput, calls=%fused_computation.46 | convolution fusion | flops 100664064 | bytes 4195328 | tf_op jit(solution)/shard_map/lm,vmnk->vlnk/dot_general | solution.py:69
  67.1 4.5 %copy.115 = f32[4,16,4,512]{1,2,3,0:T(4,128)} copy(f32[4,16,4,512]{3,1,2,0:T(8,128)} %collective-permute-done.1) | data formatting | bytes 1048576 | tf_op jit(solution)/shard_map/ppermute | solution.py:24
  71.6 26.9 %pad_maximum_fusion = f32[4,16,4,3072]{1,2,3,0:T(4,128)} fusion(f32[4,16,4,512]{1,2,3,0:T(4,128)} %copy.115, f32[4,16,4,2048]{1,2,3,0:T(4,128)} %copy.114, f32[4,16,4,512]{1,2,3,0:T(4,128)} %copy.113), kind=kLoop, calls=%fused_computation.7 | loop fusion | flops 1572864 | bytes 6291456 | tf_op jit(solution)/shard_map/concatenate | solution.py:25
  98.5 36.8 %gather_fusion.5 = f32[2048,4,16,4]{2,3,1,0:T(4,128)} fusion(f32[4,16,4,3072]{1,2,3,0:T(4,128)} %pad_maximum_fusion, s32[2048]{0:T(1024)S(1)} %fusion.36), kind=kCustom, calls=%fused_computation.clone | custom fusion | bytes 4202496 | tf_op jit(solution)/shard_map/jit(_take)/gather | solution.py:64
  135.3 14.8 %copy.116 = f32[2048,4,16,4]{0,2,3,1:T(8,128)} copy(f32[2048,4,16,4]{2,3,1,0:T(4,128)} %gather_fusion.5) | data formatting | bytes 4194304 | tf_op jit(solution)/shard_map/jit(_take)/gather | solution.py:64
  159.6 7.7 %fusion.5 = f32[4,16,16,512]{3,2,1,0:T(8,128)S(1)} fusion(f32[16,4,16,512]{3,0,2,1:T(8,128)} %fusion.26, f32[16,4,16,512]{3,0,2,1:T(8,128)} %fusion.28, f32[4,16,16,512]{3,2,1,0:T(8,128)} %reshape.98, f32[16,16,1,1]{1,0,3,2:T(8,128)S(1)} %copy-done.11, f32[4,16,512]{2,1,0:T(8,128)S(1)} %fusion.13, f32[16]{0:T(128)S(1)} %compare_convert_fusion, ...), kind=kOutput, calls=%fused_computation.18 | convolution fusion | flops 104333312 | bytes 10619972 | tf_op jit(solution)/shard_map/np,vlpk->vlnk/dot_general | solution.py:66
  174.8 4.2 %copy.124 = f32[4,16,16,512]{3,2,1,0:T(8,128)} copy(f32[4,16,16,512]{3,1,0,2:T(8,128)} %bitcast.133) | data formatting | bytes 4194304 | tf_op jit(solution)/shard_map/gather | solution.py:62
  184.5 14.1 %copy.128 = f32[4,16,4,2048]{1,2,3,0:T(4,128)} copy(f32[4,16,4,2048]{3,2,1,0:T(4,128)} %reshape.99) | data formatting | bytes 4194304 | tf_op jit(solution)/shard_map/reshape | solution.py:62
  198.6 3.6 %gather_fusion.3 = f32[16,4,16,512]{3,2,1,0:T(8,128)} fusion(f32[4,16,16,512]{3,1,2,0:T(8,128)} %copy.121, s32[1024]{0:T(1024)S(1)} %pad_clamp_fusion.1), kind=kCustom, calls=%fused_computation.5 | custom fusion | bytes 4194368 | tf_op jit(solution)/shard_map/gather | solution.py:61
  202.3 6.0 %fusion.22 = f32[4,16,512,16]{2,3,1,0:T(8,128)} fusion(f32[1,16,16]{2,1,0:T(8,128)S(1)} %copy-done.7, f32[4,16,16,512]{3,2,1,0:T(8,128)} %copy-done.1), kind=kOutput, calls=%fused_computation.42 | convolution fusion | flops 100664064 | bytes 4195328 | tf_op jit(solution)/shard_map/lm,vmnk->vlnk/dot_general | solution.py:69
  210.2 7.5 %collective-permute-start.3 = (f32[4,16,4,512]{3,1,2,0:T(8,128)}, f32[4,16,4,512]{3,1,2,0:T(8,128)S(1)}, u32[]{:S(2)}, u32[]{:S(2)}) collective-permute-start(f32[4,16,4,512]{3,1,2,0:T(8,128)} %copy.126), channel_id=1, source_target_pairs={{1,0},{2,1},{3,2},{4,3},{5,4},{6,5},{7,6},{8,7},{9,8},{10,9},{11,1... | collective-permute-start | bytes 1572872 | tf_op jit(solution)/shard_map/ppermute | solution.py:24
  224.6 5.0 %fusion.24 = f32[4,16,512,16]{2,3,1,0:T(8,128)} fusion(f32[4,16,16,512]{3,2,1,0:T(8,128)} %copy-done.1, f32[1,16,16]{2,1,0:T(8,128)S(1)} %copy-done.8), kind=kOutput, calls=%fused_computation.44 | convolution fusion | flops 100664064 | bytes 4195328 | tf_op jit(solution)/shard_map/nm,vlmk->vlnk/dot_general | solution.py:67
  229.6 4.5 %copy.127 = f32[4,16,4,512]{1,2,3,0:T(4,128)} copy(f32[4,16,4,512]{3,1,2,0:T(8,128)} %collective-permute-done.2) | data formatting | bytes 1048576 | tf_op jit(solution)/shard_map/ppermute | solution.py:23
  237.2 26.9 %pad_maximum_fusion.1 = f32[4,16,4,3072]{1,2,3,0:T(4,128)} fusion(f32[4,16,4,512]{1,2,3,0:T(4,128)} %copy.129, f32[4,16,4,2048]{1,2,3,0:T(4,128)} %copy.128, f32[4,16,4,512]{1,2,3,0:T(4,128)} %copy.127), kind=kLoop, calls=%fused_computation.8 | loop fusion | flops 1572864 | bytes 6291456 | tf_op jit(solution)/shard_map/concatenate | solution.py:25
  264.1 36.8 %gather_fusion.6 = f32[2048,4,16,4]{2,3,1,0:T(4,128)} fusion(f32[4,16,4,3072]{1,2,3,0:T(4,128)} %pad_maximum_fusion.1, s32[2048]{0:T(1024)S(1)} %fusion.36), kind=kCustom, calls=%fused_computation.1.clone | custom fusion | bytes 4202496 | tf_op jit(solution)/shard_map/jit(_take)/gather | solution.py:64
  300.9 14.4 %copy.130 = f32[2048,4,16,4]{0,2,3,1:T(8,128)} copy(f32[2048,4,16,4]{2,3,1,0:T(4,128)} %gather_fusion.6) | data formatting | bytes 4194304 | tf_op jit(solution)/shard_map/jit(_take)/gather | solution.py:64
  325.0 7.7 %fusion.3 = f32[4,16,16,512]{3,2,1,0:T(8,128)S(1)} fusion(f32[4,16,16,512]{3,2,1,0:T(8,128)} %copy-done.1, f32[4,16,512,16]{2,3,1,0:T(8,128)} %fusion.22, f32[4,16,512,16]{2,3,1,0:T(8,128)} %fusion.24, f32[4,16,16,512]{3,2,1,0:T(8,128)} %reshape.101, f32[16,16,1,1]{1,0,3,2:T(8,128)S(1)} %copy-done.11, f32[4,16,512]{2,1,0:T(8,128)S(1)} %fusion.11, ...), kind=kOutput, calls=%fused_computation.13 | convolution fusion | flops 104333312 | bytes 10619972 | tf_op jit(solution)/shard_map/np,vlpk->vlnk/dot_general | solution.py:66
  334.1 7.5 %collective-permute-start.5 = (bf16[4,8192]{1,0:T(4,128)(2,1)S(1)}, bf16[4,8192]{1,0:T(4,128)(2,1)S(1)}, u32[]{:S(2)}, u32[]{:S(2)}) collective-permute-start(bf16[4,8192]{1,0:T(4,128)(2,1)S(1)} %bitcast.137), channel_id=1, source_target_pairs={{1,0},{2,1},{3,2},{4,3},{5,4},{6,5},{7,6},{8,7},{9,8},{10,9},{11,1... | collective-permute-start | bytes 196616 | tf_op jit(solution)/shard_map/ppermute | solution.py:24
  345.1 4.4 %collective-permute-done.6 = bf16[4,24576]{1,0:T(4,128)(2,1)S(1)} collective-permute-done((bf16[4,24576]{1,0:T(4,128)(2,1)S(1)}, bf16[4,24576]{1,0:T(4,128)(2,1)S(1)}, u32[]{:S(2)}, u32[]{:S(2)}) %collective-permute-start.6) | collective-permute-done | bytes 196640 | tf_op jit(solution)/shard_map/ppermute | solution.py:32
  (89 shorter events, 78.1 us)
Async XLA Ops:
  0.6 349.6 %copy-start = (bf16[1,80,128,128]{3,2,1,0:T(8,128)(2,1)S(1)}, bf16[1,80,128,128]{3,2,1,0:T(8,128)(2,1)}, u32[]{:S(2)}) copy-start(bf16[1,80,128,128]{3,2,1,0:T(8,128)(2,1)} %param.28) | copy-start | bytes 7864324
  0.6 4.3 %copy-start.16 = (s32[16]{0:T(128)S(1)}, s32[16]{0:T(128)}, u32[]{:S(2)}) copy-start(s32[16]{0:T(128)} %constant.63) | copy-start | bytes 196
  18.4 45.7 %collective-permute-start = (f32[4,16,4,512]{3,1,2,0:T(8,128)}, f32[4,16,4,512]{3,1,2,0:T(8,128)S(1)}, u32[]{:S(2)}, u32[]{:S(2)}) collective-permute-start(f32[4,16,4,512]{3,1,2,0:T(8,128)} %copy.111), channel_id=1, source_target_pairs={{0,1},{1,2},{2,3},{3,4},{4,5},{5,6},{6,7},{7,8},{8,9},{9,10},{10,1... | collective-permute-start | bytes 1572872 | tf_op jit(solution)/shard_map/ppermute | solution.py:23
  19.4 22.1 %copy-start.9 = (s32[1,2048]{1,0:T(1,128)S(1)}, s32[1,2048]{1,0:T(1,128)}, u32[]{:S(2)}) copy-start(s32[1,2048]{1,0:T(1,128)} %param.25) | copy-start | bytes 24580
  19.4 22.2 %copy-start.15 = (s32[16]{0:T(128)S(1)}, s32[16]{0:T(128)}, u32[]{:S(2)}) copy-start(s32[16]{0:T(128)} %constant.64) | copy-start | bytes 196
  19.4 47.7 %collective-permute-start.1 = (f32[4,16,4,512]{3,1,2,0:T(8,128)}, f32[4,16,4,512]{3,1,2,0:T(8,128)}, u32[]{:S(2)}, u32[]{:S(2)}) collective-permute-start(f32[4,16,4,512]{3,1,2,0:T(8,128)} %copy.112), channel_id=1, source_target_pairs={{1,0},{2,1},{3,2},{4,3},{5,4},{6,5},{7,6},{8,7},{9,8},{10,9},{11,1... | collective-permute-start | bytes 1572872 | tf_op jit(solution)/shard_map/ppermute | solution.py:24
  49.3 3.6 %copy-start.13 = (f32[1,3]{1,0:T(1,128)S(1)}, f32[1,3]{1,0:T(1,128)}, u32[]{:S(2)}) copy-start(f32[1,3]{1,0:T(1,128)} %param.24) | copy-start | bytes 40
  49.3 4.2 %copy-start.7 = (f32[1,16,16]{2,1,0:T(8,128)S(1)}, f32[1,16,16]{2,1,0:T(8,128)}, u32[]{:S(2)}) copy-start(f32[1,16,16]{2,1,0:T(8,128)} %param.23) | copy-start | bytes 3076
  53.6 5.9 %copy-start.10 = (s32[1,16,512]{2,1,0:T(8,128)S(1)}, s32[1,16,512]{2,1,0:T(8,128)}, u32[]{:S(2)}) copy-start(s32[1,16,512]{2,1,0:T(8,128)} %param.26) | copy-start | bytes 98308
  53.6 7.3 %copy-start.2 = (f32[1,4,16,16,512]{4,3,2,1,0:T(8,128)S(1)}, f32[1,4,16,16,512]{4,3,2,1,0:T(8,128)}, u32[]{:S(2)}) copy-start(f32[1,4,16,16,512]{4,3,2,1,0:T(8,128)} %param.20) | copy-start | bytes 6291460
  53.6 7.3 %copy-start.6 = (f32[1,4,16,512]{3,2,1,0:T(8,128)S(1)}, f32[1,4,16,512]{3,2,1,0:T(8,128)}, u32[]{:S(2)}) copy-start(f32[1,4,16,512]{3,2,1,0:T(8,128)} %param.27) | copy-start | bytes 393220
  53.6 7.3 %copy-start.17 = (s32[1,80]{1,0:T(1,128)S(1)}, s32[1,80]{1,0:T(1,128)}, u32[]{:S(2)}) copy-start(s32[1,80]{1,0:T(1,128)} %param.30) | copy-start | bytes 964
  53.6 7.3 %copy-start.8 = (f32[1,16,16]{2,1,0:T(8,128)S(1)}, f32[1,16,16]{2,1,0:T(8,128)}, u32[]{:S(2)}) copy-start(f32[1,16,16]{2,1,0:T(8,128)} %param.22) | copy-start | bytes 3076
  156.3 3.3 copy-start.11
  156.3 3.3 copy-start.12
  167.4 1.3 copy-start.1
  202.3 6.0 %copy-start.5 = (f32[4,16,4,512]{3,2,1,0:T(4,128)S(1)}, f32[4,16,4,512]{3,2,1,0:T(4,128)}, u32[]{:S(2)}) copy-start(f32[4,16,4,512]{3,2,1,0:T(4,128)} %get-tuple-element.3) | copy-start | bytes 1572868
  208.2 9.4 %copy-start.3 = (f32[16,4,16,512]{3,2,1,0:T(8,128)S(1)}, f32[16,4,16,512]{3,2,1,0:T(8,128)}, u32[]{:S(2)}) copy-start(f32[16,4,16,512]{3,2,1,0:T(8,128)} %gather_fusion.3) | copy-start | bytes 6291460
  209.2 20.5 %collective-permute-start.2 = (f32[4,16,4,512]{3,1,2,0:T(8,128)}, f32[4,16,4,512]{3,1,2,0:T(8,128)}, u32[]{:S(2)}, u32[]{:S(2)}) collective-permute-start(f32[4,16,4,512]{3,1,2,0:T(8,128)} %copy.125), channel_id=1, source_target_pairs={{0,1},{1,2},{2,3},{3,4},{4,5},{5,6},{6,7},{7,8},{8,9},{9,10},{10,1... | collective-permute-start | bytes 1572872 | tf_op jit(solution)/shard_map/ppermute | solution.py:23
  210.2 23.9 %collective-permute-start.3 = (f32[4,16,4,512]{3,1,2,0:T(8,128)}, f32[4,16,4,512]{3,1,2,0:T(8,128)S(1)}, u32[]{:S(2)}, u32[]{:S(2)}) collective-permute-start(f32[4,16,4,512]{3,1,2,0:T(8,128)} %copy.126), channel_id=1, source_target_pairs={{1,0},{2,1},{3,2},{4,3},{5,4},{6,5},{7,6},{8,7},{9,8},{10,9},{11,1... | collective-permute-start | bytes 1572872 | tf_op jit(solution)/shard_map/ppermute | solution.py:24
  334.0 17.7 %copy-start.14 = (s32[1,80]{1,0:T(1,128)S(1)}, s32[1,80]{1,0:T(1,128)}, u32[]{:S(2)}) copy-start(s32[1,80]{1,0:T(1,128)} %param.29) | copy-start | bytes 964
  334.1 9.6 %collective-permute-start.4 = (bf16[4,8192]{1,0:T(4,128)(2,1)S(1)}, bf16[4,8192]{1,0:T(4,128)(2,1)S(1)}, u32[]{:S(2)}, u32[]{:S(2)}) collective-permute-start(bf16[4,8192]{1,0:T(4,128)(2,1)S(1)} %bitcast.136), channel_id=1, source_target_pairs={{0,1},{1,2},{2,3},{3,4},{4,5},{5,6},{6,7},{7,8},{8,9},{9,10},{10,1... | collective-permute-start | bytes 196616 | tf_op jit(solution)/shard_map/ppermute | solution.py:23
  334.1 9.5 %collective-permute-start.5 = (bf16[4,8192]{1,0:T(4,128)(2,1)S(1)}, bf16[4,8192]{1,0:T(4,128)(2,1)S(1)}, u32[]{:S(2)}, u32[]{:S(2)}) collective-permute-start(bf16[4,8192]{1,0:T(4,128)(2,1)S(1)} %bitcast.137), channel_id=1, source_target_pairs={{1,0},{2,1},{3,2},{4,3},{5,4},{6,5},{7,6},{8,7},{9,8},{10,9},{11,1... | collective-permute-start | bytes 196616 | tf_op jit(solution)/shard_map/ppermute | solution.py:24
  343.8 5.8 %collective-permute-start.6 = (bf16[4,24576]{1,0:T(4,128)(2,1)S(1)}, bf16[4,24576]{1,0:T(4,128)(2,1)S(1)}, u32[]{:S(2)}, u32[]{:S(2)}) collective-permute-start(bf16[4,24576]{1,0:T(4,128)(2,1)S(1)} %pad_maximum_fusion.2), channel_id=1, source_target_pairs={{0,64},{64,0},{1,65},{65,1},{2,66},{66,2},{3,67},{67,3},{4,68},{68... | collective-permute-start | bytes 589832 | tf_op jit(solution)/shard_map/ppermute | solution.py:32
  (1 other events, 1.3 us)
where the time goes:
time: 359 us; the launch traced here: 353 us
  local copies, waits for them, and re-layouts  220 us (61%)
  other arithmetic  63.3 us (18%)
  matrix products  37.1 us (10%)
  starting transfers between devices  24.6 us (7%)
  waiting for transfers between devices  6.42 us (2%)
    gather x4, local copies, waits for them, and re-layouts, shards(): partner_rows = jnp.take(extended, partner, axis=3)  103 us
    concatenate x3, other arithmetic, with_halo(): shard = jnp.concatenate([before, shard, after], axis=dim)  53.9 us
    reshape x4, local copies, waits for them, and re-layouts, shards(): current[:, :, FLIP_ORDER, :].reshape(variables, levels, 4, 4 * elements)  35 us
    ppermute x3, starting transfers between devices, with_halo(): after = lax.ppermute(leading, axis, down)  23.1 us
    dot_general x2, matrix products, shards(): jnp.einsum('np,vlpk->vlnk', spread_table, differ, precision=HIGHEST_PRECI...  15.4 us
    gather x4, local copies, waits for them, and re-layouts, shards(): current[:, :, FLIP_ORDER, :].reshape(variables, levels, 4, 4 * elements)  15.4 us
    gather x4, local copies, waits for them, and re-layouts, shards(): current[:, :, OWN_ORDER, :].reshape(variables, levels, 4, 4 * elements)  14 us
    dot_general x2, matrix products, shards(): jnp.einsum('lm,vmnk->vlnk', level_matrix, current, precision=HIGHEST_PREC...  11.8 us
  transfers between devices with their start and end apart: 7, of which 2 were waited for; matrix products, arithmetic and copies ran while one was open for 16% of the time, Pallas kernels for 0%

commit v1 on v0

v1 whole, which is shorter than its diff:
```python
import functools

import jax
import jax.numpy as jnp
import numpy as np
from jax import lax
from jax.experimental import pallas as pl
from jax.experimental.pallas import tpu as pltpu
from jax.sharding import PartitionSpec as P

F32 = jnp.float32
BF16 = jnp.bfloat16
VMEM_LIMIT = 40 * 1024 * 1024


def dot(a, b):
    return jnp.dot(a, b, preferred_element_type=F32)


def iota(shape, dim):
    return lax.broadcasted_iota(jnp.int32, shape, dim)


def node_of(edge, place):
    side = jnp.where(edge == 1, 4 * place + 3, 4 * place)
    return jnp.where(edge == 0, place, jnp.where(edge == 3, 12 + place, side))


def split_rows(rows):
    group = rows // 64
    edge = jnp.where(group == 0, 0, jnp.where(group == 1, 3, group - 1))
    return edge, (rows % 64) // 4, rows % 4


def select_matrix():
    edge, level, place = split_rows(iota((256, 256), 0))
    wanted = level * 16 + node_of(edge, place)
    return (iota((256, 256), 1) == wanted).astype(BF16)


def spread_matrix():
    edge, level, place = split_rows(iota((256, 256), 1))
    wanted = level * 16 + node_of(edge, 3 - place)
    return (iota((256, 256), 0) == wanted).astype(BF16)


def coupling_matrices(node_ref, level_ref):
    row, col = iota((256, 16), 0), iota((256, 16), 1)
    rows_t, cols_t = iota((16, 256), 0), iota((16, 256), 1)
    inner, outer = (row % 16 == col).astype(BF16), (row // 16 == col).astype(BF16)
    inner_t, outer_t = (cols_t % 16 == rows_t).astype(BF16), (cols_t // 16 == rows_t).astype(BF16)
    r, c = iota((256, 256), 0), iota((256, 256), 1)
    node = dot(dot(inner, node_ref[0].astype(BF16)).astype(BF16), inner_t)
    node = jnp.where(r // 16 == c // 16, node, 0.0).astype(BF16)
    level = dot(dot(outer, level_ref[0].astype(BF16)).astype(BF16), outer_t)
    level = jnp.where(r % 16 == c % 16, level, 0.0).astype(BF16)
    return node, level


def diagonal(metric, penalty):
    node = iota((16, metric.shape[1]), 0)
    i, j = node // 4, node % 4
    edges = ((i == 0) | (i == 3)).astype(F32) + ((j == 0) | (j == 3)).astype(F32)
    return 0.8 - 0.3 * metric - penalty * edges


def exchange_rate(coeffs_ref, mask_ref):
    mask = mask_ref[0].astype(F32)
    return coeffs_ref[0, 1] * mask + coeffs_ref[0, 2] * (1.0 - mask)


def levels_of(pattern):
    return jnp.concatenate([pattern] * 16, axis=0)


def local_kernel(
    state_ref, metric_ref, node_ref, level_ref, coeffs_ref, partner_ref, mask_ref, forcing_ref,
    part_ref, even_ref, odd_ref, inner_ref, weights_ref, edges,
):
    penalty = coeffs_ref[0, 0]
    metric = metric_ref[...]
    node, level = coupling_matrices(node_ref, level_ref)
    weights_ref[:, 0:256] = node
    weights_ref[:, 256:512] = level
    weights_ref[:, 512:768] = spread_matrix()
    select = select_matrix()
    for step in range(4):
        columns = partner_ref[0:1, 512 + 256 * step : 768 + 256 * step] - 1024
        inner_ref[:, 256 * step : 256 * (step + 1)] = (iota((1024, 256), 0) == columns).astype(BF16)
    even = lax.rem(lax.axis_index("tile"), 2) == 0
    for v in range(4):
        rows = slice(256 * v, 256 * (v + 1))
        scaled = (penalty * state_ref[rows, :]).astype(BF16)
        picked = dot(select, scaled).astype(BF16)
        first, last = picked[0:64], picked[64:128]
        even_ref[64 * v : 64 * (v + 1), :] = jnp.where(even, last, first)
        odd_ref[64 * v : 64 * (v + 1), :] = jnp.where(even, first, last)
        edges[64 * v : 64 * (v + 1), 0:512] = picked[128:192]
        edges[64 * v : 64 * (v + 1), 512:1024] = picked[192:256]
    moved = dot(edges[...], inner_ref[...]).astype(BF16)
    factor = levels_of(diagonal(metric, penalty))
    rate = exchange_rate(coeffs_ref, mask_ref)
    for v in range(4):
        rows = slice(256 * v, 256 * (v + 1))
        u = state_ref[rows, :]
        near = moved[64 * v : 64 * (v + 1)]
        p = factor * u + dot(node, (u * metric).astype(BF16)) + dot(level, u.astype(BF16))
        p = p + dot(weights_ref[:, 640:704], near[:, 0:512]) + dot(weights_ref[:, 704:768], near[:, 512:1024])
        part_ref[rows, :] = p
        part_ref[256 * v : 256 * v + 16, :] += rate * (forcing_ref[0, v] - u[0:16])
        p = part_ref[rows, :]
        picked = dot(select[0:128], (penalty * p).astype(BF16)).astype(BF16)
        first, last = picked[0:64], picked[64:128]
        even_ref[256 + 64 * v : 320 + 64 * v, :] = jnp.where(even, last, first)
        odd_ref[256 + 64 * v : 320 + 64 * v, :] = jnp.where(even, first, last)


def tables_kernel(partner_ref, rows_ref, cols_ref, before_ref, after_ref, pick_ref, sum_ref):
    before_ref[...] = (iota((512, 512), 0) == partner_ref[0:1, 0:512]).astype(BF16)
    after_ref[...] = (iota((512, 512), 0) == partner_ref[0:1, 1536:2048] - 2560).astype(BF16)
    odd = lax.rem(lax.axis_index("tile"), 2)
    slots = rows_ref.shape[1]
    wide = 4 * slots
    repeat = (iota((slots, wide), 1) // 4 == iota((slots, wide), 0)).astype(BF16)
    widen = lambda ref: dot(jnp.broadcast_to(ref[0:1, :].astype(BF16), (16, slots)), repeat)[0:1].astype(jnp.int32)
    rows, cols = widen(rows_ref), widen(cols_ref)
    tile, block = cols // 64, cols % 64
    tile = jnp.where(odd == 1, 2 - tile, tile)
    var = iota((1, wide), 1) % 4
    wanted = tile * 256 + var * 64 + (block % 4) * 16 + block // 4
    pick_ref[...] = jnp.transpose((iota((768, wide), 0) == wanted).astype(F32)).astype(BF16)
    wanted = jnp.where(rows == 64, -1, var * 64 + (rows % 4) * 16 + rows // 4)
    sum_ref[...] = (iota((256, wide), 0) == wanted).astype(BF16)


def finish_kernel(
    state_ref, part_ref, even_ref, odd_ref, before_ref, after_ref, inner_ref, weights_ref,
    metric_ref, coeffs_ref, mask_ref, forcing_ref,
    next_ref, surface_ref, edges, halo_before, halo_after,
):
    penalty = coeffs_ref[0, 0]
    metric = metric_ref[...]
    even = lax.rem(lax.axis_index("tile"), 2) == 0
    halo_before[...] = dot(jnp.where(even, odd_ref[...], even_ref[...]), before_ref[...]).astype(BF16)
    halo_after[...] = dot(jnp.where(even, even_ref[...], odd_ref[...]), after_ref[...]).astype(BF16)
    select = select_matrix()
    spread = weights_ref[:, 512:768]
    for v in range(4):
        rows = slice(256 * v, 256 * (v + 1))
        quarter = slice(64 * v, 64 * (v + 1))
        u1 = part_ref[rows, :] + dot(spread[:, 0:64], halo_before[quarter]) + dot(spread[:, 64:128], halo_after[quarter])
        next_ref[rows, :] = u1
        picked = dot(select[128:256], (penalty * u1).astype(BF16)).astype(BF16)
        edges[quarter, 0:512] = picked[0:64]
        edges[quarter, 512:1024] = picked[64:128]
    moved = dot(edges[...], inner_ref[...]).astype(BF16)
    factor = levels_of(diagonal(metric, penalty))
    node = iota((256, 1), 0) % 16
    facing = jnp.where((node // 4 == 0) | (node // 4 == 3), penalty * penalty, 0.0)
    rate = exchange_rate(coeffs_ref, mask_ref)
    for v in range(4):
        rows = slice(256 * v, 256 * (v + 1))
        far = slice(256 + 64 * v, 256 + 64 * (v + 1))
        near = moved[64 * v : 64 * (v + 1)]
        u1 = next_ref[rows, :]
        x = factor * u1 + facing * state_ref[rows, :]
        x = x + dot(weights_ref[:, 0:256], (u1 * metric).astype(BF16)) + dot(weights_ref[:, 256:512], u1.astype(BF16))
        x = x + dot(spread[:, 0:64], halo_before[far]) + dot(spread[:, 64:128], halo_after[far])
        x = x + dot(spread[:, 128:192], near[:, 0:512]) + dot(spread[:, 192:256], near[:, 512:1024])
        next_ref[rows, :] = x
        lowest = x[0:16] + rate * (forcing_ref[0, v] - u1[0:16])
        next_ref[256 * v : 256 * v + 16, :] = lowest
        for q in range(4):
            surface_ref[64 * v + 16 * q : 64 * v + 16 * (q + 1), :] = lowest[:, 128 * q : 128 * (q + 1)].astype(BF16)


def remap_kernel(far_ref, own_ref, near_ref, pick_ref, sum_ref, blocks_ref, out_ref, products):
    picked = dot(pick_ref[:, 0:256], far_ref[...])
    picked = picked + dot(pick_ref[:, 256:512], own_ref[...])
    picked = picked + dot(pick_ref[:, 512:768], near_ref[...])
    slots = blocks_ref.shape[0]
    upper = iota((8, 1), 0) < 4
    for pair in range(slots // 2):
        part = picked[8 * pair : 8 * (pair + 1)]
        left = jnp.concatenate([jnp.where(upper, part, 0.0), jnp.where(upper, 0.0, part)], axis=1).astype(BF16)
        right = jnp.concatenate([blocks_ref[2 * pair], blocks_ref[2 * pair + 1]], axis=1)
        products[8 * pair : 8 * (pair + 1), :] = lax.dot_general(
            left, right, (((1,), (1,)), ((), ())), preferred_element_type=F32
        )
    value = products[...]
    high = value.astype(BF16)
    low = (value - high.astype(F32)).astype(BF16)
    total = dot(sum_ref[...], high) + dot(sum_ref[...], low)
    for v in range(4):
        for q in range(4):
            out_ref[0, v, :, 128 * q : 128 * (q + 1)] = total[64 * v + 16 * q : 64 * v + 16 * (q + 1)]


def call(kernel, outs, scratch=(), smem=(), count=0):
    vmem = pl.BlockSpec(memory_space=pltpu.VMEM)
    specs = [pl.BlockSpec(memory_space=pltpu.SMEM) if i in smem else vmem for i in range(count)]
    return pl.pallas_call(
        kernel,
        out_shape=[jax.ShapeDtypeStruct(shape, kind) for shape, kind in outs],
        in_specs=specs,
        out_specs=[vmem] * len(outs),
        scratch_shapes=list(scratch),
        compiler_params=pltpu.CompilerParams(vmem_limit_bytes=VMEM_LIMIT),
    )


def shards(
    state, metric, element_coupling, level_coupling, coeffs, edge_partner, sea_mask, forcing,
    remap_weights, remap_rows, remap_cols,
):
    tiles = lax.axis_size("tile")
    here = [(t, t ^ 1) for t in range(tiles)]
    away = [(t, (t + 1) % tiles if t % 2 else (t - 1) % tiles) for t in range(tiles)]
    crossed = lambda pairs: [(c * tiles + a, (1 - c) * tiles + b) for c in range(2) for a, b in pairs]
    straight = [(t, t) for t in range(tiles)]
    flat = state.reshape(1024, 512)
    part, even, odd, inner, weights = call(
        local_kernel,
        [((1024, 512), F32), ((512, 512), BF16), ((512, 512), BF16), ((1024, 1024), BF16), ((256, 768), BF16)],
        [pltpu.VMEM((256, 1024), BF16)], smem=(4,), count=8,
    )(flat, metric, element_coupling, level_coupling, coeffs, edge_partner, sea_mask, forcing)
    odd = lax.ppermute(odd, "tile", away)
    even = lax.ppermute(even, "tile", here)
    slots = remap_rows.shape[1]
    before, after, pick, total = call(
        tables_kernel,
        [((512, 512), BF16), ((512, 512), BF16), ((4 * slots, 768), BF16), ((256, 4 * slots), BF16)], count=3,
    )(edge_partner, remap_rows, remap_cols)
    nxt, surface = call(
        finish_kernel,
        [((1024, 512), F32), ((256, 128), BF16)],
        [pltpu.VMEM((256, 1024), BF16), pltpu.VMEM((512, 512), BF16), pltpu.VMEM((512, 512), BF16)],
        smem=(9,), count=12,
    )(flat, part, even, odd, before, after, inner, weights, metric, coeffs, sea_mask, forcing)
    far = lax.ppermute(surface, ("comp", "tile"), crossed(away))
    near = lax.ppermute(surface, ("comp", "tile"), crossed(here))
    own = lax.ppermute(surface, ("comp", "tile"), crossed(straight))
    (new_forcing,) = call(
        remap_kernel, [(forcing.shape, F32)], [pltpu.VMEM((4 * slots, 128), F32)], count=6,
    )(far, own, near, pick, total, remap_weights[0])
    return nxt.reshape(state.shape), new_forcing


def solution(mesh):
    placed = (
        P("comp", None, None, None, "tile"),
        P("comp", "tile"),
        P("comp", None, None),
        P("comp", None, None),
        P("comp", None),
        P("comp", "tile"),
        P("comp", None, "tile"),
        P("comp", None, None, "tile"),
        P("comp", "tile", None, None),
        P("comp", "tile"),
        P("comp", "tile"),
    )
    return jax.shard_map(
        shards,
        mesh=mesh,
        in_specs=placed,
        out_specs=(P("comp", None, None, None, "tile"), P("comp", None, None, "tile")),
        check_vma=False,
    )
```

time: 359 us -> 48 us (0.13); the launches traced: 353 us -> 47.6 us
  local copies, waits for them, and re-layouts: 220 us -> 6.7 us
  other arithmetic: 63.3 us -> 0 us
  matrix products: 37.1 us -> 0 us
  Pallas kernels: 0 us -> 12.7 us
  starting transfers between devices: 24.6 us -> 19.2 us
    gather x13 -> x0, local copies, waits for them, and re-layouts: 133 us -> none  [the longest x4 103 us: shards(): partner_rows = jnp.take(extended, partner, axis=3)]
    concatenate x3 -> x0, other arithmetic: 53.9 us -> none  [with_halo(): shard = jnp.concatenate([before, shard, after], axis=dim)]
    reshape x8 -> x0, local copies, waits for them, and re-layouts: 48.8 us -> none  [the longest x4 35 us: shards(): current[:, :, FLIP_ORDER, :].reshape(variables, levels, 4, 4 * elements)]
    dot_general x8 -> x0, matrix products: 37.1 us -> none  [the longest x2 15.4 us: shards(): jnp.einsum('np,vlpk->vlnk', spread_table, differ, precision=HIGHEST_PRECI...]
    ppermute x4 -> x0, local copies, waits for them, and re-layouts: 15.1 us -> none  [the longest x2 7.56 us: with_halo(): after = lax.ppermute(leading, axis, down)]
    pallas_call x0 -> x4, Pallas kernels: none -> 12.7 us  [the longest x1 6.17 us: shards(): call(finish_kernel, [((1024, 512), F32), ((256, 128), BF16)], [pltpu.VMEM...]
    slice x7 -> x0, local copies, waits for them, and re-layouts: 7.93 us -> none  [the longest x4 5.32 us: with_halo(): last = lax.slice_in_dim(shard, length - width, length, axis=dim)]
    sub x2 -> x0, other arithmetic: 7.1 us -> none  [shards(): differ = (partner_rows - own_rows).reshape(variables, levels, 16, elements)]
  transfers between devices with their start and end apart: 7 -> 5, of which waited for: 2 -> 2; matrix products, arithmetic and copies ran while one was open for 16% -> 0% of each run, Pallas kernels for 0% -> 1%
where the time goes in v1:
time: 48 us; the launch traced here: 47.6 us
  starting transfers between devices  19.2 us (40%)
  Pallas kernels  12.7 us (26%)
  waiting for transfers between devices  8.32 us (17%)
  local copies, waits for them, and re-layouts  6.7 us (14%)
  between operations  0.7 us (1%)
    ppermute x1, starting transfers between devices, shards(): odd = lax.ppermute(odd, 'tile', away)  8.7 us
    ppermute x1, starting transfers between devices, shards(): far = lax.ppermute(surface, ('comp', 'tile'), crossed(away))  7.77 us
    unnamed x24, local copies, waits for them, and re-layouts  6.7 us
    ppermute x1, waiting for transfers between devices, shards(): odd = lax.ppermute(odd, 'tile', away)  6.37 us
    pallas_call x1, Pallas kernels, shards(): call(finish_kernel, [((1024, 512), F32), ((256, 128), BF16)], [pltpu.VMEM...  6.17 us
    pallas_call x1, Pallas kernels, shards(): call(local_kernel, [((1024, 512), F32), ((512, 512), BF16), ((512, 512),...  3.86 us
    ppermute x1, starting transfers between devices, shards(): near = lax.ppermute(surface, ('comp', 'tile'), crossed(here))  2.15 us
    pallas_call x1, Pallas kernels, shards(): call(remap_kernel, [(forcing.shape, F32)], [pltpu.VMEM((4 * slots, 128),...  2.09 us
  transfers between devices with their start and end apart: 5, of which 2 were waited for; matrix products, arithmetic and copies ran while one was open for 0% of the time, Pallas kernels for 1%

profile of v1, /device:TPU:0, one launch (start us, length us, event | category | flops | bytes accessed | tf_op | source)
XLA Modules:
  0.0 47.6 jit_solution(11447019285644729936)
XLA Ops:
  0.7 1.6 %copy-done = f32[1,4,16,16,512]{4,3,2,1,0:T(8,128)S(1)} copy-done((f32[1,4,16,16,512]{4,3,2,1,0:T(8,128)S(1)}, f32[1,4,16,16,512]{4,3,2,1,0:T(8,128)}, u32[]{:S(2)}) %copy-start) | copy-done | bytes 2097176
  2.3 0.9 %copy-done.3 = f32[1,4,16,512]{3,2,1,0:T(8,128)S(1)} copy-done((f32[1,4,16,512]{3,2,1,0:T(8,128)S(1)}, f32[1,4,16,512]{3,2,1,0:T(8,128)}, u32[]{:S(2)}) %copy-start.3) | copy-done | bytes 131096
  3.2 0.8 %copy-done.4 = s32[1,16,512]{2,1,0:T(8,128)S(1)} copy-done((s32[1,16,512]{2,1,0:T(8,128)S(1)}, s32[1,16,512]{2,1,0:T(8,128)}, u32[]{:S(2)}) %copy-start.4) | copy-done | bytes 32792
  3.9 0.7 %copy-done.5 = s32[1,2048]{1,0:T(1,128)S(1)} copy-done((s32[1,2048]{1,0:T(1,128)S(1)}, s32[1,2048]{1,0:T(1,128)}, u32[]{:S(2)}) %copy-start.5) | copy-done | bytes 8216
  4.6 0.7 %copy-done.6 = f32[1,16,16]{2,1,0:T(8,128)S(1)} copy-done((f32[1,16,16]{2,1,0:T(8,128)S(1)}, f32[1,16,16]{2,1,0:T(8,128)}, u32[]{:S(2)}) %copy-start.6) | copy-done | bytes 1048
  5.3 0.7 %copy-done.7 = f32[1,16,16]{2,1,0:T(8,128)S(1)} copy-done((f32[1,16,16]{2,1,0:T(8,128)S(1)}, f32[1,16,16]{2,1,0:T(8,128)}, u32[]{:S(2)}) %copy-start.7) | copy-done | bytes 1048
  6.0 0.7 %copy-done.8 = f32[1,512]{1,0:T(1,128)S(1)} copy-done((f32[1,512]{1,0:T(1,128)S(1)}, f32[1,512]{1,0:T(1,128)}, u32[]{:S(2)}) %copy-start.8) | copy-done | bytes 2072
  6.7 0.7 %copy-done.9 = f32[1,3]{1,0:T(1,128)S(1)} copy-done((f32[1,3]{1,0:T(1,128)S(1)}, f32[1,3]{1,0:T(1,128)}, u32[]{:S(2)}) %copy-start.9) | copy-done | bytes 36
  7.4 3.9 %shard_map.122 = (f32[1024,512]{1,0:T(8,128)S(1)}, bf16[512,512]{1,0:T(8,128)(2,1)S(1)}, bf16[512,512]{1,0:T(8,128)(2,1)S(1)}, bf16[1024,1024]{1,0:T(8,128)(2,1)S(1)}, bf16[256,768]{1,0:T(8,128)(2,1)S(1)}) custom-call(f32[1024,512]{1,0:T(8,128)S(1)} %bitcast.3, f32[1,512]{1,0:T(1,128)S(1)} %copy-done.8, f32[1,16,16]{2,1,0:T(8,128)S(1)} %copy-done.6, ...), custom_call_target="tpu_custom_call" | custom-call | tf_op jit(solution)/shard_map/pallas_call | solution.py:222
  11.2 0.1 collective-permute-start
  11.3 8.7 %collective-permute-start.1 = (bf16[512,512]{1,0:T(8,128)(2,1)S(1)}, bf16[512,512]{1,0:T(8,128)(2,1)S(1)}, u32[]{:S(2)}, u32[]{:S(2)}) collective-permute-start(bf16[512,512]{1,0:T(8,128)(2,1)S(1)} %get-tuple-element.15), channel_id=1, source_target_pairs={{0,63},{1,2},{2,1},{3,4},{4,3},{5,6},{6,5},{7,8},{8,7},{9,10},{10,... | collective-permute-start | bytes 1572872 | tf_op jit(solution)/shard_map/ppermute | solution.py:227
  20.0 0.6 %shard_map.123 = (bf16[512,512]{1,0:T(8,128)(2,1)S(1)}, bf16[512,512]{1,0:T(8,128)(2,1)S(1)}, bf16[320,768]{1,0:T(8,128)(2,1)S(1)}, bf16[256,320]{1,0:T(8,128)(2,1)S(1)}) custom-call(s32[1,2048]{1,0:T(1,128)S(1)} %copy-done.5, s32[1,80]{1,0:T(1,128)S(1)} %copy-done.10, s32[1,80]{1,0:T(1,128)S(1)} %copy-done.11), custom_call_target="tpu_custom_call" | custom-call | tf_op jit(solution)/shard_map/pallas_call | solution.py:230
  20.6 0.0 collective-permute-done.even_ref
  20.6 6.4 %collective-permute-done.1.odd_ref = bf16[512,512]{1,0:T(8,128)(2,1)S(1)} collective-permute-done((bf16[512,512]{1,0:T(8,128)(2,1)S(1)}, bf16[512,512]{1,0:T(8,128)(2,1)S(1)}, u32[]{:S(2)}, u32[]{:S(2)}) %collective-permute-start.1) | collective-permute-done | bytes 524320 | tf_op jit(solution)/shard_map/ppermute | solution.py:227
  27.0 0.0 copy-done.1
  27.0 6.2 %shard_map.124 = (f32[1024,512]{1,0:T(8,128)}, bf16[256,128]{1,0:T(8,128)(2,1)S(1)}) custom-call(f32[1024,512]{1,0:T(8,128)S(1)} %bitcast.4, f32[1024,512]{1,0:T(8,128)S(1)} %get-tuple-element.13.part_ref, bf16[512,512]{1,0:T(8,128)(2,1)S(1)} %collective-permute-done.even_ref, bf16[512,512]{1,0:T(8,128)(2,1)S(1)} %collective-permute-done.1.odd_ref, ...), custom_call_target="tpu_custom_call" | custom-call | tf_op jit(solution)/shard_map/pallas_call | solution.py:234
  33.2 2.2 %collective-permute-start.4 = (bf16[256,128]{1,0:T(8,128)(2,1)S(1)}, bf16[256,128]{1,0:T(8,128)(2,1)S(1)}, u32[]{:S(2)}, u32[]{:S(2)}) collective-permute-start(bf16[256,128]{1,0:T(8,128)(2,1)S(1)} %get-tuple-element.21), channel_id=1, source_target_pairs={{0,65},{1,64},{2,67},{3,66},{4,69},{5,68},{6,71},{7,70},{8,73},{9,... | collective-permute-start | bytes 196616 | tf_op jit(solution)/shard_map/ppermute | solution.py:241
  35.3 0.4 collective-permute-start.3
  35.8 7.8 %collective-permute-start.2 = (bf16[256,128]{1,0:T(8,128)(2,1)S(1)}, bf16[256,128]{1,0:T(8,128)(2,1)S(1)}, u32[]{:S(2)}, u32[]{:S(2)}) collective-permute-start(bf16[256,128]{1,0:T(8,128)(2,1)S(1)} %get-tuple-element.21), channel_id=1, source_target_pairs={{0,127},{1,66},{2,65},{3,68},{4,67},{5,70},{6,69},{7,72},{8,71},{9... | collective-permute-start | bytes 196616 | tf_op jit(solution)/shard_map/ppermute | solution.py:240
  43.5 0.0 collective-permute-done.4.near_ref
  43.5 0.0 collective-permute-done.3.own_ref
  43.5 1.9 %collective-permute-done.2.far_ref = bf16[256,128]{1,0:T(8,128)(2,1)S(1)} collective-permute-done((bf16[256,128]{1,0:T(8,128)(2,1)S(1)}, bf16[256,128]{1,0:T(8,128)(2,1)S(1)}, u32[]{:S(2)}, u32[]{:S(2)}) %collective-permute-start.2) | collective-permute-done | bytes 65568 | tf_op jit(solution)/shard_map/ppermute | solution.py:240
  45.5 0.0 copy-done.2
  45.5 2.1 %shard_map.125 = f32[1,4,16,512]{3,2,1,0:T(8,128)} custom-call(bf16[256,128]{1,0:T(8,128)(2,1)S(1)} %collective-permute-done.2.far_ref, bf16[256,128]{1,0:T(8,128)(2,1)S(1)} %collective-permute-done.3.own_ref, bf16[256,128]{1,0:T(8,128)(2,1)S(1)} %collective-permute-done.4.near_ref, bf16[320,768]{1,0:T(8,128)(2,1)S(1)} %get-tuple-element.22.pick_ref, ...), custom_call_target="tpu_custom_call" | custom-call | tf_op jit(solution)/shard_map/pallas_call | solution.py:243
  (14 shorter events, 0.0 us)
Async XLA Ops:
  0.6 19.4 %copy-start.11 = (s32[1,80]{1,0:T(1,128)S(1)}, s32[1,80]{1,0:T(1,128)}, u32[]{:S(2)}) copy-start(s32[1,80]{1,0:T(1,128)} %cols_ref.1) | copy-start | bytes 964
  0.6 19.4 %copy-start.10 = (s32[1,80]{1,0:T(1,128)S(1)}, s32[1,80]{1,0:T(1,128)}, u32[]{:S(2)}) copy-start(s32[1,80]{1,0:T(1,128)} %rows_ref.1) | copy-start | bytes 964
  0.7 1.6 %copy-start = (f32[1,4,16,16,512]{4,3,2,1,0:T(8,128)S(1)}, f32[1,4,16,16,512]{4,3,2,1,0:T(8,128)}, u32[]{:S(2)}) copy-start(f32[1,4,16,16,512]{4,3,2,1,0:T(8,128)} %param.11) | copy-start | bytes 6291460
  2.3 0.9 %copy-start.3 = (f32[1,4,16,512]{3,2,1,0:T(8,128)S(1)}, f32[1,4,16,512]{3,2,1,0:T(8,128)}, u32[]{:S(2)}) copy-start(f32[1,4,16,512]{3,2,1,0:T(8,128)} %forcing_ref.3) | copy-start | bytes 393220
  3.2 0.8 %copy-start.4 = (s32[1,16,512]{2,1,0:T(8,128)S(1)}, s32[1,16,512]{2,1,0:T(8,128)}, u32[]{:S(2)}) copy-start(s32[1,16,512]{2,1,0:T(8,128)} %mask_ref.3) | copy-start | bytes 98308
  3.9 0.7 %copy-start.5 = (s32[1,2048]{1,0:T(1,128)S(1)}, s32[1,2048]{1,0:T(1,128)}, u32[]{:S(2)}) copy-start(s32[1,2048]{1,0:T(1,128)} %partner_ref.3) | copy-start | bytes 24580
  4.6 0.7 %copy-start.6 = (f32[1,16,16]{2,1,0:T(8,128)S(1)}, f32[1,16,16]{2,1,0:T(8,128)}, u32[]{:S(2)}) copy-start(f32[1,16,16]{2,1,0:T(8,128)} %node_ref.1) | copy-start | bytes 3076
  5.3 0.7 %copy-start.7 = (f32[1,16,16]{2,1,0:T(8,128)S(1)}, f32[1,16,16]{2,1,0:T(8,128)}, u32[]{:S(2)}) copy-start(f32[1,16,16]{2,1,0:T(8,128)} %level_ref.1) | copy-start | bytes 3076
  6.0 0.7 %copy-start.8 = (f32[1,512]{1,0:T(1,128)S(1)}, f32[1,512]{1,0:T(1,128)}, u32[]{:S(2)}) copy-start(f32[1,512]{1,0:T(1,128)} %metric_ref.3) | copy-start | bytes 6148
  6.7 0.7 %copy-start.9 = (f32[1,3]{1,0:T(1,128)S(1)}, f32[1,3]{1,0:T(1,128)}, u32[]{:S(2)}) copy-start(f32[1,3]{1,0:T(1,128)} %coeffs_ref.3) | copy-start | bytes 40
  7.4 19.6 %copy-start.1 = (f32[1,4,16,16,512]{4,3,2,1,0:T(8,128)S(1)}, f32[1,4,16,16,512]{4,3,2,1,0:T(8,128)}, u32[]{:S(2)}) copy-start(f32[1,4,16,16,512]{4,3,2,1,0:T(8,128)} %param.11) | copy-start | bytes 6291460
  11.2 9.4 %collective-permute-start = (bf16[512,512]{1,0:T(8,128)(2,1)S(1)}, bf16[512,512]{1,0:T(8,128)(2,1)S(1)}, u32[]{:S(2)}, u32[]{:S(2)}) collective-permute-start(bf16[512,512]{1,0:T(8,128)(2,1)S(1)} %get-tuple-element.14), channel_id=1, source_target_pairs={{0,1},{1,0},{2,3},{3,2},{4,5},{5,4},{6,7},{7,6},{8,9},{9,8},{10,11... | collective-permute-start | bytes 1572872 | tf_op jit(solution)/shard_map/ppermute | solution.py:228
  11.3 15.7 %collective-permute-start.1 = (bf16[512,512]{1,0:T(8,128)(2,1)S(1)}, bf16[512,512]{1,0:T(8,128)(2,1)S(1)}, u32[]{:S(2)}, u32[]{:S(2)}) collective-permute-start(bf16[512,512]{1,0:T(8,128)(2,1)S(1)} %get-tuple-element.15), channel_id=1, source_target_pairs={{0,63},{1,2},{2,1},{3,4},{4,3},{5,6},{6,5},{7,8},{8,7},{9,10},{10,... | collective-permute-start | bytes 1572872 | tf_op jit(solution)/shard_map/ppermute | solution.py:227
  27.0 18.5 %copy-start.2 = (bf16[1,80,128,128]{3,2,1,0:T(8,128)(2,1)S(1)}, bf16[1,80,128,128]{3,2,1,0:T(8,128)(2,1)}, u32[]{:S(2)}) copy-start(bf16[1,80,128,128]{3,2,1,0:T(8,128)(2,1)} %param.19) | copy-start | bytes 7864324
  33.2 10.4 %collective-permute-start.4 = (bf16[256,128]{1,0:T(8,128)(2,1)S(1)}, bf16[256,128]{1,0:T(8,128)(2,1)S(1)}, u32[]{:S(2)}, u32[]{:S(2)}) collective-permute-start(bf16[256,128]{1,0:T(8,128)(2,1)S(1)} %get-tuple-element.21), channel_id=1, source_target_pairs={{0,65},{1,64},{2,67},{3,66},{4,69},{5,68},{6,71},{7,70},{8,73},{9,... | collective-permute-start | bytes 196616 | tf_op jit(solution)/shard_map/ppermute | solution.py:241
  35.3 8.2 %collective-permute-start.3 = (bf16[256,128]{1,0:T(8,128)(2,1)S(1)}, bf16[256,128]{1,0:T(8,128)(2,1)S(1)}, u32[]{:S(2)}, u32[]{:S(2)}) collective-permute-start(bf16[256,128]{1,0:T(8,128)(2,1)S(1)} %get-tuple-element.21), channel_id=1, source_target_pairs={{0,64},{1,65},{2,66},{3,67},{4,68},{5,69},{6,70},{7,71},{8,72},{9,... | collective-permute-start | bytes 196616 | tf_op jit(solution)/shard_map/ppermute | solution.py:242
  35.8 9.7 %collective-permute-start.2 = (bf16[256,128]{1,0:T(8,128)(2,1)S(1)}, bf16[256,128]{1,0:T(8,128)(2,1)S(1)}, u32[]{:S(2)}, u32[]{:S(2)}) collective-permute-start(bf16[256,128]{1,0:T(8,128)(2,1)S(1)} %get-tuple-element.21), channel_id=1, source_target_pairs={{0,127},{1,66},{2,65},{3,68},{4,67},{5,70},{6,69},{7,72},{8,71},{9... | collective-permute-start | bytes 196616 | tf_op jit(solution)/shard_map/ppermute | solution.py:240

commit v2 on v1

--- a/solution.py
+++ b/solution.py
@@ -64,60 +64,175 @@
     return 0.8 - 0.3 * metric - penalty * edges
 
 
-def exchange_rate(coeffs_ref, mask_ref):
-    mask = mask_ref[0].astype(F32)
-    return coeffs_ref[0, 1] * mask + coeffs_ref[0, 2] * (1.0 - mask)
+def exchange_rate(coeffs, mask):
+    mask = mask.astype(F32)
+    return coeffs[:, 1:2] * mask + coeffs[:, 2:3] * (1.0 - mask)
 
 
 def levels_of(pattern):
     return jnp.concatenate([pattern] * 16, axis=0)
 
 
+def halves(value):
+    high = value.astype(BF16)
+    return high, (value - high.astype(F32)).astype(BF16)
+
+
+def low_select():
+    row = iota((64, 64), 0)
+    group = row // 16
+    edge = jnp.where(group == 0, 0, jnp.where(group == 1, 3, group - 1))
+    wanted = (row % 16 // 4) * 16 + node_of(edge, row % 4)
+    return (iota((64, 64), 1) == wanted).astype(BF16)
+
+
+def low_spread(first, second):
+    col = iota((64, 64), 1)
+    edge = jnp.where(col < 32, first, second)
+    wanted = (col % 16 // 4) * 16 + node_of(edge, 3 - col % 4)
+    return (iota((64, 64), 0) == wanted).astype(BF16)
+
+
+def low_node_matrix(node):
+    row, col = iota((64, 64), 0), iota((64, 64), 1)
+    rows_of = (iota((64, 16), 0) % 16 == iota((64, 16), 1)).astype(BF16)
+    cols_of = (iota((16, 64), 1) % 16 == iota((16, 64), 0)).astype(BF16)
+    parts = [dot(dot(rows_of, part).astype(BF16), cols_of) for part in halves(node)]
+    high, low = [jnp.where(row // 16 == col // 16, part, 0.0).astype(BF16) for part in parts]
+    return jnp.concatenate([high, high, low], axis=1)
+
+
+def low_node_product(matrix, value):
+    high, low = halves(value)
+    return dot(matrix, jnp.concatenate([high, low, high], axis=0))
+
+
+def mix_to_lowest(level, ref, add):
+    parts = []
+    for v in range(4):
+        total = add
+        for m in range(16):
+            term = level[0:1, m : m + 1] * ref[256 * v + 16 * m : 256 * v + 16 * (m + 1), :]
+            total = term if total is None else total + term
+        parts.append(total)
+    return jnp.concatenate(parts, axis=0)
+
+
 def local_kernel(
-    state_ref, metric_ref, node_ref, level_ref, coeffs_ref, partner_ref, mask_ref, forcing_ref,
-    part_ref, even_ref, odd_ref, inner_ref, weights_ref, edges,
+    state_hbm, metric_hbm, node_hbm, level_hbm, coeffs_hbm, partner_hbm, mask_hbm, forcing_hbm,
+    part_ref, even_ref, odd_ref, even_low_ref, odd_low_ref, inner_ref, before_ref, after_ref,
+    weights_ref, low_ref, base_ref, factor_ref, low_node_ref,
+    state_ref, metric_ref, node_ref, level_ref, coeffs_ref, partner_ref, mask_ref, forcing_ref, edges, sems,
 ):
-    penalty = coeffs_ref[0, 0]
+    copies = [
+        pltpu.make_async_copy(source, target, sems.at[i])
+        for i, (source, target) in enumerate([
+            (partner_hbm, partner_ref), (node_hbm, node_ref), (level_hbm, level_ref), (coeffs_hbm, coeffs_ref),
+            (metric_hbm, metric_ref), (state_hbm, state_ref), (mask_hbm, mask_ref), (forcing_hbm, forcing_ref),
+        ])
+    ]
+    for copy in copies:
+        copy.start()
+    select, select_low = select_matrix(), low_select()
+    spread_inner, spread = low_spread(1, 2), spread_matrix()
+    weights_ref[:, 512:768] = spread
+    for copy in copies[:5]:
+        copy.wait()
+    for step in range(4):
+        columns = partner_ref[0:1, 512 + 256 * step : 768 + 256 * step] - 1024
+        inner_ref[:, 256 * step : 256 * (step + 1)] = (iota((1024, 256), 0) == columns).astype(BF16)
+    before_ref[...] = (iota((512, 512), 0) == partner_ref[0:1, 0:512]).astype(BF16)
+    after_ref[...] = (iota((512, 512), 0) == partner_ref[0:1, 1536:2048] - 2560).astype(BF16)
+    coeffs = coeffs_ref[...]
+    penalty = coeffs[:, 0:1]
     metric = metric_ref[...]
     node, level = coupling_matrices(node_ref, level_ref)
     weights_ref[:, 0:256] = node
     weights_ref[:, 256:512] = level
-    weights_ref[:, 512:768] = spread_matrix()
-    select = select_matrix()
-    for step in range(4):
-        columns = partner_ref[0:1, 512 + 256 * step : 768 + 256 * step] - 1024
-        inner_ref[:, 256 * step : 256 * (step + 1)] = (iota((1024, 256), 0) == columns).astype(BF16)
+    low_node = low_node_matrix(node_ref[0])
+    low_node_ref[...] = low_node
     even = lax.rem(lax.axis_index("tile"), 2) == 0
-    for v in range(4):
-        rows = slice(256 * v, 256 * (v + 1))
-        scaled = (penalty * state_ref[rows, :]).astype(BF16)
+    factor = diagonal(metric, penalty)
+    for copy in copies[5:]:
+        copy.wait()
+    for v in range(4):
+        scaled = (penalty * state_ref[256 * v : 256 * (v + 1), :]).astype(BF16)
         picked = dot(select, scaled).astype(BF16)
         first, last = picked[0:64], picked[64:128]
         even_ref[64 * v : 64 * (v + 1), :] = jnp.where(even, last, first)
         odd_ref[64 * v : 64 * (v + 1), :] = jnp.where(even, first, last)
         edges[64 * v : 64 * (v + 1), 0:512] = picked[128:192]
         edges[64 * v : 64 * (v + 1), 512:1024] = picked[192:256]
+    lowest = jnp.concatenate([state_ref[256 * v : 256 * v + 16, :] for v in range(4)], axis=0)
+    high, low = [dot(select_low, part).astype(BF16) for part in halves(penalty * lowest)]
+    even_low_ref[0:16, :] = jnp.where(even, high[16:32], high[0:16])
+    even_low_ref[16:32, :] = jnp.where(even, low[16:32], low[0:16])
+    odd_low_ref[0:16, :] = jnp.where(even, high[0:16], high[16:32])
+    odd_low_ref[16:32, :] = jnp.where(even, low[0:16], low[16:32])
+    edges[256:272, 0:512] = high[32:48]
+    edges[256:272, 512:1024] = high[48:64]
+    edges[272:288, 0:512] = low[32:48]
+    edges[272:288, 512:1024] = low[48:64]
     moved = dot(edges[...], inner_ref[...]).astype(BF16)
-    factor = levels_of(diagonal(metric, penalty))
-    rate = exchange_rate(coeffs_ref, mask_ref)
+    rate = exchange_rate(coeffs, mask_ref[0])
+    rates = jnp.concatenate([rate] * 4, axis=0)
+    forced = rates * jnp.concatenate([forcing_ref[0, v] for v in range(4)], axis=0)
+    factor_low = factor - rate
+    factor_ref[...] = factor_low
+    mixed = mix_to_lowest(level_ref[0], state_ref, None)
+    near = moved[256:288]
+    p_low = jnp.concatenate([factor_low] * 4, axis=0) * lowest + forced + mixed
+    p_low = p_low + low_node_product(low_node, lowest * metric)
+    p_low = p_low + dot(spread_inner, jnp.concatenate([near[:, 0:512], near[:, 512:1024]], axis=0))
+    low_ref[...] = p_low
+    high, low = [dot(select_low[0:32], part).astype(BF16) for part in halves(penalty * (p_low + mixed))]
+    even_low_ref[32:48, :] = jnp.where(even, high[16:32], high[0:16])
+    even_low_ref[48:64, :] = jnp.where(even, low[16:32], low[0:16])
+    odd_low_ref[32:48, :] = jnp.where(even, high[0:16], high[16:32])
+    odd_low_ref[48:64, :] = jnp.where(even, low[0:16], low[16:32])
+    factors = levels_of(factor)
     for v in range(4):
         rows = slice(256 * v, 256 * (v + 1))
         u = state_ref[rows, :]
         near = moved[64 * v : 64 * (v + 1)]
-        p = factor * u + dot(node, (u * metric).astype(BF16)) + dot(level, u.astype(BF16))
-        p = p + dot(weights_ref[:, 640:704], near[:, 0:512]) + dot(weights_ref[:, 704:768], near[:, 512:1024])
+        p = factors * u + dot(node, (u * metric).astype(BF16)) + dot(level, u.astype(BF16))
+        p = p + dot(spread[:, 128:192], near[:, 0:512]) + dot(spread[:, 192:256], near[:, 512:1024])
+        p = jnp.concatenate([p_low[16 * v : 16 * (v + 1)], p[16:256]], axis=0)
         part_ref[rows, :] = p
-        part_ref[256 * v : 256 * v + 16, :] += rate * (forcing_ref[0, v] - u[0:16])
-        p = part_ref[rows, :]
         picked = dot(select[0:128], (penalty * p).astype(BF16)).astype(BF16)
         first, last = picked[0:64], picked[64:128]
         even_ref[256 + 64 * v : 320 + 64 * v, :] = jnp.where(even, last, first)
         odd_ref[256 + 64 * v : 320 + 64 * v, :] = jnp.where(even, first, last)
-
-
-def tables_kernel(partner_ref, rows_ref, cols_ref, before_ref, after_ref, pick_ref, sum_ref):
-    before_ref[...] = (iota((512, 512), 0) == partner_ref[0:1, 0:512]).astype(BF16)
-    after_ref[...] = (iota((512, 512), 0) == partner_ref[0:1, 1536:2048] - 2560).astype(BF16)
+    mixed = mix_to_lowest(level_ref[0], part_ref, None)
+    node_at = iota((64, 1), 0) % 16
+    facing = jnp.where((node_at // 4 == 0) | (node_at // 4 == 3), penalty * penalty, 0.0)
+    base_ref[...] = mixed + forced + facing * lowest
+
+
+def lowest_kernel(
+    low_ref, base_ref, factor_ref, low_node_ref, metric_ref, coeffs_ref, even_ref, odd_ref, before_ref, after_ref, inner_ref,
+    surface_ref,
+):
+    penalty = coeffs_ref[:, 0:1]
+    even = lax.rem(lax.axis_index("tile"), 2) == 0
+    before = dot(jnp.where(even, odd_ref[...], even_ref[...]), before_ref[...]).astype(BF16)
+    after = dot(jnp.where(even, even_ref[...], odd_ref[...]), after_ref[...]).astype(BF16)
+    outer, inner, select = low_spread(0, 3), low_spread(1, 2), low_select()
+    u1 = low_ref[...] + dot(outer, jnp.concatenate([before[0:32], after[0:32]], axis=0))
+    high, low = [dot(select[32:64], part).astype(BF16) for part in halves(penalty * u1)]
+    sides = [jnp.concatenate([high[at : at + 16], low[at : at + 16]], axis=0) for at in (0, 16)]
+    near = dot(jnp.concatenate(sides, axis=1), inner_ref[...]).astype(BF16)
+    x = base_ref[...] + jnp.concatenate([factor_ref[...]] * 4, axis=0) * u1
+    x = x + low_node_product(low_node_ref[...], u1 * metric_ref[...])
+    x = x + dot(outer, jnp.concatenate([before[32:64], after[32:64]], axis=0))
+    x = x + dot(inner, jnp.concatenate([near[:, 0:512], near[:, 512:1024]], axis=0))
+    x = x.astype(BF16)
+    for v in range(4):
+        for q in range(4):
+            surface_ref[64 * v + 16 * q : 64 * v + 16 * (q + 1), :] = x[16 * v : 16 * (v + 1), 128 * q : 128 * (q + 1)]
+
+
+def tables_kernel(rows_ref, cols_ref, even_in, odd_in, pick_ref, sum_ref, even_out, odd_out):
     odd = lax.rem(lax.axis_index("tile"), 2)
     slots = rows_ref.shape[1]
     wide = 4 * slots
@@ -136,9 +251,10 @@
 def finish_kernel(
     state_ref, part_ref, even_ref, odd_ref, before_ref, after_ref, inner_ref, weights_ref,
     metric_ref, coeffs_ref, mask_ref, forcing_ref,
-    next_ref, surface_ref, edges, halo_before, halo_after,
+    next_hbm, next_ref, edges, halo_before, halo_after, sems,
 ):
-    penalty = coeffs_ref[0, 0]
+    coeffs = coeffs_ref[...]
+    penalty = coeffs[:, 0:1]
     metric = metric_ref[...]
     even = lax.rem(lax.axis_index("tile"), 2) == 0
     halo_before[...] = dot(jnp.where(even, odd_ref[...], even_ref[...]), before_ref[...]).astype(BF16)
@@ -157,7 +273,8 @@
     factor = levels_of(diagonal(metric, penalty))
     node = iota((256, 1), 0) % 16
     facing = jnp.where((node // 4 == 0) | (node // 4 == 3), penalty * penalty, 0.0)
-    rate = exchange_rate(coeffs_ref, mask_ref)
+    rate = exchange_rate(coeffs, mask_ref[0])
+    copies = []
     for v in range(4):
         rows = slice(256 * v, 256 * (v + 1))
         far = slice(256 + 64 * v, 256 + 64 * (v + 1))
@@ -170,11 +287,13 @@
         next_ref[rows, :] = x
         lowest = x[0:16] + rate * (forcing_ref[0, v] - u1[0:16])
         next_ref[256 * v : 256 * v + 16, :] = lowest
-        for q in range(4):
-            surface_ref[64 * v + 16 * q : 64 * v + 16 * (q + 1), :] = lowest[:, 128 * q : 128 * (q + 1)].astype(BF16)
-
-
-def remap_kernel(far_ref, own_ref, near_ref, pick_ref, sum_ref, blocks_ref, out_ref, products):
+        copies.append(pltpu.make_async_copy(next_ref.at[rows], next_hbm.at[rows], sems.at[v]))
+        copies[-1].start()
+    for copy in copies:
+        copy.wait()
+
+
+def remap_kernel(own_ref, near_ref, far_ref, pick_ref, sum_ref, blocks_ref, out_ref, products):
     picked = dot(pick_ref[:, 0:256], far_ref[...])
     picked = picked + dot(pick_ref[:, 256:512], own_ref[...])
     picked = picked + dot(pick_ref[:, 512:768], near_ref[...])
@@ -196,15 +315,18 @@
             out_ref[0, v, :, 128 * q : 128 * (q + 1)] = total[64 * v + 16 * q : 64 * v + 16 * (q + 1)]
 
 
-def call(kernel, outs, scratch=(), smem=(), count=0):
-    vmem = pl.BlockSpec(memory_space=pltpu.VMEM)
-    specs = [pl.BlockSpec(memory_space=pltpu.SMEM) if i in smem else vmem for i in range(count)]
+def call(kernel, outs, scratch=(), inputs="", results="", aliases={}, cost=0):
+    spaces = {"v": pltpu.VMEM, "h": pltpu.HBM, "a": pl.ANY}
+    place = lambda kind: pl.BlockSpec(memory_space=spaces[kind])
+    results = results or "v" * len(outs)
     return pl.pallas_call(
         kernel,
         out_shape=[jax.ShapeDtypeStruct(shape, kind) for shape, kind in outs],
-        in_specs=specs,
-        out_specs=[vmem] * len(outs),
+        in_specs=[place(kind) for kind in inputs],
+        out_specs=[place(kind) for kind in results],
+        input_output_aliases=aliases,
         scratch_shapes=list(scratch),
+        cost_estimate=pl.CostEstimate(flops=cost, bytes_accessed=0, transcendentals=0) if cost else None,
         compiler_params=pltpu.CompilerParams(vmem_limit_bytes=VMEM_LIMIT),
     )
 
@@ -219,30 +341,46 @@
     crossed = lambda pairs: [(c * tiles + a, (1 - c) * tiles + b) for c in range(2) for a, b in pairs]
     straight = [(t, t) for t in range(tiles)]
     flat = state.reshape(1024, 512)
-    part, even, odd, inner, weights = call(
+    inputs = (flat, metric, element_coupling, level_coupling, coeffs, edge_partner, sea_mask, forcing)
+    (part, even, odd, even_low, odd_low, inner, before, after, weights, low, base, factor, low_node) = call(
         local_kernel,
-        [((1024, 512), F32), ((512, 512), BF16), ((512, 512), BF16), ((1024, 1024), BF16), ((256, 768), BF16)],
-        [pltpu.VMEM((256, 1024), BF16)], smem=(4,), count=8,
-    )(flat, metric, element_coupling, level_coupling, coeffs, edge_partner, sea_mask, forcing)
+        [
+            ((1024, 512), F32), ((512, 512), BF16), ((512, 512), BF16), ((64, 512), BF16), ((64, 512), BF16),
+            ((1024, 1024), BF16), ((512, 512), BF16), ((512, 512), BF16), ((256, 768), BF16),
+            ((64, 512), F32), ((64, 512), F32), ((16, 512), F32), ((64, 192), BF16),
+        ],
+        [pltpu.VMEM(value.shape, value.dtype) for value in inputs]
+        + [pltpu.VMEM((288, 1024), BF16), pltpu.SemaphoreType.DMA((8,))],
+        "hhhhhhhh",
+    )(*[pltpu.with_memory_space_constraint(value, pltpu.HBM) for value in inputs])
+    odd_low = lax.ppermute(odd_low, "tile", away)
+    even_low = lax.ppermute(even_low, "tile", here)
+    slots = remap_rows.shape[1]
+    pick, total, even, odd = call(
+        tables_kernel,
+        [((4 * slots, 768), BF16), ((256, 4 * slots), BF16), (even.shape, BF16), (odd.shape, BF16)],
+        inputs="vvaa", results="vvaa", aliases={2: 2, 3: 3}, cost=4_000_000_000,
+    )(remap_rows, remap_cols, even, odd)
     odd = lax.ppermute(odd, "tile", away)
     even = lax.ppermute(even, "tile", here)
-    slots = remap_rows.shape[1]
-    before, after, pick, total = call(
-        tables_kernel,
-        [((512, 512), BF16), ((512, 512), BF16), ((4 * slots, 768), BF16), ((256, 4 * slots), BF16)], count=3,
-    )(edge_partner, remap_rows, remap_cols)
-    nxt, surface = call(
-        finish_kernel,
-        [((1024, 512), F32), ((256, 128), BF16)],
-        [pltpu.VMEM((256, 1024), BF16), pltpu.VMEM((512, 512), BF16), pltpu.VMEM((512, 512), BF16)],
-        smem=(9,), count=12,
-    )(flat, part, even, odd, before, after, inner, weights, metric, coeffs, sea_mask, forcing)
+    (surface,) = call(lowest_kernel, [((256, 128), BF16)], inputs="v" * 11, cost=40_000_000_000)(
+        low, base, factor, low_node, metric, coeffs, even_low, odd_low, before, after, inner
+    )
     far = lax.ppermute(surface, ("comp", "tile"), crossed(away))
     near = lax.ppermute(surface, ("comp", "tile"), crossed(here))
     own = lax.ppermute(surface, ("comp", "tile"), crossed(straight))
+    (nxt,) = call(
+        finish_kernel,
+        [((1024, 512), F32)],
+        [
+            pltpu.VMEM((1024, 512), F32), pltpu.VMEM((256, 1024), BF16), pltpu.VMEM((512, 512), BF16),
+            pltpu.VMEM((512, 512), BF16), pltpu.SemaphoreType.DMA((4,)),
+        ],
+        "v" * 12, "h",
+    )(flat, part, even, odd, before, after, inner, weights, metric, coeffs, sea_mask, forcing)
     (new_forcing,) = call(
-        remap_kernel, [(forcing.shape, F32)], [pltpu.VMEM((4 * slots, 128), F32)], count=6,
-    )(far, own, near, pick, total, remap_weights[0])
+        remap_kernel, [(forcing.shape, F32)], [pltpu.VMEM((4 * slots, 128), F32)], "v" * 6,
+    )(own, near, far, pick, total, remap_weights[0])
     return nxt.reshape(state.shape), new_forcing
 
 

time: 48 us -> 41.1 us (0.86)
  the two profiles are of different devices: /device:TPU:0 before, /device:TPU:64 now
where the time goes in v2:
time: 41.1 us; the launch traced here: 41 us
  Pallas kernels  15.2 us (37%)
  waiting for transfers between devices  14.6 us (36%)
  starting transfers between devices  10.4 us (25%)
  between operations  0.79 us (2%)
    ppermute x1, waiting for transfers between devices, shards(): far = lax.ppermute(surface, ('comp', 'tile'), crossed(away))  7.69 us
    ppermute x1, starting transfers between devices, shards(): odd = lax.ppermute(odd, 'tile', away)  7.53 us
    pallas_call x1, Pallas kernels, shards(): call(local_kernel, [((1024, 512), F32), ((512, 512), BF16), ((512, 512),...  6.38 us
    pallas_call x1, Pallas kernels, shards(): call(finish_kernel, [((1024, 512), F32)], [pltpu.VMEM((1024, 512), F32),...  5.12 us
    ppermute x1, waiting for transfers between devices, shards(): near = lax.ppermute(surface, ('comp', 'tile'), crossed(here))  3.65 us
    ppermute x1, waiting for transfers between devices, shards(): own = lax.ppermute(surface, ('comp', 'tile'), crossed(straight))  3.27 us
    pallas_call x1, Pallas kernels, shards(): call(remap_kernel, [(forcing.shape, F32)], [pltpu.VMEM((4 * slots, 128),...  2.09 us
    ppermute x1, starting transfers between devices, shards(): own = lax.ppermute(surface, ('comp', 'tile'), crossed(straight))  1.7 us
  transfers between devices with their start and end apart: 7, of which 3 were waited for; matrix products, arithmetic and copies ran while one was open for 0% of the time, Pallas kernels for 9%

profile of v2, /device:TPU:64, one launch (start us, length us, event | category | flops | bytes accessed | tf_op | source)
XLA Modules:
  0.0 41.0 jit_solution(17648258148646438466)
XLA Ops:
  0.7 6.4 %shard_map.122 = (f32[1024,512]{1,0:T(8,128)S(1)}, bf16[512,512]{1,0:T(8,128)(2,1)S(1)}, bf16[512,512]{1,0:T(8,128)(2,1)S(1)}, bf16[64,512]{1,0:T(8,128)(2,1)S(1...) custom-call(f32[1024,512]{1,0:T(8,128)} %bitcast.3, ...), custom_call_target="tpu_custom_call" | custom-call | tf_op jit(solution)/shard_map/pallas_call | solution.py:345
  7.0 0.1 collective-permute-start.2
  7.1 0.1 collective-permute-start.3
  7.2 0.0 copy-start.4
  7.3 0.0 copy-start.5
  7.3 0.4 %shard_map.123 = (bf16[320,768]{1,0:T(8,128)(2,1)S(1)}, bf16[256,320]{1,0:T(8,128)(2,1)S(1)}, bf16[512,512]{1,0:T(8,128)(2,1)S(1)}, bf16[512,512]{1,0:T(8,128)(2,1)S(1)}) custom-call(s32[1,80]{1,0:T(1,128)S(1)} %copy-done.6, s32[1,80]{1,0:T(1,128)S(1)} %copy-done.7, ...), custom_call_target="tpu_custom_call", output_to_operand_aliasing={{2}: (2, {}), {3}: (3, {})} | custom-call | flops 4000000000 | tf_op jit(solution)/shard_map/pallas_call | solution.py:359
  7.7 0.8 %collective-permute-start = (bf16[512,512]{1,0:T(8,128)(2,1)S(1)}, bf16[512,512]{1,0:T(8,128)(2,1)S(1)}, u32[]{:S(2)}, u32[]{:S(2)}) collective-permute-start(bf16[512,512]{1,0:T(8,128)(2,1)S(1)} %get-tuple-element.22), channel_id=1, source_target_pairs={{0,1},{1,0},{2,3},{3,2},{4,5},{5,4},{6,7},{7,6},{8,9},{9,8},{10,11... | collective-permute-start | bytes 1572872 | tf_op jit(solution)/shard_map/ppermute | solution.py:365
  8.5 7.5 %collective-permute-start.1 = (bf16[512,512]{1,0:T(8,128)(2,1)S(1)}, bf16[512,512]{1,0:T(8,128)(2,1)S(1)}, u32[]{:S(2)}, u32[]{:S(2)}) collective-permute-start(bf16[512,512]{1,0:T(8,128)(2,1)S(1)} %get-tuple-element.23), channel_id=1, source_target_pairs={{0,63},{1,2},{2,1},{3,4},{4,3},{5,6},{6,5},{7,8},{8,7},{9,10},{10,... | collective-permute-start | bytes 1572872 | tf_op jit(solution)/shard_map/ppermute | solution.py:364
  16.1 0.0 collective-permute-done.2.even_ref
  16.1 0.0 collective-permute-done.3.odd_ref
  16.1 0.0 copy-start.1
  16.1 1.1 %shard_map.125 = bf16[256,128]{1,0:T(8,128)(2,1)S(1)} custom-call(f32[64,512]{1,0:T(8,128)S(1)} %get-tuple-element.28.low_ref, f32[64,512]{1,0:T(8,128)S(1)} %get-tuple-element.29.base_ref, f32[16,512]{1,0:T(8,128)S(1)} %get-tuple-element.30.factor_ref, bf16[64,192]{1,0:T(8,128)(2,1)S(1)} %get-tuple-element.31.low_node_ref, f32[1,512]{1,0:T(1,128)S(1)} %copy-done.4, ...), custom_call_target="tpu_custom_call" | custom-call | flops 40000000000 | tf_op jit(solution)/shard_map/pallas_call | solution.py:366
  17.2 0.0 copy-start.2
  17.2 0.0 copy-start.3
  17.3 0.1 collective-permute-start.6
  17.3 0.1 collective-permute-start.5
  17.4 1.7 %collective-permute-start.4 = (bf16[256,128]{1,0:T(8,128)(2,1)S(1)}, bf16[256,128]{1,0:T(8,128)(2,1)S(1)}, u32[]{:S(2)}, u32[]{:S(2)}) collective-permute-start(bf16[256,128]{1,0:T(8,128)(2,1)S(1)} %shard_map.125), channel_id=1, source_target_pairs={{0,64},{1,65},{2,66},{3,67},{4,68},{5,69},{6,70},{7,71},{8,72},{9,... | collective-permute-start | bytes 196616 | tf_op jit(solution)/shard_map/ppermute | solution.py:371
  19.1 7.7 %collective-permute-done.6.far_ref = bf16[256,128]{1,0:T(8,128)(2,1)S(1)} collective-permute-done((bf16[256,128]{1,0:T(8,128)(2,1)S(1)}, bf16[256,128]{1,0:T(8,128)(2,1)S(1)}, u32[]{:S(2)}, u32[]{:S(2)}) %collective-permute-start.6) | collective-permute-done | bytes 65568 | tf_op jit(solution)/shard_map/ppermute | solution.py:369
  26.8 3.7 %collective-permute-done.5.near_ref = bf16[256,128]{1,0:T(8,128)(2,1)S(1)} collective-permute-done((bf16[256,128]{1,0:T(8,128)(2,1)S(1)}, bf16[256,128]{1,0:T(8,128)(2,1)S(1)}, u32[]{:S(2)}, u32[]{:S(2)}) %collective-permute-start.5) | collective-permute-done | bytes 65568 | tf_op jit(solution)/shard_map/ppermute | solution.py:370
  30.5 3.3 %collective-permute-done.4.own_ref = bf16[256,128]{1,0:T(8,128)(2,1)S(1)} collective-permute-done((bf16[256,128]{1,0:T(8,128)(2,1)S(1)}, bf16[256,128]{1,0:T(8,128)(2,1)S(1)}, u32[]{:S(2)}, u32[]{:S(2)}) %collective-permute-start.4) | collective-permute-done | bytes 65568 | tf_op jit(solution)/shard_map/ppermute | solution.py:371
  33.8 2.1 %shard_map.126 = f32[1,4,16,512]{3,2,1,0:T(8,128)} custom-call(bf16[256,128]{1,0:T(8,128)(2,1)S(1)} %collective-permute-done.4.own_ref, bf16[256,128]{1,0:T(8,128)(2,1)S(1)} %collective-permute-done.5.near_ref, bf16[256,128]{1,0:T(8,128)(2,1)S(1)} %collective-permute-done.6.far_ref, bf16[320,768]{1,0:T(8,128)(2,1)S(1)} %get-tuple-element.34.pick_ref, ...), custom_call_target="tpu_custom_call" | custom-call | tf_op jit(solution)/shard_map/pallas_call | solution.py:381
  35.8 0.0 collective-permute-done.even_ref
  35.9 0.0 collective-permute-done.1.odd_ref
  35.9 5.1 %shard_map.124 = f32[1024,512]{1,0:T(8,128)} custom-call(f32[1024,512]{1,0:T(8,128)S(1)} %bitcast.4, f32[1024,512]{1,0:T(8,128)S(1)} %get-tuple-element.19.part_ref, bf16[512,512]{1,0:T(8,128)(2,1)S(1)} %collective-permute-done.even_ref, bf16[512,512]{1,0:T(8,128)(2,1)S(1)} %collective-permute-done.1.odd_ref, ...), custom_call_target="tpu_custom_call" | custom-call | tf_op jit(solution)/shard_map/pallas_call | solution.py:372
  (11 shorter events, 0.0 us)
Async XLA Ops:
  0.6 6.6 %copy-start.7 = (s32[1,80]{1,0:T(1,128)S(1)}, s32[1,80]{1,0:T(1,128)}, u32[]{:S(2)}) copy-start(s32[1,80]{1,0:T(1,128)} %cols_ref.1) | copy-start | bytes 964
  0.6 6.6 %copy-start.6 = (s32[1,80]{1,0:T(1,128)S(1)}, s32[1,80]{1,0:T(1,128)}, u32[]{:S(2)}) copy-start(s32[1,80]{1,0:T(1,128)} %rows_ref.1) | copy-start | bytes 964
  7.0 9.0 %collective-permute-start.2 = (bf16[64,512]{1,0:T(8,128)(2,1)S(1)}, bf16[64,512]{1,0:T(8,128)(2,1)S(1)}, u32[]{:S(2)}, u32[]{:S(2)}) collective-permute-start(bf16[64,512]{1,0:T(8,128)(2,1)S(1)} %get-tuple-element.32), channel_id=1, source_target_pairs={{0,1},{1,0},{2,3},{3,2},{4,5},{5,4},{6,7},{7,6},{8,9},{9,8},{10,11... | collective-permute-start | bytes 196616 | tf_op jit(solution)/shard_map/ppermute | solution.py:357
  7.1 8.9 %collective-permute-start.3 = (bf16[64,512]{1,0:T(8,128)(2,1)S(1)}, bf16[64,512]{1,0:T(8,128)(2,1)S(1)}, u32[]{:S(2)}, u32[]{:S(2)}) collective-permute-start(bf16[64,512]{1,0:T(8,128)(2,1)S(1)} %get-tuple-element.33), channel_id=1, source_target_pairs={{0,63},{1,2},{2,1},{3,4},{4,3},{5,6},{6,5},{7,8},{8,7},{9,10},{10,... | collective-permute-start | bytes 196616 | tf_op jit(solution)/shard_map/ppermute | solution.py:356
  7.2 8.8 %copy-start.4 = (f32[1,512]{1,0:T(1,128)S(1)}, f32[1,512]{1,0:T(1,128)}, u32[]{:S(2)}) copy-start(f32[1,512]{1,0:T(1,128)} %metric_ref.3) | copy-start | bytes 6148
  7.3 8.8 %copy-start.5 = (f32[1,3]{1,0:T(1,128)S(1)}, f32[1,3]{1,0:T(1,128)}, u32[]{:S(2)}) copy-start(f32[1,3]{1,0:T(1,128)} %coeffs_ref.3) | copy-start | bytes 40
  7.7 28.1 %collective-permute-start = (bf16[512,512]{1,0:T(8,128)(2,1)S(1)}, bf16[512,512]{1,0:T(8,128)(2,1)S(1)}, u32[]{:S(2)}, u32[]{:S(2)}) collective-permute-start(bf16[512,512]{1,0:T(8,128)(2,1)S(1)} %get-tuple-element.22), channel_id=1, source_target_pairs={{0,1},{1,0},{2,3},{3,2},{4,5},{5,4},{6,7},{7,6},{8,9},{9,8},{10,11... | collective-permute-start | bytes 1572872 | tf_op jit(solution)/shard_map/ppermute | solution.py:365
  8.5 27.3 %collective-permute-start.1 = (bf16[512,512]{1,0:T(8,128)(2,1)S(1)}, bf16[512,512]{1,0:T(8,128)(2,1)S(1)}, u32[]{:S(2)}, u32[]{:S(2)}) collective-permute-start(bf16[512,512]{1,0:T(8,128)(2,1)S(1)} %get-tuple-element.23), channel_id=1, source_target_pairs={{0,63},{1,2},{2,1},{3,4},{4,3},{5,6},{6,5},{7,8},{8,7},{9,10},{10,... | collective-permute-start | bytes 1572872 | tf_op jit(solution)/shard_map/ppermute | solution.py:364
  16.1 17.7 %copy-start.1 = (bf16[1,80,128,128]{3,2,1,0:T(8,128)(2,1)S(1)}, bf16[1,80,128,128]{3,2,1,0:T(8,128)(2,1)}, u32[]{:S(2)}) copy-start(bf16[1,80,128,128]{3,2,1,0:T(8,128)(2,1)} %param.19) | copy-start | bytes 7864324
  17.2 18.6 %copy-start = (f32[1,4,16,16,512]{4,3,2,1,0:T(8,128)S(1)}, f32[1,4,16,16,512]{4,3,2,1,0:T(8,128)}, u32[]{:S(2)}) copy-start(f32[1,4,16,16,512]{4,3,2,1,0:T(8,128)} %param.11) | copy-start | bytes 6291460
  17.2 18.6 %copy-start.2 = (f32[1,4,16,512]{3,2,1,0:T(8,128)S(1)}, f32[1,4,16,512]{3,2,1,0:T(8,128)}, u32[]{:S(2)}) copy-start(f32[1,4,16,512]{3,2,1,0:T(8,128)} %forcing_ref.1) | copy-start | bytes 393220
  17.2 18.6 %copy-start.3 = (s32[1,16,512]{2,1,0:T(8,128)S(1)}, s32[1,16,512]{2,1,0:T(8,128)}, u32[]{:S(2)}) copy-start(s32[1,16,512]{2,1,0:T(8,128)} %mask_ref.1) | copy-start | bytes 98308
  17.3 9.6 %collective-permute-start.6 = (bf16[256,128]{1,0:T(8,128)(2,1)S(1)}, bf16[256,128]{1,0:T(8,128)(2,1)S(1)}, u32[]{:S(2)}, u32[]{:S(2)}) collective-permute-start(bf16[256,128]{1,0:T(8,128)(2,1)S(1)} %shard_map.125), channel_id=1, source_target_pairs={{0,127},{1,66},{2,65},{3,68},{4,67},{5,70},{6,69},{7,72},{8,71},{9... | collective-permute-start | bytes 196616 | tf_op jit(solution)/shard_map/ppermute | solution.py:369
  17.3 13.1 %collective-permute-start.5 = (bf16[256,128]{1,0:T(8,128)(2,1)S(1)}, bf16[256,128]{1,0:T(8,128)(2,1)S(1)}, u32[]{:S(2)}, u32[]{:S(2)}) collective-permute-start(bf16[256,128]{1,0:T(8,128)(2,1)S(1)} %shard_map.125), channel_id=1, source_target_pairs={{0,65},{1,64},{2,67},{3,66},{4,69},{5,68},{6,71},{7,70},{8,73},{9,... | collective-permute-start | bytes 196616 | tf_op jit(solution)/shard_map/ppermute | solution.py:370
  17.4 16.3 %collective-permute-start.4 = (bf16[256,128]{1,0:T(8,128)(2,1)S(1)}, bf16[256,128]{1,0:T(8,128)(2,1)S(1)}, u32[]{:S(2)}, u32[]{:S(2)}) collective-permute-start(bf16[256,128]{1,0:T(8,128)(2,1)S(1)} %shard_map.125), channel_id=1, source_target_pairs={{0,64},{1,65},{2,66},{3,67},{4,68},{5,69},{6,70},{7,71},{8,72},{9,... | collective-permute-start | bytes 196616 | tf_op jit(solution)/shard_map/ppermute | solution.py:371

commit v3 on v2

v3 whole, which is shorter than its diff:
```python
import functools

import jax
import jax.numpy as jnp
import numpy as np
from jax import lax
from jax.experimental import pallas as pl
from jax.experimental.pallas import tpu as pltpu
from jax.sharding import PartitionSpec as P

F32 = jnp.float32
BF16 = jnp.bfloat16
VMEM_LIMIT = 40 * 1024 * 1024


def dot(a, b):
    return jnp.dot(a, b, preferred_element_type=F32)


def iota(shape, dim):
    return lax.broadcasted_iota(jnp.int32, shape, dim)


def ends():
    here = jnp.where(lax.rem(lax.axis_index("tile"), 2) == 0, 12, 0)
    return here, 12 - here


def group_node(group, place):
    here, away = ends()
    side = jnp.where(group == 2, 4 * place + 3, 4 * place)
    return jnp.where(group == 0, here + place, jnp.where(group == 1, away + place, side))


def spread_matrix():
    col = iota((256, 256), 1)
    wanted = (col % 16) * 16 + group_node(col // 64, 3 - col // 16 % 4)
    return (iota((256, 256), 0) == wanted).astype(BF16)


def coupling_matrices(node_ref, level_ref):
    rows, cols = iota((16, 256), 0), iota((16, 256), 1)
    inner, outer = (cols % 16 == rows).astype(BF16), (cols // 16 == rows).astype(BF16)
    r, c = iota((256, 256), 0), iota((256, 256), 1)
    node = jnp.concatenate([dot(node_ref[0].astype(BF16), inner)] * 16, axis=0)
    node = jnp.where(r // 16 == c // 16, node, 0.0).astype(BF16)
    level = dot(level_ref[0].astype(BF16), outer)
    level = jnp.concatenate([jnp.broadcast_to(level[l : l + 1], (16, 256)) for l in range(16)], axis=0)
    level = jnp.where(r % 16 == c % 16, level, 0.0).astype(BF16)
    return node, level


def diagonal(metric, penalty):
    node = iota((16, metric.shape[1]), 0)
    i, j = node // 4, node % 4
    edges = ((i == 0) | (i == 3)).astype(F32) + ((j == 0) | (j == 3)).astype(F32)
    return 0.8 - 0.3 * metric - penalty * edges


def exchange_rate(coeffs_ref, mask):
    mask = mask.astype(F32)
    return coeffs_ref[0, 1] * mask + coeffs_ref[0, 2] * (1.0 - mask)


def levels_of(pattern):
    return jnp.concatenate([pattern] * 16, axis=0)


def halves(value):
    high = value.astype(BF16)
    return high, (value - high.astype(F32)).astype(BF16)


def low_select():
    row = iota((64, 64), 0)
    wanted = (row % 16 // 4) * 16 + group_node(row // 16, row % 4)
    return (iota((64, 64), 1) == wanted).astype(BF16)


def low_spread(first, second):
    col = iota((64, 64), 1)
    wanted = (col % 16 // 4) * 16 + group_node(jnp.where(col < 32, first, second), 3 - col % 4)
    return (iota((64, 64), 0) == wanted).astype(BF16)


def low_node_matrix(node):
    row, col = iota((64, 64), 0), iota((64, 64), 1)
    rows_of = (iota((64, 16), 0) % 16 == iota((64, 16), 1)).astype(BF16)
    cols_of = (iota((16, 64), 1) % 16 == iota((16, 64), 0)).astype(BF16)
    parts = [dot(dot(rows_of, part).astype(BF16), cols_of) for part in halves(node)]
    high, low = [jnp.where(row // 16 == col // 16, part, 0.0).astype(BF16) for part in parts]
    return jnp.concatenate([high, high, low], axis=1)


def low_node_product(matrix, value):
    high, low = halves(value)
    return dot(matrix, jnp.concatenate([high, low, high], axis=0))


LANES = [slice(128 * c, 128 * (c + 1)) for c in range(4)]
SIDE_NODES = ((3, 7, 11, 15), (0, 4, 8, 12))


def whole_rows(ref, start, count):
    return jnp.concatenate([ref[c, start : start + count, :] for c in range(4)], axis=1)


def mix_to_lowest(level, ref):
    parts = []
    for v in range(4):
        total = level[0, 0, 0] * whole_rows(ref, 256 * v, 16)
        for m in range(1, 16):
            total = total + level[0, 0, m] * whole_rows(ref, 256 * v + 16 * m, 16)
        parts.append(total)
    return jnp.concatenate(parts, axis=0)


def pack_node(ref, v, c, node, scale):
    return (scale * ref[c, pl.ds(256 * v + node, 16, stride=16), :]).astype(BF16)


def pack_facing(ref, scale, here_ref, away_ref, start):
    for target, first in zip((here_ref, away_ref), ends()):
        for v in range(4):
            for place in range(4):
                at = start + 64 * v + 16 * place
                for c in range(4):
                    target[at : at + 16, LANES[c]] = pack_node(ref, v, c, first + place, scale)


def pack_sides(ref, scale, edges):
    for side in range(2):
        for v in range(4):
            for place in range(4):
                at = 64 * v + 16 * place
                for c in range(4):
                    lanes = slice(512 * side + 128 * c, 512 * side + 128 * (c + 1))
                    edges[at : at + 16, lanes] = pack_node(ref, v, c, SIDE_NODES[side][place], scale)


def local_kernel(
    state_hbm, metric_hbm, node_hbm, level_hbm, coeffs_hbm, partner_hbm, mask_hbm, forcing_hbm,
    state_ref, part_ref, here_ref, away_ref, here_low_ref, away_low_ref, inner_ref,
    weights_ref, low_ref, base_ref, factor_ref, low_node_ref,
    metric_ref, node_ref, level_ref, coeffs_ref, partner_ref, mask_ref, forcing_ref, level_smem, edges, sems,
):
    pairs = [
        (partner_hbm, partner_ref), (node_hbm, node_ref), (level_hbm, level_ref), (coeffs_hbm, coeffs_ref),
        (metric_hbm, metric_ref),
    ]
    pairs += [(state_hbm.at[:, LANES[c]], state_ref.at[c]) for c in range(4)]
    pairs += [(mask_hbm, mask_ref), (forcing_hbm, forcing_ref), (level_hbm, level_smem)]
    copies = [pltpu.make_async_copy(source, target, sems.at[i]) for i, (source, target) in enumerate(pairs)]
    for copy in copies:
        copy.start()
    select_low, spread_inner = low_select(), low_spread(2, 3)
    weights_ref[:, 512:768] = spread_matrix()
    for copy in copies[:5]:
        copy.wait()
    for step in range(4):
        columns = partner_ref[0:1, 512 + 256 * step : 768 + 256 * step] - 1024
        hit = iota((1024, 256), 0) == columns
        inner_ref[:, 256 * step : 256 * (step + 1)] = jnp.where(hit, 1.0, 0.0).astype(BF16)
    penalty = coeffs_ref[0, 0]
    metric = metric_ref[...]
    node, level = coupling_matrices(node_ref, level_ref)
    weights_ref[:, 0:256] = node
    weights_ref[:, 256:512] = level
    low_node = low_node_matrix(node_ref[0])
    low_node_ref[...] = low_node
    factor = diagonal(metric, penalty)
    for copy in copies[5:]:
        copy.wait()
    pack_sides(state_ref, penalty, edges)
    lowest = jnp.concatenate([whole_rows(state_ref, 256 * v, 16) for v in range(4)], axis=0)
    high, low = [dot(select_low, part).astype(BF16) for part in halves(penalty * lowest)]
    here_low_ref[0:16, :] = high[0:16]
    here_low_ref[16:32, :] = low[0:16]
    away_low_ref[0:16, :] = high[16:32]
    away_low_ref[16:32, :] = low[16:32]
    edges[256:272, 0:512] = high[32:48]
    edges[256:272, 512:1024] = high[48:64]
    edges[272:288, 0:512] = low[32:48]
    edges[272:288, 512:1024] = low[48:64]
    moved = dot(edges[...], inner_ref[...]).astype(BF16)
    pack_facing(state_ref, penalty, here_ref, away_ref, 0)
    rate = exchange_rate(coeffs_ref, mask_ref[0])
    rates = jnp.concatenate([rate] * 4, axis=0)
    forced = rates * jnp.concatenate([forcing_ref[0, v] for v in range(4)], axis=0)
    factor_low = factor - rate
    factor_ref[...] = factor_low
    mixed = mix_to_lowest(level_smem, state_ref)
    near = moved[256:288]
    p_low = jnp.concatenate([factor_low] * 4, axis=0) * lowest + forced + mixed
    p_low = p_low + low_node_product(low_node, lowest * metric)
    p_low = p_low + dot(spread_inner, jnp.concatenate([near[:, 0:512], near[:, 512:1024]], axis=0))
    low_ref[...] = p_low
    high, low = [dot(select_low[0:32], part).astype(BF16) for part in halves(penalty * (p_low + mixed))]
    here_low_ref[32:48, :] = high[0:16]
    here_low_ref[48:64, :] = low[0:16]
    away_low_ref[32:48, :] = high[16:32]
    away_low_ref[48:64, :] = low[16:32]
    factors = levels_of(factor)
    for v in range(4):
        u = whole_rows(state_ref, 256 * v, 256)
        operand = [(u * metric).astype(BF16), u.astype(BF16)]
        operand += [moved[64 * v : 64 * (v + 1), 512 * side : 512 * (side + 1)] for side in range(2)]
        p = dot(jnp.concatenate([weights_ref[:, 0:512], weights_ref[:, 640:768]], axis=1), jnp.concatenate(operand, axis=0))
        p = jnp.concatenate([p_low[16 * v : 16 * (v + 1)], (factors * u + p)[16:256]], axis=0)
        for c in range(4):
            part_ref[c, 256 * v : 256 * (v + 1), :] = p[:, LANES[c]]
    pack_facing(part_ref, penalty, here_ref, away_ref, 256)
    mixed = mix_to_lowest(level_smem, part_ref)
    node_at = iota((64, 1), 0) % 16
    facing = jnp.where((node_at // 4 == 0) | (node_at // 4 == 3), penalty * penalty, 0.0)
    base_ref[...] = mixed + forced + facing * lowest


def lowest_kernel(
    low_ref, base_ref, factor_ref, low_node_ref, metric_ref, coeffs_ref, here_ref, away_ref, here_map, away_map, inner_ref,
    surface_ref,
):
    penalty = coeffs_ref[:, 0:1]
    here = dot(here_ref[...], here_map[...]).astype(BF16)
    away = dot(away_ref[...], away_map[...]).astype(BF16)
    outer, inner, select = low_spread(0, 1), low_spread(2, 3), low_select()
    u1 = low_ref[...] + dot(outer, jnp.concatenate([here[0:32], away[0:32]], axis=0))
    high, low = [dot(select[32:64], part).astype(BF16) for part in halves(penalty * u1)]
    sides = [jnp.concatenate([high[at : at + 16], low[at : at + 16]], axis=0) for at in (0, 16)]
    near = dot(jnp.concatenate(sides, axis=1), inner_ref[...]).astype(BF16)
    x = base_ref[...] + jnp.concatenate([factor_ref[...]] * 4, axis=0) * u1
    x = x + low_node_product(low_node_ref[...], u1 * metric_ref[...])
    x = x + dot(outer, jnp.concatenate([here[32:64], away[32:64]], axis=0))
    x = x + dot(inner, jnp.concatenate([near[:, 0:512], near[:, 512:1024]], axis=0))
    x = x.astype(BF16)
    for v in range(4):
        for q in range(4):
            surface_ref[64 * v + 16 * q : 64 * v + 16 * (q + 1), :] = x[16 * v : 16 * (v + 1), 128 * q : 128 * (q + 1)]


def tables_kernel(
    partner_ref, rows_ref, cols_ref, here_in, away_in,
    here_map, away_map, pick_ref, sum_ref, here_out, away_out,
):
    last = ends()[0] == 12
    before, after = partner_ref[0:1, 0:512], partner_ref[0:1, 1536:2048] - 2560
    here_map[...] = jnp.where(iota((512, 512), 0) == jnp.where(last, after, before), 1.0, 0.0).astype(BF16)
    away_map[...] = jnp.where(iota((512, 512), 0) == jnp.where(last, before, after), 1.0, 0.0).astype(BF16)
    odd = lax.rem(lax.axis_index("tile"), 2)
    slots = rows_ref.shape[1]
    wide = 4 * slots
    repeat = (iota((slots, wide), 1) // 4 == iota((slots, wide), 0)).astype(BF16)
    widen = lambda ref: dot(jnp.broadcast_to(ref[0:1, :].astype(BF16), (16, slots)), repeat)[0:1].astype(jnp.int32)
    rows, cols = widen(rows_ref), widen(cols_ref)
    tile, block = cols // 64, cols % 64
    tile = jnp.where(odd == 1, 2 - tile, tile)
    var = iota((1, wide), 1) % 4
    wanted = tile * 256 + var * 64 + (block % 4) * 16 + block // 4
    pick_ref[...] = jnp.transpose((iota((768, wide), 0) == wanted).astype(F32)).astype(BF16)
    wanted = jnp.where(rows == 64, -1, var * 64 + (rows % 4) * 16 + rows // 4)
    sum_ref[...] = (iota((256, wide), 0) == wanted).astype(BF16)


def finish_kernel(
    state_ref, part_ref, here_ref, away_ref, here_map, away_map, inner_ref, weights_ref,
    metric_ref, coeffs_ref, mask_ref, forcing_ref,
    next_hbm, middle_ref, next_ref, edges, sems,
):
    penalty = coeffs_ref[:, 0:1]
    metric = metric_ref[...]
    here = dot(here_ref[...], here_map[...]).astype(BF16)
    away = dot(away_ref[...], away_map[...]).astype(BF16)
    for v in range(4):
        rows = slice(64 * v, 64 * (v + 1))
        halo = dot(weights_ref[:, 512:640], jnp.concatenate([here[rows], away[rows]], axis=0))
        for c in range(4):
            middle_ref[c, 256 * v : 256 * (v + 1), :] = part_ref[c, 256 * v : 256 * (v + 1), :] + halo[:, LANES[c]]
    pack_sides(middle_ref, penalty, edges)
    moved = dot(edges[...], inner_ref[...]).astype(BF16)
    factors = levels_of(diagonal(metric, penalty))
    node = iota((256, 1), 0) % 16
    facing = jnp.where((node // 4 == 0) | (node // 4 == 3), penalty * penalty, 0.0)
    mask = mask_ref[0].astype(F32)
    rate = coeffs_ref[:, 1:2] * mask + coeffs_ref[:, 2:3] * (1.0 - mask)
    copies = []
    for v in range(4):
        u1 = whole_rows(middle_ref, 256 * v, 256)
        rows = slice(64 * v, 64 * (v + 1))
        far = slice(256 + 64 * v, 256 + 64 * (v + 1))
        operand = [(u1 * metric).astype(BF16), u1.astype(BF16), here[far], away[far]]
        operand += [moved[rows, 512 * side : 512 * (side + 1)] for side in range(2)]
        x = factors * u1 + facing * whole_rows(state_ref, 256 * v, 256)
        x = x + dot(weights_ref[...], jnp.concatenate(operand, axis=0))
        added = rate * (forcing_ref[0, v] - u1[0:16])
        next_ref[256 * v : 256 * (v + 1), :] = jnp.concatenate([x[0:16] + added, x[16:256]], axis=0)
        rows = pl.ds(256 * v, 256)
        copies.append(pltpu.make_async_copy(next_ref.at[rows], next_hbm.at[rows], sems.at[v]))
        copies[-1].start()
    for copy in copies:
        copy.wait()


def remap_kernel(own_ref, near_ref, far_ref, pick_ref, sum_ref, blocks_ref, out_ref, products):
    picked = dot(pick_ref[:, 0:256], far_ref[...])
    picked = picked + dot(pick_ref[:, 256:512], own_ref[...])
    picked = picked + dot(pick_ref[:, 512:768], near_ref[...])
    slots = blocks_ref.shape[0]
    upper = iota((8, 1), 0) < 4
    for pair in range(slots // 2):
        part = picked[8 * pair : 8 * (pair + 1)]
        left = jnp.concatenate([jnp.where(upper, part, 0.0), jnp.where(upper, 0.0, part)], axis=1).astype(BF16)
        right = jnp.concatenate([blocks_ref[2 * pair], blocks_ref[2 * pair + 1]], axis=1)
        products[8 * pair : 8 * (pair + 1), :] = lax.dot_general(
            left, right, (((1,), (1,)), ((), ())), preferred_element_type=F32
        )
    value = products[...]
    high = value.astype(BF16)
    low = (value - high.astype(F32)).astype(BF16)
    total = dot(sum_ref[...], high) + dot(sum_ref[...], low)
    for v in range(4):
        for q in range(4):
            out_ref[0, v, :, 128 * q : 128 * (q + 1)] = total[64 * v + 16 * q : 64 * v + 16 * (q + 1)]


def call(kernel, outs, scratch=(), inputs="", results="", aliases={}, cost=0):
    spaces = {"v": pltpu.VMEM, "s": pltpu.SMEM, "h": pltpu.HBM, "a": pl.ANY}
    place = lambda kind: pl.BlockSpec(memory_space=spaces[kind])
    results = results or "v" * len(outs)
    return pl.pallas_call(
        kernel,
        out_shape=[jax.ShapeDtypeStruct(shape, kind) for shape, kind in outs],
        in_specs=[place(kind) for kind in inputs],
        out_specs=[place(kind) for kind in results],
        input_output_aliases=aliases,
        scratch_shapes=list(scratch),
        cost_estimate=pl.CostEstimate(flops=cost, bytes_accessed=0, transcendentals=0) if cost else None,
        compiler_params=pltpu.CompilerParams(vmem_limit_bytes=VMEM_LIMIT),
    )


def shards(
    state, metric, element_coupling, level_coupling, coeffs, edge_partner, sea_mask, forcing,
    remap_weights, remap_rows, remap_cols,
):
    tiles = lax.axis_size("tile")
    here = [(t, t ^ 1) for t in range(tiles)]
    away = [(t, (t + 1) % tiles if t % 2 else (t - 1) % tiles) for t in range(tiles)]
    crossed = lambda pairs: [(c * tiles + a, (1 - c) * tiles + b) for c in range(2) for a, b in pairs]
    straight = [(t, t) for t in range(tiles)]
    flat = state.reshape(1024, 512)
    inputs = (flat, metric, element_coupling, level_coupling, coeffs, edge_partner, sea_mask, forcing)
    (chunks, part, here_edge, away_edge, here_low, away_low, inner, weights, low, base, factor, low_node) = call(
        local_kernel,
        [
            ((4, 1024, 128), F32), ((4, 1024, 128), F32), ((512, 512), BF16), ((512, 512), BF16), ((64, 512), BF16),
            ((64, 512), BF16), ((1024, 1024), BF16), ((256, 768), BF16),
            ((64, 512), F32), ((64, 512), F32), ((16, 512), F32), ((64, 192), BF16),
        ],
        [(pltpu.SMEM if value is coeffs else pltpu.VMEM)(value.shape, value.dtype) for value in inputs[1:]]
        + [pltpu.SMEM((1, 16, 16), F32), pltpu.VMEM((288, 1024), BF16), pltpu.SemaphoreType.DMA((12,))],
        "hhhhhhhh",
    )(*[pltpu.with_memory_space_constraint(value, pltpu.HBM) for value in inputs])
    away_low = lax.ppermute(away_low, "tile", away)
    here_low = lax.ppermute(here_low, "tile", here)
    slots = remap_rows.shape[1]
    here_map, away_map, pick, total, here_edge, away_edge = call(
        tables_kernel,
        [
            ((512, 512), BF16), ((512, 512), BF16), ((4 * slots, 768), BF16), ((256, 4 * slots), BF16),
            (here_edge.shape, BF16), (away_edge.shape, BF16),
        ],
        inputs="vvvaa", results="vvvvaa", aliases={3: 4, 4: 5}, cost=4_000_000_000,
    )(edge_partner, remap_rows, remap_cols, here_edge, away_edge)
    away_edge = lax.ppermute(away_edge, "tile", away)
    here_edge = lax.ppermute(here_edge, "tile", here)
    (surface,) = call(lowest_kernel, [((256, 128), BF16)], inputs="v" * 11, cost=40_000_000_000)(
        low, base, factor, low_node, metric, coeffs, here_low, away_low, here_map, away_map, inner
    )
    far = lax.ppermute(surface, ("comp", "tile"), crossed(away))
    near = lax.ppermute(surface, ("comp", "tile"), crossed(here))
    own = lax.ppermute(surface, ("comp", "tile"), crossed(straight))
    (nxt,) = call(
        finish_kernel,
        [((1024, 512), F32)],
        [
            pltpu.VMEM((4, 1024, 128), F32), pltpu.VMEM((1024, 512), F32), pltpu.VMEM((256, 1024), BF16),
            pltpu.SemaphoreType.DMA((4,)),
        ],
        "v" * 12, "h",
    )(chunks, part, here_edge, away_edge, here_map, away_map, inner, weights, metric, coeffs, sea_mask, forcing)
    (new_forcing,) = call(
        remap_kernel, [(forcing.shape, F32)], [pltpu.VMEM((4 * slots, 128), F32)], "v" * 6,
    )(own, near, far, pick, total, remap_weights[0])
    return nxt.reshape(state.shape), new_forcing


def solution(mesh):
    placed = (
        P("comp", None, None, None, "tile"),
        P("comp", "tile"),
        P("comp", None, None),
        P("comp", None, None),
        P("comp", None),
        P("comp", "tile"),
        P("comp", None, "tile"),
        P("comp", None, None, "tile"),
        P("comp", "tile", None, None),
        P("comp", "tile"),
        P("comp", "tile"),
    )
    return jax.shard_map(
        shards,
        mesh=mesh,
        in_specs=placed,
        out_specs=(P("comp", None, None, None, "tile"), P("comp", None, None, "tile")),
        check_vma=False,
    )
```

time: 41.1 us -> 38.9 us (0.946)
  Pallas kernels: 15.2 us -> 12.9 us
    pallas_call x3, Pallas kernels: 11.9 us -> 9.67 us  [the longest x1 5.39 us: shards(): call(local_kernel, [((4, 1024, 128), F32), ((4, 1024, 128), F32), ((512,...]
  transfers between devices with their start and end apart: 7 -> 7, of which waited for: 3 -> 3; matrix products, arithmetic and copies ran while one was open for 0% -> 0% of each run, Pallas kernels for 9% -> 10%
where the time goes in v3:
time: 38.9 us; the launch traced here: 38.8 us
  waiting for transfers between devices  14.6 us (38%)
  Pallas kernels  12.9 us (33%)
  starting transfers between devices  10.4 us (27%)
  between operations  0.79 us (2%)
    ppermute x1, waiting for transfers between devices, shards(): far = lax.ppermute(surface, ('comp', 'tile'), crossed(away))  7.7 us
    ppermute x1, starting transfers between devices, shards(): away_edge = lax.ppermute(away_edge, 'tile', away)  7.53 us
    pallas_call x1, Pallas kernels, shards(): call(local_kernel, [((4, 1024, 128), F32), ((4, 1024, 128), F32), ((512,...  5.39 us
    pallas_call x1, Pallas kernels, shards(): call(finish_kernel, [((1024, 512), F32)], [pltpu.VMEM((4, 1024, 128), F32...  3.71 us
    ppermute x1, waiting for transfers between devices, shards(): near = lax.ppermute(surface, ('comp', 'tile'), crossed(here))  3.65 us
    ppermute x1, waiting for transfers between devices, shards(): own = lax.ppermute(surface, ('comp', 'tile'), crossed(straight))  3.29 us
    pallas_call x1, Pallas kernels, shards(): call(remap_kernel, [(forcing.shape, F32)], [pltpu.VMEM((4 * slots, 128),...  2.09 us
    ppermute x1, starting transfers between devices, shards(): own = lax.ppermute(surface, ('comp', 'tile'), crossed(straight))  1.71 us
  transfers between devices with their start and end apart: 7, of which 3 were waited for; matrix products, arithmetic and copies ran while one was open for 0% of the time, Pallas kernels for 10%

profile of v3, /device:TPU:64, one launch (start us, length us, event | category | flops | bytes accessed | tf_op | source)
XLA Modules:
  0.0 38.8 jit_solution(9284056981343933148)
XLA Ops:
  0.7 5.4 %shard_map.122 = (f32[4,1024,128]{2,1,0:T(8,128)S(1)}, f32[4,1024,128]{2,1,0:T(8,128)S(1)}, bf16[512,512]{1,0:T(8,128)(2,1)S(1)}, bf16[512,512]{1,0:T(8,128)(2,1...) custom-call(f32[1024,512]{1,0:T(8,128)} %bitcast.4, ...), custom_call_target="tpu_custom_call" | custom-call | tf_op jit(solution)/shard_map/pallas_call | solution.py:352
  6.1 0.1 collective-permute-start.2
  6.2 0.1 collective-permute-start.3
  6.2 0.0 copy-done.3
  6.3 0.0 copy-start.4
  6.3 0.0 copy-start.5
  6.3 0.6 %shard_map.123 = (bf16[512,512]{1,0:T(8,128)(2,1)S(1)}, bf16[512,512]{1,0:T(8,128)(2,1)S(1)}, bf16[320,768]{1,0:T(8,128)(2,1)S(1)}, bf16[256,320]{1,0:T(8,128)(2...) custom-call(s32[1,2048]{1,0:T(1,128)S(1)} %copy-done.3, ...), custom_call_target="tpu_custom_call", output_to_operand_aliasing={{4}: (3, {}), {5}: (4, {})} | custom-call | flops 4000000000 | tf_op jit(solution)/shard_map/pallas_call | solution.py:366
  6.9 0.8 %collective-permute-start = (bf16[512,512]{1,0:T(8,128)(2,1)S(1)}, bf16[512,512]{1,0:T(8,128)(2,1)S(1)}, u32[]{:S(2)}, u32[]{:S(2)}) collective-permute-start(bf16[512,512]{1,0:T(8,128)(2,1)S(1)} %get-tuple-element.24), channel_id=1, source_target_pairs={{0,1},{1,0},{2,3},{3,2},{4,5},{5,4},{6,7},{7,6},{8,9},{9,8},{10,11... | collective-permute-start | bytes 1572872 | tf_op jit(solution)/shard_map/ppermute | solution.py:375
  7.7 7.5 %collective-permute-start.1 = (bf16[512,512]{1,0:T(8,128)(2,1)S(1)}, bf16[512,512]{1,0:T(8,128)(2,1)S(1)}, u32[]{:S(2)}, u32[]{:S(2)}) collective-permute-start(bf16[512,512]{1,0:T(8,128)(2,1)S(1)} %get-tuple-element.25), channel_id=1, source_target_pairs={{0,63},{1,2},{2,1},{3,4},{4,3},{5,6},{6,5},{7,8},{8,7},{9,10},{10,... | collective-permute-start | bytes 1572872 | tf_op jit(solution)/shard_map/ppermute | solution.py:374
  15.2 0.0 collective-permute-done.2.here_ref
  15.2 0.0 collective-permute-done.3.away_ref
  15.3 0.0 copy-start
  15.3 1.1 %shard_map.125 = bf16[256,128]{1,0:T(8,128)(2,1)S(1)} custom-call(f32[64,512]{1,0:T(8,128)S(1)} %get-tuple-element.30.low_ref, f32[64,512]{1,0:T(8,128)S(1)} %get-tuple-element.31.base_ref, f32[16,512]{1,0:T(8,128)S(1)} %get-tuple-element.32.factor_ref, bf16[64,192]{1,0:T(8,128)(2,1)S(1)} %get-tuple-element.33.low_node_ref, f32[1,512]{1,0:T(1,128)S(1)} %copy-done.4, ...), custom_call_target="tpu_custom_call" | custom-call | flops 40000000000 | tf_op jit(solution)/shard_map/pallas_call | solution.py:376
  16.4 0.0 copy-start.2
  16.4 0.1 collective-permute-start.6
  16.5 0.1 collective-permute-start.5
  16.6 1.7 %collective-permute-start.4 = (bf16[256,128]{1,0:T(8,128)(2,1)S(1)}, bf16[256,128]{1,0:T(8,128)(2,1)S(1)}, u32[]{:S(2)}, u32[]{:S(2)}) collective-permute-start(bf16[256,128]{1,0:T(8,128)(2,1)S(1)} %shard_map.125), channel_id=1, source_target_pairs={{0,64},{1,65},{2,66},{3,67},{4,68},{5,69},{6,70},{7,71},{8,72},{9,... | collective-permute-start | bytes 196616 | tf_op jit(solution)/shard_map/ppermute | solution.py:381
  18.3 7.7 %collective-permute-done.6.far_ref = bf16[256,128]{1,0:T(8,128)(2,1)S(1)} collective-permute-done((bf16[256,128]{1,0:T(8,128)(2,1)S(1)}, bf16[256,128]{1,0:T(8,128)(2,1)S(1)}, u32[]{:S(2)}, u32[]{:S(2)}) %collective-permute-start.6) | collective-permute-done | bytes 65568 | tf_op jit(solution)/shard_map/ppermute | solution.py:379
  26.0 3.6 %collective-permute-done.5.near_ref = bf16[256,128]{1,0:T(8,128)(2,1)S(1)} collective-permute-done((bf16[256,128]{1,0:T(8,128)(2,1)S(1)}, bf16[256,128]{1,0:T(8,128)(2,1)S(1)}, u32[]{:S(2)}, u32[]{:S(2)}) %collective-permute-start.5) | collective-permute-done | bytes 65568 | tf_op jit(solution)/shard_map/ppermute | solution.py:380
  29.7 3.3 %collective-permute-done.4.own_ref = bf16[256,128]{1,0:T(8,128)(2,1)S(1)} collective-permute-done((bf16[256,128]{1,0:T(8,128)(2,1)S(1)}, bf16[256,128]{1,0:T(8,128)(2,1)S(1)}, u32[]{:S(2)}, u32[]{:S(2)}) %collective-permute-start.4) | collective-permute-done | bytes 65568 | tf_op jit(solution)/shard_map/ppermute | solution.py:381
  33.0 2.1 %shard_map.126 = f32[1,4,16,512]{3,2,1,0:T(8,128)} custom-call(bf16[256,128]{1,0:T(8,128)(2,1)S(1)} %collective-permute-done.4.own_ref, bf16[256,128]{1,0:T(8,128)(2,1)S(1)} %collective-permute-done.5.near_ref, bf16[256,128]{1,0:T(8,128)(2,1)S(1)} %collective-permute-done.6.far_ref, bf16[320,768]{1,0:T(8,128)(2,1)S(1)} %get-tuple-element.36.pick_ref, ...), custom_call_target="tpu_custom_call" | custom-call | tf_op jit(solution)/shard_map/pallas_call | solution.py:391
  35.0 0.0 collective-permute-done.here_ref
  35.0 0.0 collective-permute-done.1.away_ref
  35.1 3.7 %shard_map.124 = f32[1024,512]{1,0:T(8,128)} custom-call(f32[4,1024,128]{2,1,0:T(8,128)S(1)} %get-tuple-element.20.state_ref, f32[4,1024,128]{2,1,0:T(8,128)S(1)} %get-tuple-element.21.part_ref, bf16[512,512]{1,0:T(8,128)(2,1)S(1)} %collective-permute-done.here_ref, bf16[512,512]{1,0:T(8,128)(2,1)S(1)} %collective-permute-done.1.away_ref, ...), custom_call_target="tpu_custom_call" | custom-call | tf_op jit(solution)/shard_map/pallas_call | solution.py:382
  (11 shorter events, 0.0 us)
Async XLA Ops:
  0.6 5.6 %copy-start.3 = (s32[1,2048]{1,0:T(1,128)S(1)}, s32[1,2048]{1,0:T(1,128)}, u32[]{:S(2)}) copy-start(s32[1,2048]{1,0:T(1,128)} %partner_ref.1) | copy-start | bytes 24580
  0.6 5.6 %copy-start.7 = (s32[1,80]{1,0:T(1,128)S(1)}, s32[1,80]{1,0:T(1,128)}, u32[]{:S(2)}) copy-start(s32[1,80]{1,0:T(1,128)} %cols_ref.1) | copy-start | bytes 964
  0.7 5.6 %copy-start.6 = (s32[1,80]{1,0:T(1,128)S(1)}, s32[1,80]{1,0:T(1,128)}, u32[]{:S(2)}) copy-start(s32[1,80]{1,0:T(1,128)} %rows_ref.1) | copy-start | bytes 964
  6.1 9.2 %collective-permute-start.2 = (bf16[64,512]{1,0:T(8,128)(2,1)S(1)}, bf16[64,512]{1,0:T(8,128)(2,1)S(1)}, u32[]{:S(2)}, u32[]{:S(2)}) collective-permute-start(bf16[64,512]{1,0:T(8,128)(2,1)S(1)} %get-tuple-element.34), channel_id=1, source_target_pairs={{0,1},{1,0},{2,3},{3,2},{4,5},{5,4},{6,7},{7,6},{8,9},{9,8},{10,11... | collective-permute-start | bytes 196616 | tf_op jit(solution)/shard_map/ppermute | solution.py:364
  6.2 9.1 %collective-permute-start.3 = (bf16[64,512]{1,0:T(8,128)(2,1)S(1)}, bf16[64,512]{1,0:T(8,128)(2,1)S(1)}, u32[]{:S(2)}, u32[]{:S(2)}) collective-permute-start(bf16[64,512]{1,0:T(8,128)(2,1)S(1)} %get-tuple-element.35), channel_id=1, source_target_pairs={{0,63},{1,2},{2,1},{3,4},{4,3},{5,6},{6,5},{7,8},{8,7},{9,10},{10,... | collective-permute-start | bytes 196616 | tf_op jit(solution)/shard_map/ppermute | solution.py:363
  6.3 9.0 %copy-start.4 = (f32[1,512]{1,0:T(1,128)S(1)}, f32[1,512]{1,0:T(1,128)}, u32[]{:S(2)}) copy-start(f32[1,512]{1,0:T(1,128)} %metric_ref.3) | copy-start | bytes 6148
  6.3 9.0 %copy-start.5 = (f32[1,3]{1,0:T(1,128)S(1)}, f32[1,3]{1,0:T(1,128)}, u32[]{:S(2)}) copy-start(f32[1,3]{1,0:T(1,128)} %coeffs_ref.3) | copy-start | bytes 40
  6.9 28.2 %collective-permute-start = (bf16[512,512]{1,0:T(8,128)(2,1)S(1)}, bf16[512,512]{1,0:T(8,128)(2,1)S(1)}, u32[]{:S(2)}, u32[]{:S(2)}) collective-permute-start(bf16[512,512]{1,0:T(8,128)(2,1)S(1)} %get-tuple-element.24), channel_id=1, source_target_pairs={{0,1},{1,0},{2,3},{3,2},{4,5},{5,4},{6,7},{7,6},{8,9},{9,8},{10,11... | collective-permute-start | bytes 1572872 | tf_op jit(solution)/shard_map/ppermute | solution.py:375
  7.7 27.3 %collective-permute-start.1 = (bf16[512,512]{1,0:T(8,128)(2,1)S(1)}, bf16[512,512]{1,0:T(8,128)(2,1)S(1)}, u32[]{:S(2)}, u32[]{:S(2)}) collective-permute-start(bf16[512,512]{1,0:T(8,128)(2,1)S(1)} %get-tuple-element.25), channel_id=1, source_target_pairs={{0,63},{1,2},{2,1},{3,4},{4,3},{5,6},{6,5},{7,8},{8,7},{9,10},{10,... | collective-permute-start | bytes 1572872 | tf_op jit(solution)/shard_map/ppermute | solution.py:374
  15.3 17.7 %copy-start = (bf16[1,80,128,128]{3,2,1,0:T(8,128)(2,1)S(1)}, bf16[1,80,128,128]{3,2,1,0:T(8,128)(2,1)}, u32[]{:S(2)}) copy-start(bf16[1,80,128,128]{3,2,1,0:T(8,128)(2,1)} %param.19) | copy-start | bytes 7864324
  16.4 18.7 %copy-start.1 = (f32[1,4,16,512]{3,2,1,0:T(8,128)S(1)}, f32[1,4,16,512]{3,2,1,0:T(8,128)}, u32[]{:S(2)}) copy-start(f32[1,4,16,512]{3,2,1,0:T(8,128)} %forcing_ref.1) | copy-start | bytes 393220
  16.4 18.7 %copy-start.2 = (s32[1,16,512]{2,1,0:T(8,128)S(1)}, s32[1,16,512]{2,1,0:T(8,128)}, u32[]{:S(2)}) copy-start(s32[1,16,512]{2,1,0:T(8,128)} %mask_ref.1) | copy-start | bytes 98308
  16.4 9.6 %collective-permute-start.6 = (bf16[256,128]{1,0:T(8,128)(2,1)S(1)}, bf16[256,128]{1,0:T(8,128)(2,1)S(1)}, u32[]{:S(2)}, u32[]{:S(2)}) collective-permute-start(bf16[256,128]{1,0:T(8,128)(2,1)S(1)} %shard_map.125), channel_id=1, source_target_pairs={{0,127},{1,66},{2,65},{3,68},{4,67},{5,70},{6,69},{7,72},{8,71},{9... | collective-permute-start | bytes 196616 | tf_op jit(solution)/shard_map/ppermute | solution.py:379
  16.5 13.2 %collective-permute-start.5 = (bf16[256,128]{1,0:T(8,128)(2,1)S(1)}, bf16[256,128]{1,0:T(8,128)(2,1)S(1)}, u32[]{:S(2)}, u32[]{:S(2)}) collective-permute-start(bf16[256,128]{1,0:T(8,128)(2,1)S(1)} %shard_map.125), channel_id=1, source_target_pairs={{0,65},{1,64},{2,67},{3,66},{4,69},{5,68},{6,71},{7,70},{8,73},{9,... | collective-permute-start | bytes 196616 | tf_op jit(solution)/shard_map/ppermute | solution.py:380
  16.6 16.3 %collective-permute-start.4 = (bf16[256,128]{1,0:T(8,128)(2,1)S(1)}, bf16[256,128]{1,0:T(8,128)(2,1)S(1)}, u32[]{:S(2)}, u32[]{:S(2)}) collective-permute-start(bf16[256,128]{1,0:T(8,128)(2,1)S(1)} %shard_map.125), channel_id=1, source_target_pairs={{0,64},{1,65},{2,66},{3,67},{4,68},{5,69},{6,70},{7,71},{8,72},{9,... | collective-permute-start | bytes 196616 | tf_op jit(solution)/shard_map/ppermute | solution.py:381

commit v4 on v3

--- a/solution.py
+++ b/solution.py
@@ -59,7 +59,7 @@
 
 def exchange_rate(coeffs_ref, mask):
     mask = mask.astype(F32)
-    return coeffs_ref[0, 1] * mask + coeffs_ref[0, 2] * (1.0 - mask)
+    return coeffs_ref[:, 1:2] * mask + coeffs_ref[:, 2:3] * (1.0 - mask)
 
 
 def levels_of(pattern):
@@ -138,30 +138,33 @@
                     edges[at : at + 16, lanes] = pack_node(ref, v, c, SIDE_NODES[side][place], scale)
 
 
-def local_kernel(
-    state_hbm, metric_hbm, node_hbm, level_hbm, coeffs_hbm, partner_hbm, mask_hbm, forcing_hbm,
-    state_ref, part_ref, here_ref, away_ref, here_low_ref, away_low_ref, inner_ref,
-    weights_ref, low_ref, base_ref, factor_ref, low_node_ref,
-    metric_ref, node_ref, level_ref, coeffs_ref, partner_ref, mask_ref, forcing_ref, level_smem, edges, sems,
-):
-    pairs = [
-        (partner_hbm, partner_ref), (node_hbm, node_ref), (level_hbm, level_ref), (coeffs_hbm, coeffs_ref),
-        (metric_hbm, metric_ref),
-    ]
+def first_kernel(state_hbm, partner_hbm, coeffs_hbm, state_ref, here_ref, away_ref, inner_ref, partner_ref, coeffs_ref, sems):
+    pairs = [(partner_hbm, partner_ref), (coeffs_hbm, coeffs_ref)]
     pairs += [(state_hbm.at[:, LANES[c]], state_ref.at[c]) for c in range(4)]
-    pairs += [(mask_hbm, mask_ref), (forcing_hbm, forcing_ref), (level_hbm, level_smem)]
     copies = [pltpu.make_async_copy(source, target, sems.at[i]) for i, (source, target) in enumerate(pairs)]
     for copy in copies:
         copy.start()
-    select_low, spread_inner = low_select(), low_spread(2, 3)
-    weights_ref[:, 512:768] = spread_matrix()
-    for copy in copies[:5]:
-        copy.wait()
+    copies[0].wait()
     for step in range(4):
         columns = partner_ref[0:1, 512 + 256 * step : 768 + 256 * step] - 1024
         hit = iota((1024, 256), 0) == columns
         inner_ref[:, 256 * step : 256 * (step + 1)] = jnp.where(hit, 1.0, 0.0).astype(BF16)
-    penalty = coeffs_ref[0, 0]
+    for copy in copies[1:]:
+        copy.wait()
+    pack_facing(state_ref, coeffs_ref[0, 0], here_ref, away_ref, 0)
+
+
+def local_kernel(
+    state_ref, inner_ref, metric_ref, node_ref, level_ref, coeffs_ref, mask_ref, forcing_ref, order_ref,
+    part_ref, here_ref, away_ref, here_low_ref, away_low_ref,
+    weights_ref, low_ref, base_ref, factor_ref, low_node_ref,
+    level_smem, edges, sem,
+):
+    scalars = pltpu.make_async_copy(level_ref, level_smem, sem)
+    scalars.start()
+    select_low, spread_inner = low_select(), low_spread(2, 3)
+    weights_ref[:, 512:768] = spread_matrix()
+    penalty = coeffs_ref[:, 0:1]
     metric = metric_ref[...]
     node, level = coupling_matrices(node_ref, level_ref)
     weights_ref[:, 0:256] = node
@@ -169,8 +172,6 @@
     low_node = low_node_matrix(node_ref[0])
     low_node_ref[...] = low_node
     factor = diagonal(metric, penalty)
-    for copy in copies[5:]:
-        copy.wait()
     pack_sides(state_ref, penalty, edges)
     lowest = jnp.concatenate([whole_rows(state_ref, 256 * v, 16) for v in range(4)], axis=0)
     high, low = [dot(select_low, part).astype(BF16) for part in halves(penalty * lowest)]
@@ -183,12 +184,12 @@
     edges[272:288, 0:512] = low[32:48]
     edges[272:288, 512:1024] = low[48:64]
     moved = dot(edges[...], inner_ref[...]).astype(BF16)
-    pack_facing(state_ref, penalty, here_ref, away_ref, 0)
     rate = exchange_rate(coeffs_ref, mask_ref[0])
     rates = jnp.concatenate([rate] * 4, axis=0)
     forced = rates * jnp.concatenate([forcing_ref[0, v] for v in range(4)], axis=0)
     factor_low = factor - rate
     factor_ref[...] = factor_low
+    scalars.wait()
     mixed = mix_to_lowest(level_smem, state_ref)
     near = moved[256:288]
     p_low = jnp.concatenate([factor_low] * 4, axis=0) * lowest + forced + mixed
@@ -209,7 +210,7 @@
         p = jnp.concatenate([p_low[16 * v : 16 * (v + 1)], (factors * u + p)[16:256]], axis=0)
         for c in range(4):
             part_ref[c, 256 * v : 256 * (v + 1), :] = p[:, LANES[c]]
-    pack_facing(part_ref, penalty, here_ref, away_ref, 256)
+    pack_facing(part_ref, penalty, here_ref, away_ref, 0)
     mixed = mix_to_lowest(level_smem, part_ref)
     node_at = iota((64, 1), 0) % 16
     facing = jnp.where((node_at // 4 == 0) | (node_at // 4 == 3), penalty * penalty, 0.0)
@@ -218,7 +219,7 @@
 
 def lowest_kernel(
     low_ref, base_ref, factor_ref, low_node_ref, metric_ref, coeffs_ref, here_ref, away_ref, here_map, away_map, inner_ref,
-    surface_ref,
+    order_ref, surface_ref,
 ):
     penalty = coeffs_ref[:, 0:1]
     here = dot(here_ref[...], here_map[...]).astype(BF16)
@@ -239,8 +240,7 @@
 
 
 def tables_kernel(
-    partner_ref, rows_ref, cols_ref, here_in, away_in,
-    here_map, away_map, pick_ref, sum_ref, here_out, away_out,
+    partner_ref, rows_ref, cols_ref, here_map, away_map, pick_ref, sum_ref,
 ):
     last = ends()[0] == 12
     before, after = partner_ref[0:1, 0:512], partner_ref[0:1, 1536:2048] - 2560
@@ -262,14 +262,14 @@
 
 
 def finish_kernel(
-    state_ref, part_ref, here_ref, away_ref, here_map, away_map, inner_ref, weights_ref,
+    state_ref, part_ref, here_first, away_first, here_ref, away_ref, here_map, away_map, inner_ref, weights_ref,
     metric_ref, coeffs_ref, mask_ref, forcing_ref,
     next_hbm, middle_ref, next_ref, edges, sems,
 ):
     penalty = coeffs_ref[:, 0:1]
     metric = metric_ref[...]
-    here = dot(here_ref[...], here_map[...]).astype(BF16)
-    away = dot(away_ref[...], away_map[...]).astype(BF16)
+    here = dot(jnp.concatenate([here_first[...], here_ref[...]], axis=0), here_map[...]).astype(BF16)
+    away = dot(jnp.concatenate([away_first[...], away_ref[...]], axis=0), away_map[...]).astype(BF16)
     for v in range(4):
         rows = slice(64 * v, 64 * (v + 1))
         halo = dot(weights_ref[:, 512:640], jnp.concatenate([here[rows], away[rows]], axis=0))
@@ -280,8 +280,7 @@
     factors = levels_of(diagonal(metric, penalty))
     node = iota((256, 1), 0) % 16
     facing = jnp.where((node // 4 == 0) | (node // 4 == 3), penalty * penalty, 0.0)
-    mask = mask_ref[0].astype(F32)
-    rate = coeffs_ref[:, 1:2] * mask + coeffs_ref[:, 2:3] * (1.0 - mask)
+    rate = exchange_rate(coeffs_ref, mask_ref[0])
     copies = []
     for v in range(4):
         u1 = whole_rows(middle_ref, 256 * v, 256)
@@ -305,14 +304,16 @@
     picked = picked + dot(pick_ref[:, 256:512], own_ref[...])
     picked = picked + dot(pick_ref[:, 512:768], near_ref[...])
     slots = blocks_ref.shape[0]
-    upper = iota((8, 1), 0) < 4
-    for pair in range(slots // 2):
-        part = picked[8 * pair : 8 * (pair + 1)]
+    for quad in range(slots // 4):
+        part = picked[16 * quad : 16 * (quad + 1)]
+        upper = iota((16, 1), 0) % 8 < 4
         left = jnp.concatenate([jnp.where(upper, part, 0.0), jnp.where(upper, 0.0, part)], axis=1).astype(BF16)
-        right = jnp.concatenate([blocks_ref[2 * pair], blocks_ref[2 * pair + 1]], axis=1)
-        products[8 * pair : 8 * (pair + 1), :] = lax.dot_general(
-            left, right, (((1,), (1,)), ((), ())), preferred_element_type=F32
+        right = [jnp.concatenate([blocks_ref[4 * quad + 2 * h], blocks_ref[4 * quad + 2 * h + 1]], axis=1) for h in range(2)]
+        both = lax.dot_general(
+            left, jnp.concatenate(right, axis=0), (((1,), (1,)), ((), ())), preferred_element_type=F32
         )
+        products[16 * quad : 16 * quad + 8, :] = both[0:8, 0:128]
+        products[16 * quad + 8 : 16 * (quad + 1), :] = both[8:16, 128:256]
     value = products[...]
     high = value.astype(BF16)
     low = (value - high.astype(F32)).astype(BF16)
@@ -348,33 +349,40 @@
     crossed = lambda pairs: [(c * tiles + a, (1 - c) * tiles + b) for c in range(2) for a, b in pairs]
     straight = [(t, t) for t in range(tiles)]
     flat = state.reshape(1024, 512)
-    inputs = (flat, metric, element_coupling, level_coupling, coeffs, edge_partner, sea_mask, forcing)
-    (chunks, part, here_edge, away_edge, here_low, away_low, inner, weights, low, base, factor, low_node) = call(
+    hbm = lambda *values: [pltpu.with_memory_space_constraint(value, pltpu.HBM) for value in values]
+    chunks, here_first, away_first, inner = call(
+        first_kernel,
+        [((4, 1024, 128), F32), ((256, 512), BF16), ((256, 512), BF16), ((1024, 1024), BF16)],
+        [pltpu.VMEM(edge_partner.shape, jnp.int32), pltpu.SMEM(coeffs.shape, F32), pltpu.SemaphoreType.DMA((6,))],
+        "hhh",
+    )(*hbm(flat, edge_partner, coeffs))
+    away_first = lax.ppermute(away_first, "tile", away)
+    here_first = lax.ppermute(here_first, "tile", here)
+    inputs = (metric, element_coupling, level_coupling, coeffs, sea_mask, forcing)
+    (part, here_edge, away_edge, here_low, away_low, weights, low, base, factor, low_node) = call(
         local_kernel,
         [
-            ((4, 1024, 128), F32), ((4, 1024, 128), F32), ((512, 512), BF16), ((512, 512), BF16), ((64, 512), BF16),
-            ((64, 512), BF16), ((1024, 1024), BF16), ((256, 768), BF16),
+            ((4, 1024, 128), F32), ((256, 512), BF16), ((256, 512), BF16), ((64, 512), BF16),
+            ((64, 512), BF16), ((256, 768), BF16),
             ((64, 512), F32), ((64, 512), F32), ((16, 512), F32), ((64, 192), BF16),
         ],
-        [(pltpu.SMEM if value is coeffs else pltpu.VMEM)(value.shape, value.dtype) for value in inputs[1:]]
-        + [pltpu.SMEM((1, 16, 16), F32), pltpu.VMEM((288, 1024), BF16), pltpu.SemaphoreType.DMA((12,))],
-        "hhhhhhhh",
-    )(*[pltpu.with_memory_space_constraint(value, pltpu.HBM) for value in inputs])
+        [pltpu.SMEM((1, 16, 16), F32), pltpu.VMEM((288, 1024), BF16), pltpu.SemaphoreType.DMA],
+        "v" * 8 + "a",
+    )(chunks, inner, *inputs, here_first)
     away_low = lax.ppermute(away_low, "tile", away)
     here_low = lax.ppermute(here_low, "tile", here)
     slots = remap_rows.shape[1]
-    here_map, away_map, pick, total, here_edge, away_edge = call(
+    here_map, away_map, pick, total = call(
         tables_kernel,
         [
             ((512, 512), BF16), ((512, 512), BF16), ((4 * slots, 768), BF16), ((256, 4 * slots), BF16),
-            (here_edge.shape, BF16), (away_edge.shape, BF16),
         ],
-        inputs="vvvaa", results="vvvvaa", aliases={3: 4, 4: 5}, cost=4_000_000_000,
-    )(edge_partner, remap_rows, remap_cols, here_edge, away_edge)
+        inputs="vvv", results="vvvv", cost=4_000_000_000,
+    )(edge_partner, remap_rows, remap_cols)
     away_edge = lax.ppermute(away_edge, "tile", away)
     here_edge = lax.ppermute(here_edge, "tile", here)
-    (surface,) = call(lowest_kernel, [((256, 128), BF16)], inputs="v" * 11, cost=40_000_000_000)(
-        low, base, factor, low_node, metric, coeffs, here_low, away_low, here_map, away_map, inner
+    (surface,) = call(lowest_kernel, [((256, 128), BF16)], inputs="v" * 11 + "a", cost=40_000_000_000)(
+        low, base, factor, low_node, metric, coeffs, here_low, away_low, here_map, away_map, inner, here_edge
     )
     far = lax.ppermute(surface, ("comp", "tile"), crossed(away))
     near = lax.ppermute(surface, ("comp", "tile"), crossed(here))
@@ -386,8 +394,8 @@
             pltpu.VMEM((4, 1024, 128), F32), pltpu.VMEM((1024, 512), F32), pltpu.VMEM((256, 1024), BF16),
             pltpu.SemaphoreType.DMA((4,)),
         ],
-        "v" * 12, "h",
-    )(chunks, part, here_edge, away_edge, here_map, away_map, inner, weights, metric, coeffs, sea_mask, forcing)
+        "v" * 14, "h",
+    )(chunks, part, here_first, away_first, here_edge, away_edge, here_map, away_map, inner, weights, metric, coeffs, sea_mask, forcing)
     (new_forcing,) = call(
         remap_kernel, [(forcing.shape, F32)], [pltpu.VMEM((4 * slots, 128), F32)], "v" * 6,
     )(own, near, far, pick, total, remap_weights[0])

time: 38.9 us -> 37.2 us (0.956)
  the two profiles are of different devices: /device:TPU:64 before, /device:TPU:0 now
where the time goes in v4:
time: 37.2 us; the launch traced here: 37 us
  starting transfers between devices  18.1 us (49%)
  Pallas kernels  12.8 us (34%)
  waiting for transfers between devices  5.28 us (14%)
  between operations  0.81 us (2%)
    ppermute x1, starting transfers between devices, shards(): away_first = lax.ppermute(away_first, 'tile', away)  8.71 us
    ppermute x1, starting transfers between devices, shards(): away_edge = lax.ppermute(away_edge, 'tile', away)  6.12 us
    pallas_call x1, Pallas kernels, shards(): call(finish_kernel, [((1024, 512), F32)], [pltpu.VMEM((4, 1024, 128), F32...  3.72 us
    pallas_call x1, Pallas kernels, shards(): call(local_kernel, [((4, 1024, 128), F32), ((256, 512), BF16), ((256, 512...  3.23 us
    ppermute x1, waiting for transfers between devices, shards(): far = lax.ppermute(surface, ('comp', 'tile'), crossed(away))  2.33 us
    pallas_call x1, Pallas kernels, shards(): call(first_kernel, [((4, 1024, 128), F32), ((256, 512), BF16), ((256, 512...  2.13 us
    pallas_call x1, Pallas kernels, shards(): call(remap_kernel, [(forcing.shape, F32)], [pltpu.VMEM((4 * slots, 128),...  2.05 us
    ppermute x1, starting transfers between devices, shards(): far = lax.ppermute(surface, ('comp', 'tile'), crossed(away))  1.57 us
  transfers between devices with their start and end apart: 9, of which 3 were waited for; matrix products, arithmetic and copies ran while one was open for 0% of the time, Pallas kernels for 23%

profile of v4, /device:TPU:0, one launch (start us, length us, event | category | flops | bytes accessed | tf_op | source)
XLA Modules:
  0.0 37.0 jit_solution(6696965838845867090)
XLA Ops:
  0.7 2.1 %shard_map.122 = (f32[4,1024,128]{2,1,0:T(8,128)S(1)}, bf16[256,512]{1,0:T(8,128)(2,1)S(1)}, bf16[256,512]{1,0:T(8,128)(2,1)S(1)}, bf16[1024,1024]{1,0:T(8,128)(2,1)S(1)}) custom-call(f32[1024,512]{1,0:T(8,128)} %bitcast.4, s32[1,2048]{1,0:T(1,128)} %partner_ref.1, f32[1,3]{1,0:T(1,128)} %coeffs_ref.5), custom_call_target="tpu_custom_call" | custom-call | tf_op jit(solution)/shard_map/pallas_call | solution.py:353
  2.8 0.1 collective-permute-start
  2.9 8.7 %collective-permute-start.1 = (bf16[256,512]{1,0:T(8,128)(2,1)S(1)}, bf16[256,512]{1,0:T(8,128)(2,1)S(1)}, u32[]{:S(2)}, u32[]{:S(2)}) collective-permute-start(bf16[256,512]{1,0:T(8,128)(2,1)S(1)} %get-tuple-element.24), channel_id=1, source_target_pairs={{0,63},{1,2},{2,1},{3,4},{4,3},{5,6},{6,5},{7,8},{8,7},{9,10},{10,... | collective-permute-start | bytes 786440 | tf_op jit(solution)/shard_map/ppermute | solution.py:359
  11.7 0.0 copy-start.5
  11.7 0.0 copy-start.8
  11.7 0.0 copy-start.9
  11.7 3.2 %shard_map.123 = (f32[4,1024,128]{2,1,0:T(8,128)S(1)}, bf16[256,512]{1,0:T(8,128)(2,1)S(1)}, bf16[256,512]{1,0:T(8,128)(2,1)S(1)}, bf16[64,512]{1,0:T(8,128)(2,1...) custom-call(f32[4,1024,128]{2,1,0:T(8,128)S(1)} %get-tuple-element.2, ...), custom_call_target="tpu_custom_call" | custom-call | tf_op jit(solution)/shard_map/pallas_call | solution.py:362
  15.0 0.1 collective-permute-start.4
  15.0 1.5 %collective-permute-start.5 = (bf16[64,512]{1,0:T(8,128)(2,1)S(1)}, bf16[64,512]{1,0:T(8,128)(2,1)S(1)}, u32[]{:S(2)}, u32[]{:S(2)}) collective-permute-start(bf16[64,512]{1,0:T(8,128)(2,1)S(1)} %get-tuple-element.35), channel_id=1, source_target_pairs={{0,63},{1,2},{2,1},{3,4},{4,3},{5,6},{6,5},{7,8},{8,7},{9,10},{10,... | collective-permute-start | bytes 196616 | tf_op jit(solution)/shard_map/ppermute | solution.py:372
  16.6 0.0 collective-permute-start.2
  16.6 0.6 %shard_map.124 = (bf16[512,512]{1,0:T(8,128)(2,1)S(1)}, bf16[512,512]{1,0:T(8,128)(2,1)S(1)}, bf16[320,768]{1,0:T(8,128)(2,1)S(1)}, bf16[256,320]{1,0:T(8,128)(2,1)S(1)}) custom-call(s32[1,2048]{1,0:T(1,128)S(1)} %copy-done.5, s32[1,80]{1,0:T(1,128)S(1)} %copy-done.8, s32[1,80]{1,0:T(1,128)S(1)} %copy-done.9), custom_call_target="tpu_custom_call" | custom-call | flops 4000000000 | tf_op jit(solution)/shard_map/pallas_call | solution.py:375
  17.2 6.1 %collective-permute-start.3 = (bf16[256,512]{1,0:T(8,128)(2,1)S(1)}, bf16[256,512]{1,0:T(8,128)(2,1)S(1)}, u32[]{:S(2)}, u32[]{:S(2)}) collective-permute-start(bf16[256,512]{1,0:T(8,128)(2,1)S(1)} %get-tuple-element.26), channel_id=1, source_target_pairs={{0,63},{1,2},{2,1},{3,4},{4,3},{5,6},{6,5},{7,8},{8,7},{9,10},{10,... | collective-permute-start | bytes 786440 | tf_op jit(solution)/shard_map/ppermute | solution.py:382
  23.3 0.0 collective-permute-done.4.here_ref
  23.3 1.4 %collective-permute-done.5.away_ref = bf16[64,512]{1,0:T(8,128)(2,1)S(1)} collective-permute-done((bf16[64,512]{1,0:T(8,128)(2,1)S(1)}, bf16[64,512]{1,0:T(8,128)(2,1)S(1)}, u32[]{:S(2)}, u32[]{:S(2)}) %collective-permute-start.5) | collective-permute-done | bytes 65568 | tf_op jit(solution)/shard_map/ppermute | solution.py:372
  24.6 0.0 collective-permute-done.2.here_ref.order_ref
  24.6 1.1 %shard_map.126 = bf16[256,128]{1,0:T(8,128)(2,1)S(1)} custom-call(f32[64,512]{1,0:T(8,128)S(1)} %get-tuple-element.30.low_ref, f32[64,512]{1,0:T(8,128)S(1)} %get-tuple-element.31.base_ref, f32[16,512]{1,0:T(8,128)S(1)} %get-tuple-element.32.factor_ref, bf16[64,192]{1,0:T(8,128)(2,1)S(1)} %get-tuple-element.33.low_node_ref, f32[1,512]{1,0:T(1,128)S(1)} %copy-done.6, ...), custom_call_target="tpu_custom_call" | custom-call | flops 40000000000 | tf_op jit(solution)/shard_map/pallas_call | solution.py:384
  25.8 1.6 %collective-permute-start.8 = (bf16[256,128]{1,0:T(8,128)(2,1)S(1)}, bf16[256,128]{1,0:T(8,128)(2,1)S(1)}, u32[]{:S(2)}, u32[]{:S(2)}) collective-permute-start(bf16[256,128]{1,0:T(8,128)(2,1)S(1)} %shard_map.126), channel_id=1, source_target_pairs={{0,127},{1,66},{2,65},{3,68},{4,67},{5,70},{6,69},{7,72},{8,71},{9... | collective-permute-start | bytes 196616 | tf_op jit(solution)/shard_map/ppermute | solution.py:387
  27.3 0.0 collective-permute-start.7
  27.3 0.0 collective-permute-start.6
  27.3 0.0 collective-permute-done.1.away_first
  27.4 1.6 %collective-permute-done.3.away_ref = bf16[256,512]{1,0:T(8,128)(2,1)S(1)} collective-permute-done((bf16[256,512]{1,0:T(8,128)(2,1)S(1)}, bf16[256,512]{1,0:T(8,128)(2,1)S(1)}, u32[]{:S(2)}, u32[]{:S(2)}) %collective-permute-start.3) | collective-permute-done | bytes 262176 | tf_op jit(solution)/shard_map/ppermute | solution.py:382
  28.9 3.7 %shard_map.125 = f32[1024,512]{1,0:T(8,128)} custom-call(f32[4,1024,128]{2,1,0:T(8,128)S(1)} %get-tuple-element.20.state_ref, f32[4,1024,128]{2,1,0:T(8,128)S(1)} %get-tuple-element.23.part_ref, bf16[256,512]{1,0:T(8,128)(2,1)S(1)} %collective-permute-done.order_ref.here_first, bf16[256,512]{1,0:T(8,128)(2,1)S(1)} %collective-permute-done.1.away_first, ...), custom_call_target="tpu_custom_call" | custom-call | tf_op jit(solution)/shard_map/pallas_call | solution.py:390
  32.6 2.3 %collective-permute-done.8.far_ref = bf16[256,128]{1,0:T(8,128)(2,1)S(1)} collective-permute-done((bf16[256,128]{1,0:T(8,128)(2,1)S(1)}, bf16[256,128]{1,0:T(8,128)(2,1)S(1)}, u32[]{:S(2)}, u32[]{:S(2)}) %collective-permute-start.8) | collective-permute-done | bytes 65568 | tf_op jit(solution)/shard_map/ppermute | solution.py:387
  35.0 2.0 %shard_map.127 = f32[1,4,16,512]{3,2,1,0:T(8,128)} custom-call(bf16[256,128]{1,0:T(8,128)(2,1)S(1)} %collective-permute-done.6.own_ref, bf16[256,128]{1,0:T(8,128)(2,1)S(1)} %collective-permute-done.7.near_ref, bf16[256,128]{1,0:T(8,128)(2,1)S(1)} %collective-permute-done.8.far_ref, bf16[320,768]{1,0:T(8,128)(2,1)S(1)} %get-tuple-element.36.pick_ref, ...), custom_call_target="tpu_custom_call" | custom-call | tf_op jit(solution)/shard_map/pallas_call | solution.py:399
  (20 shorter events, 0.0 us)
Async XLA Ops:
  0.6 11.0 %copy-start.7 = (f32[1,3]{1,0:T(1,128)S(1)}, f32[1,3]{1,0:T(1,128)}, u32[]{:S(2)}) copy-start(f32[1,3]{1,0:T(1,128)} %coeffs_ref.5) | copy-start | bytes 40
  0.6 11.0 %copy-start.6 = (f32[1,512]{1,0:T(1,128)S(1)}, f32[1,512]{1,0:T(1,128)}, u32[]{:S(2)}) copy-start(f32[1,512]{1,0:T(1,128)} %metric_ref.5) | copy-start | bytes 6148
  0.7 11.0 %copy-start.1 = (f32[1,4,16,512]{3,2,1,0:T(8,128)S(1)}, f32[1,4,16,512]{3,2,1,0:T(8,128)}, u32[]{:S(2)}) copy-start(f32[1,4,16,512]{3,2,1,0:T(8,128)} %forcing_ref.3) | copy-start | bytes 393220
  0.7 11.0 %copy-start.2 = (s32[1,16,512]{2,1,0:T(8,128)S(1)}, s32[1,16,512]{2,1,0:T(8,128)}, u32[]{:S(2)}) copy-start(s32[1,16,512]{2,1,0:T(8,128)} %mask_ref.3) | copy-start | bytes 98308
  0.7 11.0 %copy-start.4 = (f32[1,16,16]{2,1,0:T(8,128)S(1)}, f32[1,16,16]{2,1,0:T(8,128)}, u32[]{:S(2)}) copy-start(f32[1,16,16]{2,1,0:T(8,128)} %level_ref.1) | copy-start | bytes 3076
  0.7 11.0 %copy-start.3 = (f32[1,16,16]{2,1,0:T(8,128)S(1)}, f32[1,16,16]{2,1,0:T(8,128)}, u32[]{:S(2)}) copy-start(f32[1,16,16]{2,1,0:T(8,128)} %node_ref.1) | copy-start | bytes 3076
  2.8 8.8 %collective-permute-start = (bf16[256,512]{1,0:T(8,128)(2,1)S(1)}, bf16[256,512]{1,0:T(8,128)(2,1)S(1)}, u32[]{:S(2)}, u32[]{:S(2)}) collective-permute-start(bf16[256,512]{1,0:T(8,128)(2,1)S(1)} %get-tuple-element.22), channel_id=1, source_target_pairs={{0,1},{1,0},{2,3},{3,2},{4,5},{5,4},{6,7},{7,6},{8,9},{9,8},{10,11... | collective-permute-start | bytes 786440 | tf_op jit(solution)/shard_map/ppermute | solution.py:360
  2.9 24.4 %collective-permute-start.1 = (bf16[256,512]{1,0:T(8,128)(2,1)S(1)}, bf16[256,512]{1,0:T(8,128)(2,1)S(1)}, u32[]{:S(2)}, u32[]{:S(2)}) collective-permute-start(bf16[256,512]{1,0:T(8,128)(2,1)S(1)} %get-tuple-element.24), channel_id=1, source_target_pairs={{0,63},{1,2},{2,1},{3,4},{4,3},{5,6},{6,5},{7,8},{8,7},{9,10},{10,... | collective-permute-start | bytes 786440 | tf_op jit(solution)/shard_map/ppermute | solution.py:359
  11.7 4.9 %copy-start.5 = (s32[1,2048]{1,0:T(1,128)S(1)}, s32[1,2048]{1,0:T(1,128)}, u32[]{:S(2)}) copy-start(s32[1,2048]{1,0:T(1,128)} %partner_ref.1) | copy-start | bytes 24580
  11.7 4.9 %copy-start.8 = (s32[1,80]{1,0:T(1,128)S(1)}, s32[1,80]{1,0:T(1,128)}, u32[]{:S(2)}) copy-start(s32[1,80]{1,0:T(1,128)} %rows_ref.1) | copy-start | bytes 964
  11.7 4.9 %copy-start.9 = (s32[1,80]{1,0:T(1,128)S(1)}, s32[1,80]{1,0:T(1,128)}, u32[]{:S(2)}) copy-start(s32[1,80]{1,0:T(1,128)} %cols_ref.1) | copy-start | bytes 964
  15.0 8.3 %collective-permute-start.4 = (bf16[64,512]{1,0:T(8,128)(2,1)S(1)}, bf16[64,512]{1,0:T(8,128)(2,1)S(1)}, u32[]{:S(2)}, u32[]{:S(2)}) collective-permute-start(bf16[64,512]{1,0:T(8,128)(2,1)S(1)} %get-tuple-element.34), channel_id=1, source_target_pairs={{0,1},{1,0},{2,3},{3,2},{4,5},{5,4},{6,7},{7,6},{8,9},{9,8},{10,11... | collective-permute-start | bytes 196616 | tf_op jit(solution)/shard_map/ppermute | solution.py:373
  15.0 9.6 %collective-permute-start.5 = (bf16[64,512]{1,0:T(8,128)(2,1)S(1)}, bf16[64,512]{1,0:T(8,128)(2,1)S(1)}, u32[]{:S(2)}, u32[]{:S(2)}) collective-permute-start(bf16[64,512]{1,0:T(8,128)(2,1)S(1)} %get-tuple-element.35), channel_id=1, source_target_pairs={{0,63},{1,2},{2,1},{3,4},{4,3},{5,6},{6,5},{7,8},{8,7},{9,10},{10,... | collective-permute-start | bytes 196616 | tf_op jit(solution)/shard_map/ppermute | solution.py:372
  16.6 8.1 %collective-permute-start.2 = (bf16[256,512]{1,0:T(8,128)(2,1)S(1)}, bf16[256,512]{1,0:T(8,128)(2,1)S(1)}, u32[]{:S(2)}, u32[]{:S(2)}) collective-permute-start(bf16[256,512]{1,0:T(8,128)(2,1)S(1)} %get-tuple-element.25), channel_id=1, source_target_pairs={{0,1},{1,0},{2,3},{3,2},{4,5},{5,4},{6,7},{7,6},{8,9},{9,8},{10,11... | collective-permute-start | bytes 786440 | tf_op jit(solution)/shard_map/ppermute | solution.py:383
  17.2 11.8 %collective-permute-start.3 = (bf16[256,512]{1,0:T(8,128)(2,1)S(1)}, bf16[256,512]{1,0:T(8,128)(2,1)S(1)}, u32[]{:S(2)}, u32[]{:S(2)}) collective-permute-start(bf16[256,512]{1,0:T(8,128)(2,1)S(1)} %get-tuple-element.26), channel_id=1, source_target_pairs={{0,63},{1,2},{2,1},{3,4},{4,3},{5,6},{6,5},{7,8},{8,7},{9,10},{10,... | collective-permute-start | bytes 786440 | tf_op jit(solution)/shard_map/ppermute | solution.py:382
  25.8 9.2 %collective-permute-start.8 = (bf16[256,128]{1,0:T(8,128)(2,1)S(1)}, bf16[256,128]{1,0:T(8,128)(2,1)S(1)}, u32[]{:S(2)}, u32[]{:S(2)}) collective-permute-start(bf16[256,128]{1,0:T(8,128)(2,1)S(1)} %shard_map.126), channel_id=1, source_target_pairs={{0,127},{1,66},{2,65},{3,68},{4,67},{5,70},{6,69},{7,72},{8,71},{9... | collective-permute-start | bytes 196616 | tf_op jit(solution)/shard_map/ppermute | solution.py:387
  27.3 7.6 %collective-permute-start.7 = (bf16[256,128]{1,0:T(8,128)(2,1)S(1)}, bf16[256,128]{1,0:T(8,128)(2,1)S(1)}, u32[]{:S(2)}, u32[]{:S(2)}) collective-permute-start(bf16[256,128]{1,0:T(8,128)(2,1)S(1)} %shard_map.126), channel_id=1, source_target_pairs={{0,65},{1,64},{2,67},{3,66},{4,69},{5,68},{6,71},{7,70},{8,73},{9,... | collective-permute-start | bytes 196616 | tf_op jit(solution)/shard_map/ppermute | solution.py:388
  27.3 7.6 %collective-permute-start.6 = (bf16[256,128]{1,0:T(8,128)(2,1)S(1)}, bf16[256,128]{1,0:T(8,128)(2,1)S(1)}, u32[]{:S(2)}, u32[]{:S(2)}) collective-permute-start(bf16[256,128]{1,0:T(8,128)(2,1)S(1)} %shard_map.126), channel_id=1, source_target_pairs={{0,64},{1,65},{2,66},{3,67},{4,68},{5,69},{6,70},{7,71},{8,72},{9,... | collective-permute-start | bytes 196616 | tf_op jit(solution)/shard_map/ppermute | solution.py:389
  28.9 6.1 %copy-start = (bf16[1,80,128,128]{3,2,1,0:T(8,128)(2,1)S(1)}, bf16[1,80,128,128]{3,2,1,0:T(8,128)(2,1)}, u32[]{:S(2)}) copy-start(bf16[1,80,128,128]{3,2,1,0:T(8,128)(2,1)} %param.19) | copy-start | bytes 7864324

commit v5 on v4

--- a/solution.py
+++ b/solution.py
@@ -42,12 +42,15 @@
     rows, cols = iota((16, 256), 0), iota((16, 256), 1)
     inner, outer = (cols % 16 == rows).astype(BF16), (cols // 16 == rows).astype(BF16)
     r, c = iota((256, 256), 0), iota((256, 256), 1)
-    node = jnp.concatenate([dot(node_ref[0].astype(BF16), inner)] * 16, axis=0)
-    node = jnp.where(r // 16 == c // 16, node, 0.0).astype(BF16)
-    level = dot(level_ref[0].astype(BF16), outer)
-    level = jnp.concatenate([jnp.broadcast_to(level[l : l + 1], (16, 256)) for l in range(16)], axis=0)
-    level = jnp.where(r % 16 == c % 16, level, 0.0).astype(BF16)
-    return node, level
+    both = []
+    for part in halves(node_ref[0]):
+        node = jnp.concatenate([dot(part, inner)] * 16, axis=0)
+        both.append(jnp.where(r // 16 == c // 16, node, 0.0).astype(BF16))
+    for part in halves(level_ref[0]):
+        level = dot(part, outer)
+        level = jnp.concatenate([jnp.broadcast_to(level[l : l + 1], (16, 256)) for l in range(16)], axis=0)
+        both.append(jnp.where(r % 16 == c % 16, level, 0.0).astype(BF16))
+    return both[0], both[2], both[1], both[3]
 
 
 def diagonal(metric, penalty):
@@ -166,9 +169,8 @@
     weights_ref[:, 512:768] = spread_matrix()
     penalty = coeffs_ref[:, 0:1]
     metric = metric_ref[...]
-    node, level = coupling_matrices(node_ref, level_ref)
-    weights_ref[:, 0:256] = node
-    weights_ref[:, 256:512] = level
+    for part, start in zip(coupling_matrices(node_ref, level_ref), (0, 256, 768, 1024)):
+        weights_ref[:, start : start + 256] = part
     low_node = low_node_matrix(node_ref[0])
     low_node_ref[...] = low_node
     factor = diagonal(metric, penalty)
@@ -206,7 +208,8 @@
         u = whole_rows(state_ref, 256 * v, 256)
         operand = [(u * metric).astype(BF16), u.astype(BF16)]
         operand += [moved[64 * v : 64 * (v + 1), 512 * side : 512 * (side + 1)] for side in range(2)]
-        p = dot(jnp.concatenate([weights_ref[:, 0:512], weights_ref[:, 640:768]], axis=1), jnp.concatenate(operand, axis=0))
+        operand += operand[0:2]
+        p = dot(jnp.concatenate([weights_ref[:, 0:512], weights_ref[:, 640:1280]], axis=1), jnp.concatenate(operand, axis=0))
         p = jnp.concatenate([p_low[16 * v : 16 * (v + 1)], (factors * u + p)[16:256]], axis=0)
         for c in range(4):
             part_ref[c, 256 * v : 256 * (v + 1), :] = p[:, LANES[c]]
@@ -288,6 +291,7 @@
         far = slice(256 + 64 * v, 256 + 64 * (v + 1))
         operand = [(u1 * metric).astype(BF16), u1.astype(BF16), here[far], away[far]]
         operand += [moved[rows, 512 * side : 512 * (side + 1)] for side in range(2)]
+        operand += operand[0:2]
         x = factors * u1 + facing * whole_rows(state_ref, 256 * v, 256)
         x = x + dot(weights_ref[...], jnp.concatenate(operand, axis=0))
         added = rate * (forcing_ref[0, v] - u1[0:16])
@@ -363,7 +367,7 @@
         local_kernel,
         [
             ((4, 1024, 128), F32), ((256, 512), BF16), ((256, 512), BF16), ((64, 512), BF16),
-            ((64, 512), BF16), ((256, 768), BF16),
+            ((64, 512), BF16), ((256, 1280), BF16),
             ((64, 512), F32), ((64, 512), F32), ((16, 512), F32), ((64, 192), BF16),
         ],
         [pltpu.SMEM((1, 16, 16), F32), pltpu.VMEM((288, 1024), BF16), pltpu.SemaphoreType.DMA],

time: 37.2 us -> 37.8 us (1.016)
  Pallas kernels: 12.8 us -> 13.9 us
  waiting for transfers between devices: 5.28 us -> 4.75 us
    pallas_call x1, Pallas kernels: 3.23 us -> 3.82 us  [shards(): call(local_kernel, [((4, 1024, 128), F32), ((256, 512), BF16), ((256, 512...]
    pallas_call x1, Pallas kernels: 3.72 us -> 4.26 us  [shards(): call(finish_kernel, [((1024, 512), F32)], [pltpu.VMEM((4, 1024, 128), F32...]
    ppermute x1, waiting for transfers between devices: 2.33 us -> 1.79 us  [shards(): far = lax.ppermute(surface, ('comp', 'tile'), crossed(away))]
  transfers between devices with their start and end apart: 9 -> 9, of which waited for: 3 -> 3; matrix products, arithmetic and copies ran while one was open for 0% -> 0% of each run, Pallas kernels for 23% -> 26%
where the time goes in v5:
time: 37.8 us; the launch traced here: 37.6 us
  starting transfers between devices  18.1 us (48%)
  Pallas kernels  13.9 us (37%)
  waiting for transfers between devices  4.75 us (13%)
  between operations  0.81 us (2%)
    ppermute x1, starting transfers between devices, shards(): away_first = lax.ppermute(away_first, 'tile', away)  8.71 us
    ppermute x1, starting transfers between devices, shards(): away_edge = lax.ppermute(away_edge, 'tile', away)  6.12 us
    pallas_call x1, Pallas kernels, shards(): call(finish_kernel, [((1024, 512), F32)], [pltpu.VMEM((4, 1024, 128), F32...  4.26 us
    pallas_call x1, Pallas kernels, shards(): call(local_kernel, [((4, 1024, 128), F32), ((256, 512), BF16), ((256, 512...  3.82 us
    pallas_call x1, Pallas kernels, shards(): call(first_kernel, [((4, 1024, 128), F32), ((256, 512), BF16), ((256, 512...  2.13 us
    pallas_call x1, Pallas kernels, shards(): call(remap_kernel, [(forcing.shape, F32)], [pltpu.VMEM((4 * slots, 128),...  2.04 us
    ppermute x1, waiting for transfers between devices, shards(): far = lax.ppermute(surface, ('comp', 'tile'), crossed(away))  1.79 us
    ppermute x1, waiting for transfers between devices, shards(): away_edge = lax.ppermute(away_edge, 'tile', away)  1.56 us
  transfers between devices with their start and end apart: 9, of which 3 were waited for; matrix products, arithmetic and copies ran while one was open for 0% of the time, Pallas kernels for 26%

profile of v5, /device:TPU:0, one launch (start us, length us, event | category | flops | bytes accessed | tf_op | source)
XLA Modules:
  0.0 37.6 jit_solution(16797505472536435461)
XLA Ops:
  0.7 2.1 %shard_map.122 = (f32[4,1024,128]{2,1,0:T(8,128)S(1)}, bf16[256,512]{1,0:T(8,128)(2,1)S(1)}, bf16[256,512]{1,0:T(8,128)(2,1)S(1)}, bf16[1024,1024]{1,0:T(8,128)(2,1)S(1)}) custom-call(f32[1024,512]{1,0:T(8,128)} %bitcast.5, s32[1,2048]{1,0:T(1,128)} %partner_ref.1, f32[1,3]{1,0:T(1,128)} %coeffs_ref.5), custom_call_target="tpu_custom_call" | custom-call | tf_op jit(solution)/shard_map/pallas_call | solution.py:357
  2.8 0.1 collective-permute-start
  2.9 8.7 %collective-permute-start.1 = (bf16[256,512]{1,0:T(8,128)(2,1)S(1)}, bf16[256,512]{1,0:T(8,128)(2,1)S(1)}, u32[]{:S(2)}, u32[]{:S(2)}) collective-permute-start(bf16[256,512]{1,0:T(8,128)(2,1)S(1)} %get-tuple-element.24), channel_id=1, source_target_pairs={{0,63},{1,2},{2,1},{3,4},{4,3},{5,6},{6,5},{7,8},{8,7},{9,10},{10,... | collective-permute-start | bytes 786440 | tf_op jit(solution)/shard_map/ppermute | solution.py:363
  11.6 0.0 collective-permute-done.order_ref.here_first
  11.7 0.0 copy-start.5
  11.7 0.0 copy-start.8
  11.7 0.0 copy-start.9
  11.7 3.8 %shard_map.123 = (f32[4,1024,128]{2,1,0:T(8,128)S(1)}, bf16[256,512]{1,0:T(8,128)(2,1)S(1)}, bf16[256,512]{1,0:T(8,128)(2,1)S(1)}, bf16[64,512]{1,0:T(8,128)(2,1...) custom-call(f32[4,1024,128]{2,1,0:T(8,128)S(1)} %get-tuple-element.2, ...), custom_call_target="tpu_custom_call" | custom-call | tf_op jit(solution)/shard_map/pallas_call | solution.py:366
  15.6 0.1 collective-permute-start.4
  15.6 1.5 %collective-permute-start.5 = (bf16[64,512]{1,0:T(8,128)(2,1)S(1)}, bf16[64,512]{1,0:T(8,128)(2,1)S(1)}, u32[]{:S(2)}, u32[]{:S(2)}) collective-permute-start(bf16[64,512]{1,0:T(8,128)(2,1)S(1)} %get-tuple-element.35), channel_id=1, source_target_pairs={{0,63},{1,2},{2,1},{3,4},{4,3},{5,6},{6,5},{7,8},{8,7},{9,10},{10,... | collective-permute-start | bytes 196616 | tf_op jit(solution)/shard_map/ppermute | solution.py:376
  17.2 0.0 collective-permute-start.2
  17.2 0.6 %shard_map.124 = (bf16[512,512]{1,0:T(8,128)(2,1)S(1)}, bf16[512,512]{1,0:T(8,128)(2,1)S(1)}, bf16[320,768]{1,0:T(8,128)(2,1)S(1)}, bf16[256,320]{1,0:T(8,128)(2,1)S(1)}) custom-call(s32[1,2048]{1,0:T(1,128)S(1)} %copy-done.5, s32[1,80]{1,0:T(1,128)S(1)} %copy-done.8, s32[1,80]{1,0:T(1,128)S(1)} %copy-done.9), custom_call_target="tpu_custom_call" | custom-call | flops 4000000000 | tf_op jit(solution)/shard_map/pallas_call | solution.py:379
  17.7 6.1 %collective-permute-start.3 = (bf16[256,512]{1,0:T(8,128)(2,1)S(1)}, bf16[256,512]{1,0:T(8,128)(2,1)S(1)}, u32[]{:S(2)}, u32[]{:S(2)}) collective-permute-start(bf16[256,512]{1,0:T(8,128)(2,1)S(1)} %get-tuple-element.26), channel_id=1, source_target_pairs={{0,63},{1,2},{2,1},{3,4},{4,3},{5,6},{6,5},{7,8},{8,7},{9,10},{10,... | collective-permute-start | bytes 786440 | tf_op jit(solution)/shard_map/ppermute | solution.py:386
  23.9 0.0 collective-permute-done.4.here_ref
  23.9 1.4 %collective-permute-done.5.away_ref = bf16[64,512]{1,0:T(8,128)(2,1)S(1)} collective-permute-done((bf16[64,512]{1,0:T(8,128)(2,1)S(1)}, bf16[64,512]{1,0:T(8,128)(2,1)S(1)}, u32[]{:S(2)}, u32[]{:S(2)}) %collective-permute-start.5) | collective-permute-done | bytes 65568 | tf_op jit(solution)/shard_map/ppermute | solution.py:376
  25.2 0.0 collective-permute-done.2.here_ref.order_ref
  25.2 1.1 %shard_map.126 = bf16[256,128]{1,0:T(8,128)(2,1)S(1)} custom-call(f32[64,512]{1,0:T(8,128)S(1)} %get-tuple-element.30.low_ref, f32[64,512]{1,0:T(8,128)S(1)} %get-tuple-element.31.base_ref, f32[16,512]{1,0:T(8,128)S(1)} %get-tuple-element.32.factor_ref, bf16[64,192]{1,0:T(8,128)(2,1)S(1)} %get-tuple-element.33.low_node_ref, f32[1,512]{1,0:T(1,128)S(1)} %copy-done.6, ...), custom_call_target="tpu_custom_call" | custom-call | flops 40000000000 | tf_op jit(solution)/shard_map/pallas_call | solution.py:388
  26.4 1.6 %collective-permute-start.8 = (bf16[256,128]{1,0:T(8,128)(2,1)S(1)}, bf16[256,128]{1,0:T(8,128)(2,1)S(1)}, u32[]{:S(2)}, u32[]{:S(2)}) collective-permute-start(bf16[256,128]{1,0:T(8,128)(2,1)S(1)} %shard_map.126), channel_id=1, source_target_pairs={{0,127},{1,66},{2,65},{3,68},{4,67},{5,70},{6,69},{7,72},{8,71},{9... | collective-permute-start | bytes 196616 | tf_op jit(solution)/shard_map/ppermute | solution.py:391
  27.9 0.0 collective-permute-start.7
  27.9 0.0 collective-permute-start.6
  27.9 1.6 %collective-permute-done.3.away_ref = bf16[256,512]{1,0:T(8,128)(2,1)S(1)} collective-permute-done((bf16[256,512]{1,0:T(8,128)(2,1)S(1)}, bf16[256,512]{1,0:T(8,128)(2,1)S(1)}, u32[]{:S(2)}, u32[]{:S(2)}) %collective-permute-start.3) | collective-permute-done | bytes 262176 | tf_op jit(solution)/shard_map/ppermute | solution.py:386
  29.5 4.3 %shard_map.125 = f32[1024,512]{1,0:T(8,128)} custom-call(f32[4,1024,128]{2,1,0:T(8,128)S(1)} %get-tuple-element.20.state_ref, f32[4,1024,128]{2,1,0:T(8,128)S(1)} %get-tuple-element.23.part_ref, bf16[256,512]{1,0:T(8,128)(2,1)S(1)} %collective-permute-done.order_ref.here_first, bf16[256,512]{1,0:T(8,128)(2,1)S(1)} %collective-permute-done.1.away_first, ...), custom_call_target="tpu_custom_call" | custom-call | tf_op jit(solution)/shard_map/pallas_call | solution.py:394
  33.8 1.8 %collective-permute-done.8.far_ref = bf16[256,128]{1,0:T(8,128)(2,1)S(1)} collective-permute-done((bf16[256,128]{1,0:T(8,128)(2,1)S(1)}, bf16[256,128]{1,0:T(8,128)(2,1)S(1)}, u32[]{:S(2)}, u32[]{:S(2)}) %collective-permute-start.8) | collective-permute-done | bytes 65568 | tf_op jit(solution)/shard_map/ppermute | solution.py:391
  35.6 2.0 %shard_map.127 = f32[1,4,16,512]{3,2,1,0:T(8,128)} custom-call(bf16[256,128]{1,0:T(8,128)(2,1)S(1)} %collective-permute-done.6.own_ref, bf16[256,128]{1,0:T(8,128)(2,1)S(1)} %collective-permute-done.7.near_ref, bf16[256,128]{1,0:T(8,128)(2,1)S(1)} %collective-permute-done.8.far_ref, bf16[320,768]{1,0:T(8,128)(2,1)S(1)} %get-tuple-element.36.pick_ref, ...), custom_call_target="tpu_custom_call" | custom-call | tf_op jit(solution)/shard_map/pallas_call | solution.py:403
  (20 shorter events, 0.0 us)
Async XLA Ops:
  0.6 11.0 %copy-start.7 = (f32[1,3]{1,0:T(1,128)S(1)}, f32[1,3]{1,0:T(1,128)}, u32[]{:S(2)}) copy-start(f32[1,3]{1,0:T(1,128)} %coeffs_ref.5) | copy-start | bytes 40
  0.6 11.0 %copy-start.6 = (f32[1,512]{1,0:T(1,128)S(1)}, f32[1,512]{1,0:T(1,128)}, u32[]{:S(2)}) copy-start(f32[1,512]{1,0:T(1,128)} %metric_ref.5) | copy-start | bytes 6148
  0.7 11.0 %copy-start.1 = (f32[1,4,16,512]{3,2,1,0:T(8,128)S(1)}, f32[1,4,16,512]{3,2,1,0:T(8,128)}, u32[]{:S(2)}) copy-start(f32[1,4,16,512]{3,2,1,0:T(8,128)} %forcing_ref.3) | copy-start | bytes 393220
  0.7 11.0 %copy-start.2 = (s32[1,16,512]{2,1,0:T(8,128)S(1)}, s32[1,16,512]{2,1,0:T(8,128)}, u32[]{:S(2)}) copy-start(s32[1,16,512]{2,1,0:T(8,128)} %mask_ref.3) | copy-start | bytes 98308
  0.7 11.0 %copy-start.4 = (f32[1,16,16]{2,1,0:T(8,128)S(1)}, f32[1,16,16]{2,1,0:T(8,128)}, u32[]{:S(2)}) copy-start(f32[1,16,16]{2,1,0:T(8,128)} %level_ref.1) | copy-start | bytes 3076
  0.7 11.0 %copy-start.3 = (f32[1,16,16]{2,1,0:T(8,128)S(1)}, f32[1,16,16]{2,1,0:T(8,128)}, u32[]{:S(2)}) copy-start(f32[1,16,16]{2,1,0:T(8,128)} %node_ref.1) | copy-start | bytes 3076
  2.8 8.8 %collective-permute-start = (bf16[256,512]{1,0:T(8,128)(2,1)S(1)}, bf16[256,512]{1,0:T(8,128)(2,1)S(1)}, u32[]{:S(2)}, u32[]{:S(2)}) collective-permute-start(bf16[256,512]{1,0:T(8,128)(2,1)S(1)} %get-tuple-element.22), channel_id=1, source_target_pairs={{0,1},{1,0},{2,3},{3,2},{4,5},{5,4},{6,7},{7,6},{8,9},{9,8},{10,11... | collective-permute-start | bytes 786440 | tf_op jit(solution)/shard_map/ppermute | solution.py:364
  2.9 25.0 %collective-permute-start.1 = (bf16[256,512]{1,0:T(8,128)(2,1)S(1)}, bf16[256,512]{1,0:T(8,128)(2,1)S(1)}, u32[]{:S(2)}, u32[]{:S(2)}) collective-permute-start(bf16[256,512]{1,0:T(8,128)(2,1)S(1)} %get-tuple-element.24), channel_id=1, source_target_pairs={{0,63},{1,2},{2,1},{3,4},{4,3},{5,6},{6,5},{7,8},{8,7},{9,10},{10,... | collective-permute-start | bytes 786440 | tf_op jit(solution)/shard_map/ppermute | solution.py:363
  11.7 5.5 %copy-start.5 = (s32[1,2048]{1,0:T(1,128)S(1)}, s32[1,2048]{1,0:T(1,128)}, u32[]{:S(2)}) copy-start(s32[1,2048]{1,0:T(1,128)} %partner_ref.1) | copy-start | bytes 24580
  11.7 5.5 %copy-start.8 = (s32[1,80]{1,0:T(1,128)S(1)}, s32[1,80]{1,0:T(1,128)}, u32[]{:S(2)}) copy-start(s32[1,80]{1,0:T(1,128)} %rows_ref.1) | copy-start | bytes 964
  11.7 5.5 %copy-start.9 = (s32[1,80]{1,0:T(1,128)S(1)}, s32[1,80]{1,0:T(1,128)}, u32[]{:S(2)}) copy-start(s32[1,80]{1,0:T(1,128)} %cols_ref.1) | copy-start | bytes 964
  15.6 8.3 %collective-permute-start.4 = (bf16[64,512]{1,0:T(8,128)(2,1)S(1)}, bf16[64,512]{1,0:T(8,128)(2,1)S(1)}, u32[]{:S(2)}, u32[]{:S(2)}) collective-permute-start(bf16[64,512]{1,0:T(8,128)(2,1)S(1)} %get-tuple-element.34), channel_id=1, source_target_pairs={{0,1},{1,0},{2,3},{3,2},{4,5},{5,4},{6,7},{7,6},{8,9},{9,8},{10,11... | collective-permute-start | bytes 196616 | tf_op jit(solution)/shard_map/ppermute | solution.py:377
  15.6 9.6 %collective-permute-start.5 = (bf16[64,512]{1,0:T(8,128)(2,1)S(1)}, bf16[64,512]{1,0:T(8,128)(2,1)S(1)}, u32[]{:S(2)}, u32[]{:S(2)}) collective-permute-start(bf16[64,512]{1,0:T(8,128)(2,1)S(1)} %get-tuple-element.35), channel_id=1, source_target_pairs={{0,63},{1,2},{2,1},{3,4},{4,3},{5,6},{6,5},{7,8},{8,7},{9,10},{10,... | collective-permute-start | bytes 196616 | tf_op jit(solution)/shard_map/ppermute | solution.py:376
  17.2 8.1 %collective-permute-start.2 = (bf16[256,512]{1,0:T(8,128)(2,1)S(1)}, bf16[256,512]{1,0:T(8,128)(2,1)S(1)}, u32[]{:S(2)}, u32[]{:S(2)}) collective-permute-start(bf16[256,512]{1,0:T(8,128)(2,1)S(1)} %get-tuple-element.25), channel_id=1, source_target_pairs={{0,1},{1,0},{2,3},{3,2},{4,5},{5,4},{6,7},{7,6},{8,9},{9,8},{10,11... | collective-permute-start | bytes 786440 | tf_op jit(solution)/shard_map/ppermute | solution.py:387
  17.7 11.8 %collective-permute-start.3 = (bf16[256,512]{1,0:T(8,128)(2,1)S(1)}, bf16[256,512]{1,0:T(8,128)(2,1)S(1)}, u32[]{:S(2)}, u32[]{:S(2)}) collective-permute-start(bf16[256,512]{1,0:T(8,128)(2,1)S(1)} %get-tuple-element.26), channel_id=1, source_target_pairs={{0,63},{1,2},{2,1},{3,4},{4,3},{5,6},{6,5},{7,8},{8,7},{9,10},{10,... | collective-permute-start | bytes 786440 | tf_op jit(solution)/shard_map/ppermute | solution.py:386
  26.4 9.2 %collective-permute-start.8 = (bf16[256,128]{1,0:T(8,128)(2,1)S(1)}, bf16[256,128]{1,0:T(8,128)(2,1)S(1)}, u32[]{:S(2)}, u32[]{:S(2)}) collective-permute-start(bf16[256,128]{1,0:T(8,128)(2,1)S(1)} %shard_map.126), channel_id=1, source_target_pairs={{0,127},{1,66},{2,65},{3,68},{4,67},{5,70},{6,69},{7,72},{8,71},{9... | collective-permute-start | bytes 196616 | tf_op jit(solution)/shard_map/ppermute | solution.py:391
  27.9 7.6 %collective-permute-start.7 = (bf16[256,128]{1,0:T(8,128)(2,1)S(1)}, bf16[256,128]{1,0:T(8,128)(2,1)S(1)}, u32[]{:S(2)}, u32[]{:S(2)}) collective-permute-start(bf16[256,128]{1,0:T(8,128)(2,1)S(1)} %shard_map.126), channel_id=1, source_target_pairs={{0,65},{1,64},{2,67},{3,66},{4,69},{5,68},{6,71},{7,70},{8,73},{9,... | collective-permute-start | bytes 196616 | tf_op jit(solution)/shard_map/ppermute | solution.py:392
  27.9 7.6 %collective-permute-start.6 = (bf16[256,128]{1,0:T(8,128)(2,1)S(1)}, bf16[256,128]{1,0:T(8,128)(2,1)S(1)}, u32[]{:S(2)}, u32[]{:S(2)}) collective-permute-start(bf16[256,128]{1,0:T(8,128)(2,1)S(1)} %shard_map.126), channel_id=1, source_target_pairs={{0,64},{1,65},{2,66},{3,67},{4,68},{5,69},{6,70},{7,71},{8,72},{9,... | collective-permute-start | bytes 196616 | tf_op jit(solution)/shard_map/ppermute | solution.py:393
  29.5 6.1 %copy-start = (bf16[1,80,128,128]{3,2,1,0:T(8,128)(2,1)S(1)}, bf16[1,80,128,128]{3,2,1,0:T(8,128)(2,1)}, u32[]{:S(2)}) copy-start(bf16[1,80,128,128]{3,2,1,0:T(8,128)(2,1)} %param.19) | copy-start | bytes 7864324

commit v6 on v4

--- a/solution.py
+++ b/solution.py
@@ -138,12 +138,13 @@
                     edges[at : at + 16, lanes] = pack_node(ref, v, c, SIDE_NODES[side][place], scale)
 
 
-def first_kernel(state_hbm, partner_hbm, coeffs_hbm, state_ref, here_ref, away_ref, inner_ref, partner_ref, coeffs_ref, sems):
+def first_kernel(state_hbm, partner_hbm, coeffs_hbm, state_ref, here_ref, away_ref, inner_ref, spread_ref, partner_ref, coeffs_ref, sems):
     pairs = [(partner_hbm, partner_ref), (coeffs_hbm, coeffs_ref)]
     pairs += [(state_hbm.at[:, LANES[c]], state_ref.at[c]) for c in range(4)]
     copies = [pltpu.make_async_copy(source, target, sems.at[i]) for i, (source, target) in enumerate(pairs)]
     for copy in copies:
         copy.start()
+    spread_ref[...] = spread_matrix()
     copies[0].wait()
     for step in range(4):
         columns = partner_ref[0:1, 512 + 256 * step : 768 + 256 * step] - 1024
@@ -155,7 +156,7 @@
 
 
 def local_kernel(
-    state_ref, inner_ref, metric_ref, node_ref, level_ref, coeffs_ref, mask_ref, forcing_ref, order_ref,
+    state_ref, inner_ref, spread_ref, metric_ref, node_ref, level_ref, coeffs_ref, mask_ref, forcing_ref, order_ref,
     part_ref, here_ref, away_ref, here_low_ref, away_low_ref,
     weights_ref, low_ref, base_ref, factor_ref, low_node_ref,
     level_smem, edges, sem,
@@ -163,7 +164,7 @@
     scalars = pltpu.make_async_copy(level_ref, level_smem, sem)
     scalars.start()
     select_low, spread_inner = low_select(), low_spread(2, 3)
-    weights_ref[:, 512:768] = spread_matrix()
+    weights_ref[:, 512:768] = spread_ref[...]
     penalty = coeffs_ref[:, 0:1]
     metric = metric_ref[...]
     node, level = coupling_matrices(node_ref, level_ref)
@@ -218,8 +219,8 @@
 
 
 def lowest_kernel(
-    low_ref, base_ref, factor_ref, low_node_ref, metric_ref, coeffs_ref, here_ref, away_ref, here_map, away_map, inner_ref,
-    order_ref, surface_ref,
+    low_ref, base_ref, factor_ref, low_node_ref, metric_ref, coeffs_ref, away_ref, here_ref, here_map, away_map, inner_ref,
+    surface_ref,
 ):
     penalty = coeffs_ref[:, 0:1]
     here = dot(here_ref[...], here_map[...]).astype(BF16)
@@ -240,7 +241,7 @@
 
 
 def tables_kernel(
-    partner_ref, rows_ref, cols_ref, here_map, away_map, pick_ref, sum_ref,
+    partner_ref, rows_ref, cols_ref, order_ref, first_ref, here_map, away_map, pick_ref, sum_ref,
 ):
     last = ends()[0] == 12
     before, after = partner_ref[0:1, 0:512], partner_ref[0:1, 1536:2048] - 2560
@@ -262,7 +263,7 @@
 
 
 def finish_kernel(
-    state_ref, part_ref, here_first, away_first, here_ref, away_ref, here_map, away_map, inner_ref, weights_ref,
+    state_ref, part_ref, away_first, here_first, away_ref, here_ref, here_map, away_map, inner_ref, weights_ref,
     metric_ref, coeffs_ref, mask_ref, forcing_ref,
     next_hbm, middle_ref, next_ref, edges, sems,
 ):
@@ -299,7 +300,7 @@
         copy.wait()
 
 
-def remap_kernel(own_ref, near_ref, far_ref, pick_ref, sum_ref, blocks_ref, out_ref, products):
+def remap_kernel(far_ref, near_ref, own_ref, pick_ref, sum_ref, blocks_ref, out_ref, products):
     picked = dot(pick_ref[:, 0:256], far_ref[...])
     picked = picked + dot(pick_ref[:, 256:512], own_ref[...])
     picked = picked + dot(pick_ref[:, 512:768], near_ref[...])
@@ -350,9 +351,9 @@
     straight = [(t, t) for t in range(tiles)]
     flat = state.reshape(1024, 512)
     hbm = lambda *values: [pltpu.with_memory_space_constraint(value, pltpu.HBM) for value in values]
-    chunks, here_first, away_first, inner = call(
+    chunks, here_first, away_first, inner, spread = call(
         first_kernel,
-        [((4, 1024, 128), F32), ((256, 512), BF16), ((256, 512), BF16), ((1024, 1024), BF16)],
+        [((4, 1024, 128), F32), ((256, 512), BF16), ((256, 512), BF16), ((1024, 1024), BF16), ((256, 256), BF16)],
         [pltpu.VMEM(edge_partner.shape, jnp.int32), pltpu.SMEM(coeffs.shape, F32), pltpu.SemaphoreType.DMA((6,))],
         "hhh",
     )(*hbm(flat, edge_partner, coeffs))
@@ -367,22 +368,22 @@
             ((64, 512), F32), ((64, 512), F32), ((16, 512), F32), ((64, 192), BF16),
         ],
         [pltpu.SMEM((1, 16, 16), F32), pltpu.VMEM((288, 1024), BF16), pltpu.SemaphoreType.DMA],
-        "v" * 8 + "a",
-    )(chunks, inner, *inputs, here_first)
+        "v" * 9 + "a",
+    )(chunks, inner, spread, *inputs, here_first)
     away_low = lax.ppermute(away_low, "tile", away)
     here_low = lax.ppermute(here_low, "tile", here)
+    away_edge = lax.ppermute(away_edge, "tile", away)
+    here_edge = lax.ppermute(here_edge, "tile", here)
     slots = remap_rows.shape[1]
     here_map, away_map, pick, total = call(
         tables_kernel,
         [
             ((512, 512), BF16), ((512, 512), BF16), ((4 * slots, 768), BF16), ((256, 4 * slots), BF16),
         ],
-        inputs="vvv", results="vvvv", cost=4_000_000_000,
-    )(edge_partner, remap_rows, remap_cols)
-    away_edge = lax.ppermute(away_edge, "tile", away)
-    here_edge = lax.ppermute(here_edge, "tile", here)
-    (surface,) = call(lowest_kernel, [((256, 128), BF16)], inputs="v" * 11 + "a", cost=40_000_000_000)(
-        low, base, factor, low_node, metric, coeffs, here_low, away_low, here_map, away_map, inner, here_edge
+        inputs="vvvaa", results="vvvv", cost=4000000000,
+    )(edge_partner, remap_rows, remap_cols, here_edge, away_first)
+    (surface,) = call(lowest_kernel, [((256, 128), BF16)], inputs="v" * 11, cost=40000000000)(
+        low, base, factor, low_node, metric, coeffs, away_low, here_low, here_map, away_map, inner
     )
     far = lax.ppermute(surface, ("comp", "tile"), crossed(away))
     near = lax.ppermute(surface, ("comp", "tile"), crossed(here))
@@ -395,10 +396,10 @@
             pltpu.SemaphoreType.DMA((4,)),
         ],
         "v" * 14, "h",
-    )(chunks, part, here_first, away_first, here_edge, away_edge, here_map, away_map, inner, weights, metric, coeffs, sea_mask, forcing)
+    )(chunks, part, away_first, here_first, away_edge, here_edge, here_map, away_map, inner, weights, metric, coeffs, sea_mask, forcing)
     (new_forcing,) = call(
         remap_kernel, [(forcing.shape, F32)], [pltpu.VMEM((4 * slots, 128), F32)], "v" * 6,
-    )(own, near, far, pick, total, remap_weights[0])
+    )(far, near, own, pick, total, remap_weights[0])
     return nxt.reshape(state.shape), new_forcing
 
 

time: 37.2 us -> 37.1 us (level)
    ppermute x1, waiting for transfers between devices: 2.33 us -> 3.01 us  [shards(): far = lax.ppermute(surface, ('comp', 'tile'), crossed(away))]
    ppermute x1, waiting for transfers between devices: 1.56 us -> 0.89 us  [shards(): away_edge = lax.ppermute(away_edge, 'tile', away)]
where the time goes in v6:
time: 37.1 us; the launch traced here: 37 us
  starting transfers between devices  18 us (49%)
  Pallas kernels  12.8 us (35%)
  waiting for transfers between devices  5.35 us (14%)
  between operations  0.82 us (2%)
    ppermute x1, starting transfers between devices, shards(): away_first = lax.ppermute(away_first, 'tile', away)  8.71 us
    ppermute x1, starting transfers between devices, shards(): away_edge = lax.ppermute(away_edge, 'tile', away)  6.04 us
    pallas_call x1, Pallas kernels, shards(): call(finish_kernel, [((1024, 512), F32)], [pltpu.VMEM((4, 1024, 128), F32...  3.71 us
    pallas_call x1, Pallas kernels, shards(): call(local_kernel, [((4, 1024, 128), F32), ((256, 512), BF16), ((256, 512...  3.21 us
    ppermute x1, waiting for transfers between devices, shards(): far = lax.ppermute(surface, ('comp', 'tile'), crossed(away))  3.01 us
    pallas_call x1, Pallas kernels, shards(): call(first_kernel, [((4, 1024, 128), F32), ((256, 512), BF16), ((256, 512...  2.1 us
    pallas_call x1, Pallas kernels, shards(): call(remap_kernel, [(forcing.shape, F32)], [pltpu.VMEM((4 * slots, 128),...  2.05 us
    ppermute x1, starting transfers between devices, shards(): far = lax.ppermute(surface, ('comp', 'tile'), crossed(away))  1.57 us
  transfers between devices with their start and end apart: 9, of which 3 were waited for; matrix products, arithmetic and copies ran while one was open for 0% of the time, Pallas kernels for 23%

profile of v6, /device:TPU:0, one launch (start us, length us, event | category | flops | bytes accessed | tf_op | source)
XLA Modules:
  0.0 37.0 jit_solution(5637798408333936481)
XLA Ops:
  0.7 2.1 %shard_map.122 = (f32[4,1024,128]{2,1,0:T(8,128)S(1)}, bf16[256,512]{1,0:T(8,128)(2,1)S(1)}, bf16[256,512]{1,0:T(8,128)(2,1)S(1)}, bf16[1024,1024]{1,0:T(8,128)(2,1)S(1)}, bf16[256,256]{1,0:T(8,128)(2,1)S(1)}) custom-call(f32[1024,512]{1,0:T(8,128)} %bitcast.4, s32[1,2048]{1,0:T(1,128)} %partner_ref.1, f32[1,3]{1,0:T(1,128)} %coeffs_ref.5), custom_call_target="tpu_custom_call" | custom-call | tf_op jit(solution)/shard_map/pallas_call | solution.py:354
  2.8 0.1 collective-permute-start
  2.9 8.7 %collective-permute-start.1 = (bf16[256,512]{1,0:T(8,128)(2,1)S(1)}, bf16[256,512]{1,0:T(8,128)(2,1)S(1)}, u32[]{:S(2)}, u32[]{:S(2)}) collective-permute-start(bf16[256,512]{1,0:T(8,128)(2,1)S(1)} %get-tuple-element.26), channel_id=1, source_target_pairs={{0,63},{1,2},{2,1},{3,4},{4,3},{5,6},{6,5},{7,8},{8,7},{9,10},{10,... | collective-permute-start | bytes 786440 | tf_op jit(solution)/shard_map/ppermute | solution.py:360
  11.6 0.0 collective-permute-done.order_ref.here_first
  11.7 0.0 copy-start.5
  11.7 0.0 copy-start.8
  11.7 0.0 copy-start.9
  11.7 3.2 %shard_map.123 = (f32[4,1024,128]{2,1,0:T(8,128)S(1)}, bf16[256,512]{1,0:T(8,128)(2,1)S(1)}, bf16[256,512]{1,0:T(8,128)(2,1)S(1)}, bf16[64,512]{1,0:T(8,128)(2,1...) custom-call(f32[4,1024,128]{2,1,0:T(8,128)S(1)} %get-tuple-element.2, ...), custom_call_target="tpu_custom_call" | custom-call | tf_op jit(solution)/shard_map/pallas_call | solution.py:363
  14.9 0.1 collective-permute-start.3
  15.0 1.5 %collective-permute-start.4 = (bf16[64,512]{1,0:T(8,128)(2,1)S(1)}, bf16[64,512]{1,0:T(8,128)(2,1)S(1)}, u32[]{:S(2)}, u32[]{:S(2)}) collective-permute-start(bf16[64,512]{1,0:T(8,128)(2,1)S(1)} %get-tuple-element.36), channel_id=1, source_target_pairs={{0,63},{1,2},{2,1},{3,4},{4,3},{5,6},{6,5},{7,8},{8,7},{9,10},{10,... | collective-permute-start | bytes 196616 | tf_op jit(solution)/shard_map/ppermute | solution.py:373
  16.5 0.0 collective-permute-start.5
  16.5 6.0 %collective-permute-start.2 = (bf16[256,512]{1,0:T(8,128)(2,1)S(1)}, bf16[256,512]{1,0:T(8,128)(2,1)S(1)}, u32[]{:S(2)}, u32[]{:S(2)}) collective-permute-start(bf16[256,512]{1,0:T(8,128)(2,1)S(1)} %get-tuple-element.27), channel_id=1, source_target_pairs={{0,63},{1,2},{2,1},{3,4},{4,3},{5,6},{6,5},{7,8},{8,7},{9,10},{10,... | collective-permute-start | bytes 786440 | tf_op jit(solution)/shard_map/ppermute | solution.py:375
  22.6 0.0 collective-permute-done.1.first_ref.away_first
  22.6 0.0 collective-permute-done.3.order_ref.here_ref
  22.6 0.6 %shard_map.124 = (bf16[512,512]{1,0:T(8,128)(2,1)S(1)}, bf16[512,512]{1,0:T(8,128)(2,1)S(1)}, bf16[320,768]{1,0:T(8,128)(2,1)S(1)}, bf16[256,320]{1,0:T(8,128)(2,1)S(1)}) custom-call(s32[1,2048]{1,0:T(1,128)S(1)} %copy-done.5, s32[1,80]{1,0:T(1,128)S(1)} %copy-done.8, s32[1,80]{1,0:T(1,128)S(1)} %copy-done.9, ...), custom_call_target="tpu_custom_call" | custom-call | flops 4000000000 | tf_op jit(solution)/shard_map/pallas_call | solution.py:378
  23.2 1.4 %collective-permute-done.4.away_ref = bf16[64,512]{1,0:T(8,128)(2,1)S(1)} collective-permute-done((bf16[64,512]{1,0:T(8,128)(2,1)S(1)}, bf16[64,512]{1,0:T(8,128)(2,1)S(1)}, u32[]{:S(2)}, u32[]{:S(2)}) %collective-permute-start.4) | collective-permute-done | bytes 65568 | tf_op jit(solution)/shard_map/ppermute | solution.py:373
  24.6 0.0 collective-permute-done.5.here_ref
  24.6 1.1 %shard_map.126 = bf16[256,128]{1,0:T(8,128)(2,1)S(1)} custom-call(f32[64,512]{1,0:T(8,128)S(1)} %get-tuple-element.32.low_ref, f32[64,512]{1,0:T(8,128)S(1)} %get-tuple-element.33.base_ref, f32[16,512]{1,0:T(8,128)S(1)} %get-tuple-element.34.factor_ref, bf16[64,192]{1,0:T(8,128)(2,1)S(1)} %get-tuple-element.35.low_node_ref, f32[1,512]{1,0:T(1,128)S(1)} %copy-done.6, ...), custom_call_target="tpu_custom_call" | custom-call | flops 40000000000 | tf_op jit(solution)/shard_map/pallas_call | solution.py:385
  25.7 1.6 %collective-permute-start.6 = (bf16[256,128]{1,0:T(8,128)(2,1)S(1)}, bf16[256,128]{1,0:T(8,128)(2,1)S(1)}, u32[]{:S(2)}, u32[]{:S(2)}) collective-permute-start(bf16[256,128]{1,0:T(8,128)(2,1)S(1)} %shard_map.126), channel_id=1, source_target_pairs={{0,127},{1,66},{2,65},{3,68},{4,67},{5,70},{6,69},{7,72},{8,71},{9... | collective-permute-start | bytes 196616 | tf_op jit(solution)/shard_map/ppermute | solution.py:388
  27.3 0.0 collective-permute-start.8
  27.3 0.9 %collective-permute-done.2.away_ref = bf16[256,512]{1,0:T(8,128)(2,1)S(1)} collective-permute-done((bf16[256,512]{1,0:T(8,128)(2,1)S(1)}, bf16[256,512]{1,0:T(8,128)(2,1)S(1)}, u32[]{:S(2)}, u32[]{:S(2)}) %collective-permute-start.2) | collective-permute-done | bytes 262176 | tf_op jit(solution)/shard_map/ppermute | solution.py:375
  28.2 3.7 %shard_map.125 = f32[1024,512]{1,0:T(8,128)} custom-call(f32[4,1024,128]{2,1,0:T(8,128)S(1)} %get-tuple-element.21.state_ref, f32[4,1024,128]{2,1,0:T(8,128)S(1)} %get-tuple-element.25.part_ref, bf16[256,512]{1,0:T(8,128)(2,1)S(1)} %collective-permute-done.1.first_ref.away_first, bf16[256,512]{1,0:T(8,128)(2,1)S(1)} %collective-permute-done.order_ref.here_first, ...), custom_call_target="tpu_custom_call" | custom-call | tf_op jit(solution)/shard_map/pallas_call | solution.py:391
  31.9 3.0 %collective-permute-done.6.far_ref = bf16[256,128]{1,0:T(8,128)(2,1)S(1)} collective-permute-done((bf16[256,128]{1,0:T(8,128)(2,1)S(1)}, bf16[256,128]{1,0:T(8,128)(2,1)S(1)}, u32[]{:S(2)}, u32[]{:S(2)}) %collective-permute-start.6) | collective-permute-done | bytes 65568 | tf_op jit(solution)/shard_map/ppermute | solution.py:388
  34.9 2.0 %shard_map.127 = f32[1,4,16,512]{3,2,1,0:T(8,128)} custom-call(bf16[256,128]{1,0:T(8,128)(2,1)S(1)} %collective-permute-done.6.far_ref, bf16[256,128]{1,0:T(8,128)(2,1)S(1)} %collective-permute-done.7.near_ref, bf16[256,128]{1,0:T(8,128)(2,1)S(1)} %collective-permute-done.8.own_ref, bf16[320,768]{1,0:T(8,128)(2,1)S(1)} %get-tuple-element.38.pick_ref, ...), custom_call_target="tpu_custom_call" | custom-call | tf_op jit(solution)/shard_map/pallas_call | solution.py:400
  (20 shorter events, 0.0 us)
Async XLA Ops:
  0.6 11.0 %copy-start.7 = (f32[1,3]{1,0:T(1,128)S(1)}, f32[1,3]{1,0:T(1,128)}, u32[]{:S(2)}) copy-start(f32[1,3]{1,0:T(1,128)} %coeffs_ref.5) | copy-start | bytes 40
  0.6 11.0 %copy-start.6 = (f32[1,512]{1,0:T(1,128)S(1)}, f32[1,512]{1,0:T(1,128)}, u32[]{:S(2)}) copy-start(f32[1,512]{1,0:T(1,128)} %metric_ref.5) | copy-start | bytes 6148
  0.7 11.0 %copy-start.3 = (f32[1,16,16]{2,1,0:T(8,128)S(1)}, f32[1,16,16]{2,1,0:T(8,128)}, u32[]{:S(2)}) copy-start(f32[1,16,16]{2,1,0:T(8,128)} %node_ref.1) | copy-start | bytes 3076
  0.7 11.0 %copy-start.4 = (f32[1,16,16]{2,1,0:T(8,128)S(1)}, f32[1,16,16]{2,1,0:T(8,128)}, u32[]{:S(2)}) copy-start(f32[1,16,16]{2,1,0:T(8,128)} %level_ref.1) | copy-start | bytes 3076
  0.7 11.0 %copy-start.2 = (s32[1,16,512]{2,1,0:T(8,128)S(1)}, s32[1,16,512]{2,1,0:T(8,128)}, u32[]{:S(2)}) copy-start(s32[1,16,512]{2,1,0:T(8,128)} %mask_ref.3) | copy-start | bytes 98308
  0.7 11.0 %copy-start.1 = (f32[1,4,16,512]{3,2,1,0:T(8,128)S(1)}, f32[1,4,16,512]{3,2,1,0:T(8,128)}, u32[]{:S(2)}) copy-start(f32[1,4,16,512]{3,2,1,0:T(8,128)} %forcing_ref.3) | copy-start | bytes 393220
  2.8 8.8 %collective-permute-start = (bf16[256,512]{1,0:T(8,128)(2,1)S(1)}, bf16[256,512]{1,0:T(8,128)(2,1)S(1)}, u32[]{:S(2)}, u32[]{:S(2)}) collective-permute-start(bf16[256,512]{1,0:T(8,128)(2,1)S(1)} %get-tuple-element.24), channel_id=1, source_target_pairs={{0,1},{1,0},{2,3},{3,2},{4,5},{5,4},{6,7},{7,6},{8,9},{9,8},{10,11... | collective-permute-start | bytes 786440 | tf_op jit(solution)/shard_map/ppermute | solution.py:361
  2.9 19.7 %collective-permute-start.1 = (bf16[256,512]{1,0:T(8,128)(2,1)S(1)}, bf16[256,512]{1,0:T(8,128)(2,1)S(1)}, u32[]{:S(2)}, u32[]{:S(2)}) collective-permute-start(bf16[256,512]{1,0:T(8,128)(2,1)S(1)} %get-tuple-element.26), channel_id=1, source_target_pairs={{0,63},{1,2},{2,1},{3,4},{4,3},{5,6},{6,5},{7,8},{8,7},{9,10},{10,... | collective-permute-start | bytes 786440 | tf_op jit(solution)/shard_map/ppermute | solution.py:360
  11.7 10.9 %copy-start.5 = (s32[1,2048]{1,0:T(1,128)S(1)}, s32[1,2048]{1,0:T(1,128)}, u32[]{:S(2)}) copy-start(s32[1,2048]{1,0:T(1,128)} %partner_ref.1) | copy-start | bytes 24580
  11.7 10.9 %copy-start.8 = (s32[1,80]{1,0:T(1,128)S(1)}, s32[1,80]{1,0:T(1,128)}, u32[]{:S(2)}) copy-start(s32[1,80]{1,0:T(1,128)} %rows_ref.1) | copy-start | bytes 964
  11.7 10.9 %copy-start.9 = (s32[1,80]{1,0:T(1,128)S(1)}, s32[1,80]{1,0:T(1,128)}, u32[]{:S(2)}) copy-start(s32[1,80]{1,0:T(1,128)} %cols_ref.1) | copy-start | bytes 964
  14.9 7.7 %collective-permute-start.3 = (bf16[256,512]{1,0:T(8,128)(2,1)S(1)}, bf16[256,512]{1,0:T(8,128)(2,1)S(1)}, u32[]{:S(2)}, u32[]{:S(2)}) collective-permute-start(bf16[256,512]{1,0:T(8,128)(2,1)S(1)} %get-tuple-element.28), channel_id=1, source_target_pairs={{0,1},{1,0},{2,3},{3,2},{4,5},{5,4},{6,7},{7,6},{8,9},{9,8},{10,11... | collective-permute-start | bytes 786440 | tf_op jit(solution)/shard_map/ppermute | solution.py:376
  15.0 9.6 %collective-permute-start.4 = (bf16[64,512]{1,0:T(8,128)(2,1)S(1)}, bf16[64,512]{1,0:T(8,128)(2,1)S(1)}, u32[]{:S(2)}, u32[]{:S(2)}) collective-permute-start(bf16[64,512]{1,0:T(8,128)(2,1)S(1)} %get-tuple-element.36), channel_id=1, source_target_pairs={{0,63},{1,2},{2,1},{3,4},{4,3},{5,6},{6,5},{7,8},{8,7},{9,10},{10,... | collective-permute-start | bytes 196616 | tf_op jit(solution)/shard_map/ppermute | solution.py:373
  16.5 8.1 %collective-permute-start.5 = (bf16[64,512]{1,0:T(8,128)(2,1)S(1)}, bf16[64,512]{1,0:T(8,128)(2,1)S(1)}, u32[]{:S(2)}, u32[]{:S(2)}) collective-permute-start(bf16[64,512]{1,0:T(8,128)(2,1)S(1)} %get-tuple-element.37), channel_id=1, source_target_pairs={{0,1},{1,0},{2,3},{3,2},{4,5},{5,4},{6,7},{7,6},{8,9},{9,8},{10,11... | collective-permute-start | bytes 196616 | tf_op jit(solution)/shard_map/ppermute | solution.py:374
  16.5 11.7 %collective-permute-start.2 = (bf16[256,512]{1,0:T(8,128)(2,1)S(1)}, bf16[256,512]{1,0:T(8,128)(2,1)S(1)}, u32[]{:S(2)}, u32[]{:S(2)}) collective-permute-start(bf16[256,512]{1,0:T(8,128)(2,1)S(1)} %get-tuple-element.27), channel_id=1, source_target_pairs={{0,63},{1,2},{2,1},{3,4},{4,3},{5,6},{6,5},{7,8},{8,7},{9,10},{10,... | collective-permute-start | bytes 786440 | tf_op jit(solution)/shard_map/ppermute | solution.py:375
  25.7 9.2 %collective-permute-start.6 = (bf16[256,128]{1,0:T(8,128)(2,1)S(1)}, bf16[256,128]{1,0:T(8,128)(2,1)S(1)}, u32[]{:S(2)}, u32[]{:S(2)}) collective-permute-start(bf16[256,128]{1,0:T(8,128)(2,1)S(1)} %shard_map.126), channel_id=1, source_target_pairs={{0,127},{1,66},{2,65},{3,68},{4,67},{5,70},{6,69},{7,72},{8,71},{9... | collective-permute-start | bytes 196616 | tf_op jit(solution)/shard_map/ppermute | solution.py:388
  27.3 7.6 %collective-permute-start.7 = (bf16[256,128]{1,0:T(8,128)(2,1)S(1)}, bf16[256,128]{1,0:T(8,128)(2,1)S(1)}, u32[]{:S(2)}, u32[]{:S(2)}) collective-permute-start(bf16[256,128]{1,0:T(8,128)(2,1)S(1)} %shard_map.126), channel_id=1, source_target_pairs={{0,65},{1,64},{2,67},{3,66},{4,69},{5,68},{6,71},{7,70},{8,73},{9,... | collective-permute-start | bytes 196616 | tf_op jit(solution)/shard_map/ppermute | solution.py:389
  27.3 7.6 %collective-permute-start.8 = (bf16[256,128]{1,0:T(8,128)(2,1)S(1)}, bf16[256,128]{1,0:T(8,128)(2,1)S(1)}, u32[]{:S(2)}, u32[]{:S(2)}) collective-permute-start(bf16[256,128]{1,0:T(8,128)(2,1)S(1)} %shard_map.126), channel_id=1, source_target_pairs={{0,64},{1,65},{2,66},{3,67},{4,68},{5,69},{6,70},{7,71},{8,72},{9,... | collective-permute-start | bytes 196616 | tf_op jit(solution)/shard_map/ppermute | solution.py:390
  28.2 6.7 %copy-start = (bf16[1,80,128,128]{3,2,1,0:T(8,128)(2,1)S(1)}, bf16[1,80,128,128]{3,2,1,0:T(8,128)(2,1)}, u32[]{:S(2)}) copy-start(bf16[1,80,128,128]{3,2,1,0:T(8,128)(2,1)} %param.19) | copy-start | bytes 7864324
